TPU v7x, 32 devices: a whole 2x2x4 slice. The times are simulated.
32 devices in a mesh: img: 8 (over z, y), blk: 4 (over x, core).
Axes of the slice: x: 2, y: 2, z: 4, core: 2. Of those that a mesh axis runs over, the one named last changes fastest.
Arguments:
- tokens: bfloat16 [24, 1024, 768], P('img', 'blk'), may hold values from -6 to 6
- counts: int32 [24], P('img'), may hold values from 64 to 1024, as said below
- qkv_weight: bfloat16 [768, 2304], replicated, may hold values from -0.21875 to 0.21875
- q_bias: bfloat16 [768], replicated, may hold values from -3 to 3
- v_bias: bfloat16 [768], replicated, may hold values from -3 to 3
- out_weight: bfloat16 [768, 768], replicated, may hold values from -0.875 to 0.875
- out_bias: bfloat16 [768], replicated, may hold values from -2 to 2
- norm1_gain: bfloat16 [768], replicated, may hold values from 0.5 to 1.5
- norm1_bias: bfloat16 [768], replicated, may hold values from -2 to 2
- norm2_gain: bfloat16 [768], replicated, may hold values from 0.5 to 1.5
- norm2_bias: bfloat16 [768], replicated, may hold values from -2 to 2
- fc1_weight: bfloat16 [768, 3072], replicated, may hold values from -0.21875 to 0.21875
- fc1_bias: bfloat16 [3072], replicated, may hold values from -3 to 3
- fc2_weight: bfloat16 [3072, 768], replicated, may hold values from -0.109375 to 0.109375
- fc2_bias: bfloat16 [768], replicated, may hold values from -2 to 2
- scale1: bfloat16 [768], replicated, may hold values from 0.5 to 1.5
- scale2: bfloat16 [768], replicated, may hold values from 0.5 to 1.5
- cotangent: bfloat16 [24, 1024, 768], P('img', 'blk'), may hold values from -6 to 6
Outputs:
- output: bfloat16 [24, 1024, 768], P('img', 'blk')
- grad_tokens: bfloat16 [24, 1024, 768], P('img', 'blk')
- grad_qkv_weight: float32 [768, 2304], P(('img', 'blk'))
- grad_q_bias: float32 [768], P(('img', 'blk'))
- grad_v_bias: float32 [768], P(('img', 'blk'))
- grad_out_weight: float32 [768, 768], P(('img', 'blk'))
- grad_out_bias: float32 [768], P(('img', 'blk'))
- grad_norm1_gain: float32 [768], P(('img', 'blk'))
- grad_norm1_bias: float32 [768], P(('img', 'blk'))
- grad_norm2_gain: float32 [768], P(('img', 'blk'))
- grad_norm2_bias: float32 [768], P(('img', 'blk'))
- grad_fc1_weight: float32 [768, 3072], P(('img', 'blk'))
- grad_fc1_bias: float32 [3072], P(('img', 'blk'))
- grad_fc2_weight: float32 [3072, 768], P(('img', 'blk'))
- grad_fc2_bias: float32 [768], P(('img', 'blk'))
- grad_scale1: float32 [768], P(('img', 'blk'))
- grad_scale2: float32 [768], P(('img', 'blk'))
Inputs may be any that keep to these rules, and one draw needn't show every extreme that they name: The first counts[i] rows of image i are valid patches and the rest are padding; in each aligned group of 3 images one image has all 1024 rows valid.
All inputs are finite; a program needn't handle non-finite values.
Results may differ from a plain program's by a relative error of at most 0.015.
Values may be sent and summed in bfloat16 or wider, within the bound.
A program may use at most 192 MiB of HBM per device.

v0:
```python
from functools import partial

import jax
import jax.numpy as jnp
from jax import lax
from jax.experimental import pallas as pl
from jax.experimental.pallas import tpu as pltpu
from jax.sharding import PartitionSpec as P

HEADS = 12
WIDTH = 64
score_scale = 0.125
norm_eps = 1e-06
masked_value = -1e30
inv_sqrt2 = 0.7071067811865476
inv_sqrt2pi = 0.3989422804014327
ONES = 16
VMEM_LIMIT = 60 * 1024 * 1024
f32 = jnp.float32
bf16 = jnp.bfloat16


def dot_nn(a, b):
    return lax.dot_general(a, b, (((1,), (0,)), ((), ())), preferred_element_type=f32)


def dot_nt(a, b):
    return lax.dot_general(a, b, (((1,), (1,)), ((), ())), preferred_element_type=f32)


def dot_tn(a, b):
    return lax.dot_general(a, b, (((0,), (0,)), ((), ())), preferred_element_type=f32)


def standardize(v):
    average = jnp.mean(v, axis=-1, keepdims=True)
    centered = v - average
    spread = jnp.mean(centered * centered, axis=-1, keepdims=True)
    inverse = lax.rsqrt(spread + norm_eps)
    return centered * inverse, inverse


def params(**kw):
    return pltpu.CompilerParams(vmem_limit_bytes=VMEM_LIMIT, **kw)


def place(counts, k):
    best, top = 0, counts[0]
    for i in range(1, counts.shape[0]):
        best = jnp.where(counts[i] > top, i, best)
        top = jnp.maximum(top, counts[i])
    return lax.rem(best + k, counts.shape[0])


def forward_kernel(blocks, nh, rows, image, counts, *refs):
    xs = refs[:blocks]
    vec, w, wb = refs[blocks : blocks + 3]
    n1, qkv, full, lse = refs[blocks + 3 : blocks + 7]
    outs = refs[blocks + 7 : 2 * blocks + 7]
    qt, ks, vt, peak, acc = refs[2 * blocks + 7 :]
    hw = nh * WIDTH
    count, me = counts[place(counts, image)], lax.axis_index("blk")
    gain, shift = vec[0:1, :], vec[1:2, :]
    for m in range(blocks):
        z, _ = standardize(xs[m][...].astype(f32))
        low = (z * gain + shift).astype(bf16)
        n1[m] = low
        proj = (dot_nn(low, w[...]) + wb[...]).astype(bf16)
        qkv[m] = proj
        rs = slice(m * rows, (m + 1) * rows)
        turned = proj.T
        for h in range(nh):
            q, k, v = (slice((3 * h + i) * WIDTH, (3 * h + i + 1) * WIDTH) for i in range(3))
            qt[h * WIDTH : (h + 1) * WIDTH, rs] = turned[q, :] * score_scale
            ks[h, rs, :] = proj[:, k]
            vt[h, :WIDTH, rs] = turned[v, :]
            vt[h, WIDTH:, rs] = jnp.ones((ONES, rows), bf16)
    peak[...] = jnp.full_like(peak, masked_value)
    acc[...] = jnp.zeros_like(acc)
    @pl.loop(0, blocks)
    def _(m):
        valid = count - (me ^ m) * rows
        rs = pl.ds(pl.multiple_of(m * rows, rows), rows)

        @pl.when(valid > 0)
        def _():
            keep = lax.broadcasted_iota(jnp.int32, (rows, 1), 0) < valid
            for h in range(nh):
                s = dot_nn(ks[h, rs, :], qt[h * WIDTH : (h + 1) * WIDTH, :])
                s = jnp.where(keep, s, masked_value)
                old = peak[h : h + 1, :]
                new = jnp.maximum(old, jnp.max(s, axis=0, keepdims=True))
                p = jnp.exp(s - new)
                peak[h : h + 1, :] = new
                part = dot_nn(vt[h, :, rs], p.astype(bf16))
                acc[h] = acc[h] * jnp.exp(old - new) + part

    lse[...] = jnp.zeros_like(lse)
    for h in range(nh):
        sl = slice(h * WIDTH, (h + 1) * WIDTH)
        total = acc[h, WIDTH : WIDTH + 1, :]
        lse[h : h + 1, :] = peak[h : h + 1, :] + jnp.log(total)
        done = acc[h, :WIDTH, :] / total
        full[sl, :] = done
        for m in range(blocks):
            outs[m][sl, :] = done[:, m * rows : (m + 1) * rows].astype(bf16)


def forward_image(counts, image, xs, vec, w, wb, nh):
    blocks = len(xs)
    rows, d = xs[0].shape
    length, hw = rows * blocks, nh * WIDTH
    vm = pl.BlockSpec(memory_space=pltpu.VMEM)
    return pl.pallas_call(
        partial(forward_kernel, blocks, nh, rows, image),
        name="attend_forward",
        in_specs=[pl.BlockSpec(memory_space=pltpu.SMEM)] + [vm] * (blocks + 3),
        out_specs=[vm] * (4 + blocks),
        out_shape=[
            jax.ShapeDtypeStruct((blocks, rows, d), bf16),
            jax.ShapeDtypeStruct((blocks, rows, 3 * hw), bf16),
            jax.ShapeDtypeStruct((hw, length), f32),
            jax.ShapeDtypeStruct((8, length), f32),
        ]
        + [jax.ShapeDtypeStruct((hw, rows), bf16)] * blocks,
        scratch_shapes=[
            pltpu.VMEM((hw, length), bf16),
            pltpu.VMEM((nh, length, WIDTH), bf16),
            pltpu.VMEM((nh, WIDTH + ONES, length), bf16),
            pltpu.VMEM((8, length), f32),
            pltpu.VMEM((nh, WIDTH + ONES, length), f32),
        ],
        compiler_params=params(),
        cost_estimate=pl.CostEstimate(
            flops=2 * length * d * 3 * hw + 8 * length * length * hw, bytes_accessed=8_000_000, transcendentals=0
        ),
    )(counts, *xs, vec, w, wb)


def backward_kernel(blocks, nh, rows, image, at, first, counts, *refs):
    g_far = refs[:blocks]
    n1_far, qkv_far, full_far, lse_far, w_far = refs[blocks : blocks + 5]
    refs = refs[blocks + 5 :]
    if not first:
        dw_far, sums_in = refs[:2]
        refs = refs[2:]
    dw_out, sums, keep_out, pass_out = refs[:4]
    gats, n1, qkv, full, lse, w, dw, low, qt, qs, ks, vs, gs, kt, gt, delta, dqt, gall, n1t, load_sem, save_sem = refs[4:]
    hw = nh * WIDTH
    length = rows * blocks
    wide = gall.shape[1]
    count, me = counts[place(counts, image)], lax.axis_index("blk")
    loads = []

    def load(src, dst):
        loads.append(pltpu.make_async_copy(src, dst, load_sem.at[len(loads)]))
        loads[-1].start()
        return loads[-1]

    soon = [(load(g_far[m].at[at], gats.at[m]), load(qkv_far.at[m], qkv.at[m])) for m in range(blocks)]
    full_load, lse_load = load(full_far, full), load(lse_far, lse)
    late = [load(n1_far, n1), load(w_far, w)] + ([] if first else [load(dw_far, dw)])
    saves = []

    def save(src, dst):
        saves.append(pltpu.make_async_copy(src, dst, save_sem.at[len(saves)]))
        saves[-1].start()

    dqt[...] = jnp.zeros_like(dqt)
    if wide > 3 * hw:
        gall[:, 3 * hw :] = jnp.zeros((length, wide - 3 * hw), bf16)
    for m in range(blocks):
        rs = slice(m * rows, (m + 1) * rows)
        for item in soon[m]:
            item.wait()
        proj = qkv[m]
        turned = proj.T
        g = gats[m]
        gt[:, rs] = g
        gr = g.T
        for h in range(nh):
            sl = slice(h * WIDTH, (h + 1) * WIDTH)
            q, k, v = (slice((3 * h + i) * WIDTH, (3 * h + i + 1) * WIDTH) for i in range(3))
            qt[sl, rs] = turned[q, :] * score_scale
            kt[sl, rs] = turned[k, :]
            qs[h, rs, :] = proj[:, q] * score_scale
            ks[h, rs, :] = proj[:, k]
            vs[h, rs, :] = proj[:, v]
            gs[h, rs, :] = gr[:, sl]
    full_load.wait()
    lse_load.wait()
    for h in range(nh):
        sl = slice(h * WIDTH, (h + 1) * WIDTH)
        delta[h : h + 1, :] = jnp.sum(gt[sl, :].astype(f32) * full[sl, :], axis=0, keepdims=True)
    @pl.loop(0, blocks)
    def _(m):
        valid = count - (me ^ m) * rows
        rs = pl.ds(pl.multiple_of(m * rows, rows), rows)

        @pl.when(valid > 0)
        def _():
            keep = lax.broadcasted_iota(jnp.int32, (rows, 1), 0) < valid
            for h in range(nh):
                sl = slice(h * WIDTH, (h + 1) * WIDTH)
                s = dot_nn(ks[h, rs, :], qt[sl, :])
                s = jnp.where(keep, s, masked_value)
                p = jnp.exp(s - lse[h : h + 1, :])
                dp = dot_nn(vs[h, rs, :], gt[sl, :])
                ds = (p * (dp - delta[h : h + 1, :])).astype(bf16)
                gall[rs, (3 * h + 1) * WIDTH : (3 * h + 2) * WIDTH] = dot_nn(ds, qs[h]).astype(bf16)
                gall[rs, (3 * h + 2) * WIDTH : (3 * h + 3) * WIDTH] = dot_nn(p.astype(bf16), gs[h]).astype(bf16)
                dqt[sl, :] += dot_nn(kt[sl, rs], ds)

        @pl.when(valid <= 0)
        def _():
            gall[rs, : 3 * hw] = jnp.zeros((rows, 3 * hw), bf16)

    for item in late:
        item.wait()
    for m in range(blocks):
        rs = slice(m * rows, (m + 1) * rows)
        gq = (dqt[:, rs] * score_scale).T.astype(bf16)
        for h in range(nh):
            gall[rs, 3 * h * WIDTH : (3 * h + 1) * WIDTH] = gq[:, h * WIDTH : (h + 1) * WIDTH]
        n1t[:, rs] = n1[m].T
    term = dot_nn(n1t[...], gall[...])
    dw[...] = term if first else dw[...] + term
    save(dw, dw_out)
    d = n1.shape[2]
    second = jnp.zeros((1, d), f32)
    third = jnp.zeros((1, 3 * hw), f32)
    for m in range(blocks):
        g = gall[m * rows : (m + 1) * rows, : 3 * hw]
        gn = dot_nt(g, w[...])
        second += jnp.sum(gn, axis=0, keepdims=True)
        third += jnp.sum(g.astype(f32), axis=0, keepdims=True)
        low[m] = gn.astype(bf16)
        save(low.at[m], (pass_out if m % 2 else keep_out).at[m // 2])
    sums[...] = jnp.zeros_like(sums) if first else sums_in[...]
    sums[0:1, :] += second
    sums[1:2, : 3 * hw] += third
    for item in saves:
        item.wait()


def backward_image(counts, image, gats, at, n1, qkv, full, lse, w, before, wide, nh):
    blocks = len(gats)
    hw, rows = gats[0].shape[1:]
    length, d = rows * blocks, n1.shape[2]
    vm, far = pl.BlockSpec(memory_space=pltpu.VMEM), pl.BlockSpec(memory_space=pl.ANY)
    return pl.pallas_call(
        partial(backward_kernel, blocks, nh, rows, image, at, not before),
        name="attend_backward",
        in_specs=[pl.BlockSpec(memory_space=pltpu.SMEM)] + [far] * (blocks + 5) + ([far, vm] if before else []),
        out_specs=[far, vm, far, far],
        out_shape=[
            jax.ShapeDtypeStruct((d, wide), f32),
            jax.ShapeDtypeStruct((8, d), f32),
            jax.ShapeDtypeStruct((blocks // 2, rows, d), bf16),
            jax.ShapeDtypeStruct((blocks // 2, rows, d), bf16),
        ],
        scratch_shapes=[
            pltpu.VMEM((blocks, hw, rows), bf16),
            pltpu.VMEM((blocks, rows, d), bf16),
            pltpu.VMEM((blocks, rows, 3 * hw), bf16),
            pltpu.VMEM((hw, length), f32),
            pltpu.VMEM((8, length), f32),
            pltpu.VMEM((d, 3 * hw), bf16),
            pltpu.VMEM((d, wide), f32),
            pltpu.VMEM((blocks, rows, d), bf16),
            pltpu.VMEM((hw, length), bf16),
            pltpu.VMEM((nh, length, WIDTH), bf16),
            pltpu.VMEM((nh, length, WIDTH), bf16),
            pltpu.VMEM((nh, length, WIDTH), bf16),
            pltpu.VMEM((nh, length, WIDTH), bf16),
            pltpu.VMEM((hw, length), bf16),
            pltpu.VMEM((hw, length), bf16),
            pltpu.VMEM((8, length), f32),
            pltpu.VMEM((hw, length), f32),
            pltpu.VMEM((length, wide), bf16),
            pltpu.VMEM((d, length), bf16),
            pltpu.SemaphoreType.DMA((2 * blocks + 5,)),
            pltpu.SemaphoreType.DMA((blocks + 1,)),
        ],
        compiler_params=params(),
        cost_estimate=pl.CostEstimate(
            flops=4 * length * d * 3 * hw + 20 * length * length * hw, bytes_accessed=12_000_000, transcendentals=0
        ),
    )(counts, *gats, n1, qkv, full, lse, w, *before)


def flip(index, k):
    return index + (1 << k) * (1 - 2 * lax.rem(lax.div(index, 1 << k), 2))


def flip_all(index, mask):
    for k in range(mask.bit_length()):
        if mask >> k & 1:
            index = flip(index, k)
    return index


def meet(peers):
    barrier = pltpu.get_barrier_semaphore()
    for peer in peers:
        pl.semaphore_signal(barrier, inc=1, device_id=peer, device_id_type=pl.DeviceIdType.MESH)
    pl.semaphore_wait(barrier, len(peers))


def middle_kernel(blocks, images, steps, bits, *refs):
    count = blocks * images
    copies = 4 if bits else 2
    att_far = refs[:count]
    x_far, refs = refs[count : count + images], refs[count + images :]
    cot_far, vec, ow_far, b1, w1, w2 = refs[:6]
    refs = refs[6:]
    out_far, gmid_far, gb1, sums = refs[:4]
    grads_far, refs = refs[4 : 5 + copies], refs[5 + copies :]
    gats0, gats = refs[:blocks], refs[blocks : 2 * blocks]
    refs = refs[2 * blocks :]
    atts, x, cot, ow, out, gmid, load_sem, save_sem = refs[:8]
    grads, grad_sem, refs = refs[8 : 9 + copies], refs[9 + copies], refs[10 + copies :]
    (so, g1, g2), (to1, to2) = grads[:3], grads[3:] if bits else (None, None)
    (middle, branch, n2, gm, gn2, act, gpre, keep1, keep2, s1, r1, s2, r2, ds1, dr1, ds2, dr2, *second) = refs
    ga, gs, gr, as_, ar, gss, grs, *second = second
    t = pl.program_id(0)
    me, im = lax.axis_index("blk"), lax.axis_index("img")
    core = lax.rem(me, 2)
    hw, rows = atts.shape[1:]
    d = x.shape[1]
    width = d // 2
    total_rows = images * rows
    gain2, shift2, sc1, sc2 = vec[2:3, :], vec[3:4, :], vec[4:5, :], vec[5:6, :]
    bias_o, bias2 = vec[6:7, :], vec[7:8, :]
    mesh_id = pl.DeviceIdType.MESH
    near = {"blk": flip(me, 0)}
    kin = [{"blk": flip_all(me, m)} for m in range(1, blocks)]
    final = images - 1
    turn = [k % images for k in range(1, images + 1)]

    def halves(value):
        low, high = value[:, :width], value[:, width:]
        return jnp.where(core == 0, high, low), jnp.where(core == 0, low, high)

    def att(i, m):
        return ga[m - 1] if i == final and m else atts[i * blocks + m]

    brought = [k for k in range(count) if k // blocks < final or k % blocks == 0]
    loads = [(att_far[k], atts.at[k]) for k in brought] + [(ow_far, ow), (cot_far, cot)]
    loads += [(x_far[i], x.at[i * rows : (i + 1) * rows, :]) for i in range(images)]
    loads = [pltpu.make_async_copy(src, dst, load_sem.at[k]) for k, (src, dst) in enumerate(loads)]
    saves = [pltpu.make_async_copy(src, dst, save_sem.at[k]) for k, (src, dst) in enumerate(((out, out_far), (gmid, gmid_far)))]
    far = dict(zip(("so", "g1", "g2", "to1", "to2"), grads_far))
    here = dict(zip(("so", "g1", "g2", "to1", "to2"), grads))

    def save_grad(name, k):
        src, dst = here[name], far[name]
        if name in ("g1", "to1"):
            part = pl.ds(pl.multiple_of(k * width, width), width)
            src, dst = (src.at[:, :, part], dst.at[:, :, part]) if bits else (src.at[:, part], dst.at[:, part])
        elif name != "so":
            src, dst = (src.at[:, k], dst.at[:, k]) if bits else (src.at[k], dst.at[k])
        return pltpu.make_async_copy(src, dst, grad_sem.at[("so", "g1", "g2", "to1", "to2").index(name), k])
    if bits:
        half1, half2, u1, v1, u2, v2, us1, ur1, us2, ur2 = second
        peers = [{"img": flip(im, k)} for k in bits]
        where = [lax.rem(lax.div(im, 1 << k), 2) for k in bits]

    def cross(src, dst, send, recv, k, peer):
        return pltpu.make_async_remote_copy(
            src_ref=src.at[k],
            dst_ref=dst.at[k],
            send_sem=send.at[k],
            recv_sem=recv.at[k],
            device_id=peer,
            device_id_type=mesh_id,
        )

    def head_copy(m):
        return pltpu.make_async_remote_copy(
            src_ref=att_far[final * blocks + m],
            dst_ref=ga.at[m - 1],
            send_sem=as_.at[m - 1],
            recv_sem=ar.at[m - 1],
            device_id=kin[m - 1],
            device_id_type=mesh_id,
        )

    def split(keep, got, half, send, k, bit):
        parts, low = half.shape[0], half.shape[1]
        for i in range(parts):
            to = pl.ds(pl.multiple_of((2 * i + 1 - bit) * low, low), low)
            on = pl.ds(pl.multiple_of((2 * i + bit) * low, low), low)
            send[k, i] = (keep[to, :] + got[k, to, :].astype(f32)).astype(bf16)
            half[i] = keep[on, :] + got[k, on, :].astype(f32)

    def after_core(k):
        cross(s1, r1, ds1, dr1, k, near).wait()
        if bits:
            split(keep1, r1, half1, u1, k, where[0])
            cross(u1, v1, us1, ur1, k, peers[0]).start()
        else:
            g1[:, pl.ds(pl.multiple_of(k * width, width), width)] = (keep1[...] + r1[k].astype(f32)).astype(bf16)
            save_grad("g1", k).start()
        cross(s2, r2, ds2, dr2, k, near).wait()
        if bits:
            split(keep2, r2, half2, u2, k, where[1])
            cross(u2, v2, us2, ur2, k, peers[1]).start()
        else:
            g2[k] = (keep2[...] + r2[k].astype(f32)).astype(bf16)
            save_grad("g2", k).start()

    def after_bit(k):
        if not bits:
            return
        cross(u1, v1, us1, ur1, k, peers[0]).wait()
        columns = pl.ds(pl.multiple_of(k * width, width), width)
        low = g1.shape[1]
        for i in range(half1.shape[0]):
            for into, bit in ((to1, 1 - where[1]), (g1, where[1])):
                part = pl.ds(pl.multiple_of(bit * low, low), low)
                into[i, :, columns] = (half1[i, part, :] + v1[k, i, part, :].astype(f32)).astype(bf16)
        save_grad("to1", k).start()
        save_grad("g1", k).start()
        cross(u2, v2, us2, ur2, k, peers[1]).wait()
        whole = (half2[0] + v2[k, 0].astype(f32)).astype(bf16)
        low = g2.shape[2]
        half_chunk = lax.div(k, 2)
        same = lax.rem(k, 2) == where[0]

        def put(into, name):
            for i in range(2):
                into[i, half_chunk] = whole[i * low : (i + 1) * low, :]
            save_grad(name, half_chunk).start()

        pl.when(same)(lambda: put(g2, "g2"))
        pl.when(jnp.logical_not(same))(lambda: put(to2, "to2"))

    def enter(i):
        rs = slice(i * rows, (i + 1) * rows)
        total = jnp.zeros((rows, d), f32)
        for m in range(blocks):
            start = pl.multiple_of(flip_all(me, m) * hw, hw)
            total += dot_tn(att(i, m), ow[pl.ds(start, hw), :])
        total = total + bias_o
        branch[rs, :] = total
        mid = x[rs, :].astype(f32) + sc1 * total
        middle[rs, :] = mid
        z, _ = standardize(mid)
        n2[rs, :] = (z * gain2 + shift2).astype(bf16)
        gm[rs, :] = (sc2 * cot[rs, :].astype(f32)).astype(bf16)

    @pl.when(t == 0)
    def _():
        for load in loads:
            load.start()
        meet(kin + (peers if bits else []))
        for m in range(1, blocks):
            head_copy(m).start()
        gmid[...] = jnp.zeros_like(gmid)
        gn2[...] = jnp.zeros_like(gn2)
        for load in loads:
            load.wait()
        for i in range(final):
            enter(i)

    def forward(i):
        rs = slice(i * rows, (i + 1) * rows)
        hp = dot_nn(n2[rs, :], w1[...]) + b1[...]
        phi = 0.5 + 0.5 * lax.erf(hp * inv_sqrt2)
        act[rs, :] = (hp * phi).astype(bf16)
        slope = phi + hp * (jnp.exp(-0.5 * hp * hp) * inv_sqrt2pi)
        low = (dot_nt(gm[rs, :], w2[...]) * slope).astype(bf16)
        gpre[rs, :] = low

    @pl.when(t < steps)
    def _():
        for i in range(final):
            forward(i)

    @pl.when(t == 0)
    def _():
        for m in range(1, blocks):
            head_copy(m).wait()
        enter(final)

    @pl.when(t < steps)
    def _():
        forward(final)
        gb1[...] = dot_tn(gpre[...], jnp.ones((total_rows, 128), bf16))

    @pl.when(jnp.logical_and(t >= 2, t < steps))
    def _():
        after_bit(t - 2)

    @pl.when(jnp.logical_and(t >= 1, t < steps))
    def _():
        after_core(t - 1)

    @pl.when(t < steps)
    def _():
        send, keep = halves(dot_tn(n2[...], gpre[...]))
        s1[t] = send.astype(bf16)
        keep1[...] = keep
        cross(s1, r1, ds1, dr1, t, near).start()
        send, keep = halves(dot_tn(act[...], gm[...]))
        s2[t] = send.astype(bf16)
        keep2[...] = keep
        cross(s2, r2, ds2, dr2, t, near).start()
        gmid[...] += dot_nn(act[...], w2[...])
        gn2[...] += dot_nt(gpre[...], w1[...])

    @pl.when(t == steps)
    def _():
        after_bit(steps - 2)
        after_core(steps - 1)
        zero = jnp.zeros((1, d), f32)
        g_s2, g_b2, g_gain, g_shift, g_s1, g_bo = zero, zero, zero, zero, zero, zero
        for i in turn:
            rs = slice(i * rows, (i + 1) * rows)
            mid = middle[rs, :]
            mo = gmid[rs, :] + bias2
            out[rs, :] = (mid + sc2 * mo).astype(bf16)
            go = cot[rs, :].astype(f32)
            g_s2 += jnp.sum(go * mo, axis=0, keepdims=True)
            g_b2 += jnp.sum(gm[rs, :].astype(f32), axis=0, keepdims=True)
            g = gn2[rs, :]
            z, inverse = standardize(mid)
            g_gain += jnp.sum(g * z, axis=0, keepdims=True)
            g_shift += jnp.sum(g, axis=0, keepdims=True)
            q = g * gain2
            gmd = go + inverse * (
                q - jnp.mean(q, axis=-1, keepdims=True) - z * jnp.mean(q * z, axis=-1, keepdims=True)
            )
            gmid[rs, :] = gmd
            g_s1 += jnp.sum(gmd * branch[rs, :], axis=0, keepdims=True)
            gb = (sc1 * gmd).astype(bf16)
            n2[rs, :] = gb
            g_bo += jnp.sum(gb.astype(f32), axis=0, keepdims=True)
            if i == turn[0]:
                for m in list(range(1, blocks)) + [0]:
                    start = pl.ds(pl.multiple_of(flip_all(me, m) * hw, hw), hw)
                    first = dot_nt(ow[start, :], gb).astype(bf16)
                    if m == 0:
                        gats0[0][0] = first
                    else:
                        gs[m - 1] = first
                        cross(gs, gr, gss, grs, m - 1, kin[m - 1]).start()
        for item in saves:
            item.start()
        sums[...] = jnp.concatenate([g_s2, g_b2, g_gain, g_shift, g_s1, g_bo, zero, zero], axis=0)
        for m in range(blocks):
            start = pl.ds(pl.multiple_of(flip_all(me, m) * hw, hw), hw)
            term = jnp.zeros((hw, d), f32)
            for i in range(images):
                term += dot_nn(att(i, m), n2[i * rows : (i + 1) * rows, :])
            send, keep = halves(term)
            s1[steps, start, :] = send.astype(bf16)
            keep1[start, :] = keep
        cross(s1, r1, ds1, dr1, steps, near).start()
        for m in range(blocks):
            start = pl.ds(pl.multiple_of(flip_all(me, m) * hw, hw), hw)
            for k, i in enumerate(turn[1:]):
                gats[m][k] = dot_nt(ow[start, :], n2[i * rows : (i + 1) * rows, :]).astype(bf16)
        cross(s1, r1, ds1, dr1, steps, near).wait()
        so[...] = (keep1[...] + r1[steps].astype(f32)).astype(bf16)
        save_grad("so", 0).start()
        for m in range(1, blocks):
            cross(gs, gr, gss, grs, m - 1, kin[m - 1]).wait()
            gats0[m][0] = gr[m - 1]
        after_bit(steps - 1)
        for item in saves:
            item.wait()
        save_grad("so", 0).wait()
        for name in ("g1", "to1") if bits else ("g1",):
            for k in range(steps):
                save_grad(name, k).wait()
        for name in ("g2", "to2") if bits else ("g2",):
            for k in range(g2.shape[1] if bits else steps):
                save_grad(name, k).wait()


def middle_layers(atts, xs, cot, vec, ow, b1, w1, w2, blocks, images, share, bits):
    hw, rows = atts[0].shape
    total, d = cot.shape
    ff = w1.shape[1]
    chunk, width = d, d // 2
    steps = ff // chunk
    once = dict(pipeline_mode=pl.Buffered(1))
    whole = lambda shape: pl.BlockSpec(shape, lambda j: (0,) * len(shape), **once)
    last = lambda j: jnp.minimum(j, steps - 1)
    if bits:
        low1, low2 = (blocks * share) << bits[0], (blocks * ff * share // d) << bits[1]
        shape1 = (d // (2 * low1), low1)
        shape2 = (chunk // (2 * low2), low2)
        g1_shape = (shape1[0], low1 // 2, steps * width)
        g2_shape = (2, steps // 2, low2 // 2, width)
        second = [
            pltpu.VMEM(shape1 + (width,), f32),
            pltpu.VMEM(shape2 + (width,), f32),
            pltpu.VMEM((steps,) + shape1 + (width,), bf16),
            pltpu.VMEM((steps,) + shape1 + (width,), bf16),
            pltpu.VMEM((steps,) + shape2 + (width,), bf16),
            pltpu.VMEM((steps,) + shape2 + (width,), bf16),
        ] + [pltpu.SemaphoreType.DMA((steps,))] * 4
    else:
        g1_shape, g2_shape, second = (d, steps * width), (steps, chunk, width), []
    grad_shapes = [(d, width)] + [g1_shape, g2_shape] * (2 if bits else 1)
    far = pl.BlockSpec(memory_space=pl.ANY)
    swaps = pltpu.SemaphoreType.DMA((blocks - 1,))
    second = [pltpu.VMEM((blocks - 1, hw, rows), bf16)] * 3 + [swaps] * 4 + second
    return pl.pallas_call(
        partial(middle_kernel, blocks, images, steps, bits),
        name="middle_layers",
        grid=(steps + 1,),
        in_specs=[far] * (blocks * images)
        + [far] * images
        + [
            far,
            whole(vec.shape),
            far,
            pl.BlockSpec((1, chunk), lambda j: (0, last(j))),
            pl.BlockSpec((d, chunk), lambda j: (0, last(j))),
            pl.BlockSpec((chunk, d), lambda j: (last(j), 0)),
        ],
        out_specs=[
            far,
            far,
            pl.BlockSpec((chunk, 128), lambda j: (last(j), 0)),
            whole((8, d)),
        ]
        + [far] * len(grad_shapes)
        + [whole((1, hw, rows))] * blocks
        + [whole((images - 1, hw, rows))] * blocks,
        out_shape=[
            jax.ShapeDtypeStruct((total, d), bf16),
            jax.ShapeDtypeStruct((total, d), f32),
            jax.ShapeDtypeStruct((ff, 128), f32),
            jax.ShapeDtypeStruct((8, d), f32),
        ]
        + [jax.ShapeDtypeStruct(v, bf16) for v in grad_shapes]
        + [jax.ShapeDtypeStruct((1, hw, rows), bf16)] * blocks
        + [jax.ShapeDtypeStruct((images - 1, hw, rows), bf16)] * blocks,
        scratch_shapes=[
            pltpu.VMEM((blocks * images, hw, rows), bf16),
            pltpu.VMEM((total, d), bf16),
            pltpu.VMEM((total, d), bf16),
            pltpu.VMEM((d, d), bf16),
            pltpu.VMEM((total, d), bf16),
            pltpu.VMEM((total, d), f32),
            pltpu.SemaphoreType.DMA((blocks * images + images + 2,)),
            pltpu.SemaphoreType.DMA((2,)),
        ]
        + [pltpu.VMEM(v, bf16) for v in grad_shapes]
        + [
            pltpu.SemaphoreType.DMA((5, steps)),
            pltpu.VMEM((total, d), f32),
            pltpu.VMEM((total, d), f32),
            pltpu.VMEM((total, d), bf16),
            pltpu.VMEM((total, d), bf16),
            pltpu.VMEM((total, d), f32),
            pltpu.VMEM((total, chunk), bf16),
            pltpu.VMEM((total, chunk), bf16),
            pltpu.VMEM((d, width), f32),
            pltpu.VMEM((chunk, width), f32),
            pltpu.VMEM((steps + 1, d, width), bf16),
            pltpu.VMEM((steps + 1, d, width), bf16),
            pltpu.VMEM((steps, chunk, width), bf16),
            pltpu.VMEM((steps, chunk, width), bf16),
            pltpu.SemaphoreType.DMA((steps + 1,)),
            pltpu.SemaphoreType.DMA((steps + 1,)),
            pltpu.SemaphoreType.DMA((steps,)),
            pltpu.SemaphoreType.DMA((steps,)),
        ]
        + second,
        compiler_params=params(dimension_semantics=("arbitrary",), collective_id=1, has_side_effects=True),
        cost_estimate=pl.CostEstimate(
            flops=12 * total * d * ff + 6 * total * d * d, bytes_accessed=30_000_000, transcendentals=0
        ),
    )(*atts, *xs, cot, vec, ow, b1, w1, w2)


def norm_back(x, gain, g):
    z, inverse = standardize(x.astype(f32))
    q = g * gain
    return inverse * (q - jnp.mean(q, axis=-1, keepdims=True) - z * jnp.mean(q * z, axis=-1, keepdims=True))


SMALL = 14


def last_kernel(blocks, nh, rows, share, at_piece, *refs):
    far_refs, refs = refs[:LAST_IN], refs[LAST_IN:]
    tok, e_out, o1, o2 = refs[:4]
    here, refs = refs[4 : 4 + LAST_IN], refs[4 + LAST_IN :]
    (qt, qs, ks, vs, gs, kt, gt, delta, dqt, gall, n1t, low) = refs[:12]
    (small, ext, fin, rxf, sa1, ra1, sb1, rb1, sc1, rc1, sa2, ra2, sb2, rb2, sc2, rc2) = refs[12:28]
    (sa3, ra3, sb3, rb3, sc3, rc3, sx, rx, sc, rc) = refs[28:38]
    (near_b, near_c, step, got, sz1, rz1, sg1, rg1, cg1, dg1, sg2, rg2, cg2, dg2, send_sem, recv_sem, load_sem) = refs[38:]
    gats, (n1, qkv, full, lse, w, dw, sums1, kept_a, near_a, kept_b, passed_b) = here[:4], here[4:15]
    (g1, g1y, g2, g2z, g2x, so, sums, vec, gb, gmid, *x) = here[15:]
    me, im = lax.axis_index("blk"), lax.axis_index("img")
    core, xx = lax.rem(me, 2), lax.div(me, 2)
    y, z0, z1 = lax.rem(im, 2), lax.rem(lax.div(im, 2), 2), lax.div(im, 4)
    to_core, to_x = {"blk": flip(me, 0)}, {"blk": flip(me, 1)}
    to_y, to_z0, to_z1 = {"img": flip(im, 0)}, {"img": flip(im, 1)}, {"img": flip(im, 2)}
    d = n1.shape[2]
    hw, chip, four = nh * WIDTH, 2 * share, 4 * share
    wide = dw.shape[1]
    cut = sa1.shape[2]
    used = w.shape[1]
    slots = iter(range(send_sem.shape[0]))
    loads = [
        pltpu.make_async_copy(far.at[at_piece] if k < 4 else far, here[k], load_sem.at[k]) for k, far in enumerate(far_refs)
    ]
    for load in loads:
        load.start()

    def need(*wanted):
        for k in range(LAST_IN):
            if any(here[k] is item for item in wanted):
                loads[k].wait()

    def copy(src, dst, peer):
        k = next(slots)
        return pltpu.make_async_remote_copy(
            src_ref=src,
            dst_ref=dst,
            send_sem=send_sem.at[k],
            recv_sem=recv_sem.at[k],
            device_id=peer,
            device_id_type=pl.DeviceIdType.MESH,
        )

    def at(block, size):
        return pl.ds(pl.multiple_of(block * size, size), size)

    def rows_of(i, j, k):
        return at((2 * i + j) * 2 + k, four)

    meet([to_core, to_x, to_y, to_z0, to_z1])
    need(passed_b)
    pass_b = copy(passed_b, near_b, to_core)
    pass_b.start()
    need(kept_a, near_a)
    step[0] = (kept_a[1].astype(f32) + near_a[1].astype(f32)).astype(bf16)
    step_a = copy(step.at[0], got.at[0], to_x)
    step_a.start()
    need(so)
    for i in range(2):
        for j in range(2):
            sc1[i, j] = so[rows_of(i, j, 1 - y), :]
    c1 = copy(sc1, rc1, to_y)
    c1.start()

    def sum_1(block):
        return g1[block].astype(f32) + g1y[block].astype(f32)

    need(g1, g1y)
    sz1[...] = sum_1(1 - z1).astype(bf16)
    g1_z = copy(sz1, rz1, to_z1)
    g1_z.start()

    need(qkv, full, lse, *gats)
    dqt[...] = jnp.zeros_like(dqt)
    gall[:, 3 * hw :] = jnp.zeros((gall.shape[0], wide - 3 * hw), bf16)
    for m in range(blocks):
        rs = slice(m * rows, (m + 1) * rows)
        proj = qkv[m]
        turned = proj.T
        g = gats[m][...]
        gt[:, rs] = g
        gr = g.T
        for h in range(nh):
            sl = slice(h * WIDTH, (h + 1) * WIDTH)
            q, k, v = (slice((3 * h + i) * WIDTH, (3 * h + i + 1) * WIDTH) for i in range(3))
            qt[sl, rs] = turned[q, :] * score_scale
            kt[sl, rs] = turned[k, :]
            qs[h, rs, :] = proj[:, q] * score_scale
            ks[h, rs, :] = proj[:, k]
            vs[h, rs, :] = proj[:, v]
            gs[h, rs, :] = gr[:, sl]
    for h in range(nh):
        sl = slice(h * WIDTH, (h + 1) * WIDTH)
        delta[h : h + 1, :] = jnp.sum(gt[sl, :].astype(f32) * full[sl, :], axis=0, keepdims=True)

    def attend(h):
        sl = slice(h * WIDTH, (h + 1) * WIDTH)

        @pl.loop(0, blocks)
        def _(m):
            rs = at(m, rows)
            s = dot_nn(ks[h, rs, :], qt[sl, :])
            p = jnp.exp(s - lse[h : h + 1, :])
            dp = dot_nn(vs[h, rs, :], gt[sl, :])
            ds = (p * (dp - delta[h : h + 1, :])).astype(bf16)
            gall[rs, (3 * h + 1) * WIDTH : (3 * h + 2) * WIDTH] = dot_nn(ds, qs[h]).astype(bf16)
            gall[rs, (3 * h + 2) * WIDTH : (3 * h + 3) * WIDTH] = dot_nn(p.astype(bf16), gs[h]).astype(bf16)
            dqt[sl, :] += dot_nn(kt[sl, rs], ds)

        gall[:, 3 * h * WIDTH : (3 * h + 1) * WIDTH] = (dqt[sl, :] * score_scale).T.astype(bf16)

    pass_b.wait()
    need(kept_b)
    step[1] = (kept_b[1].astype(f32) + near_b[1].astype(f32)).astype(bf16)
    step_b = copy(step.at[1], got.at[1], to_x)
    step_b.start()

    for h in range(nh - 1):
        attend(h)
    need(n1, dw)
    for m in range(blocks):
        n1t[:, m * rows : (m + 1) * rows] = n1[m].T
    dw[:, :cut] += dot_nn(n1t[...], gall[:, :cut])
    for i in range(2):
        for j in range(2):
            sa1[2 * i + j] = dw[rows_of(i, j, 1 - y), :cut].astype(bf16)
    a1 = copy(sa1, ra1, to_y)
    a1.start()
    c1.wait()
    for i in range(2):
        sc2[i] = (so[rows_of(i, 1 - z0, y), :].astype(f32) + rc1[i, 1 - z0].astype(f32)).astype(bf16)
    c2 = copy(sc2, rc2, to_z0)
    c2.start()

    def terms2(block):
        return g2[xx, block].astype(f32) + g2z[xx, block].astype(f32) + g2x[block].astype(f32)

    need(g2, g2z, g2x)
    sg2[...] = terms2(1 - z1).astype(bf16)
    g2_z = copy(sg2, rg2, to_z1)
    g2_z.start()

    attend(nh - 1)
    need(w)
    second = jnp.zeros((1, d), f32)
    for m in (1, 3, 2, 0):
        gn = dot_nt(gall[m * rows : (m + 1) * rows, :used], w[...])
        second += jnp.sum(gn, axis=0, keepdims=True)
        low[m // 2 + 2 * (m % 2)] = gn.astype(bf16)
        if m == 3:
            pass_c = copy(low.at[2:4], near_c, to_core)
            pass_c.start()
    third = jnp.sum(gall[:, :used].astype(f32), axis=0, keepdims=True)

    need(sums, sums1, gb, vec)
    rest = wide - cut
    ext[...] = dw[:, cut:] + dot_nn(n1t[...], gall[:, cut:])
    small[...] = jnp.zeros_like(small)
    half = rest - 128
    base = used - cut - half
    third = third + sums1[1:2, :used]

    def placed(part):
        row = jnp.concatenate([third[:, (3 * h + part) * WIDTH : (3 * h + part + 1) * WIDTH] for h in range(nh)], axis=1)
        spread = jnp.zeros((1, d), f32)
        for b in range(blocks):
            pieces = [jnp.zeros((1, hw), f32) if k != b else row for k in range(blocks)]
            spread = jnp.where(me == b, jnp.concatenate(pieces, axis=1), spread)
        return spread

    rows_in = [placed(0), placed(2), sums[5:6], None, second + sums1[0:1], sums[2:3], sums[3:4], sums[1:2], sums[4:5], sums[0:1]]
    for k, row in enumerate(rows_in):
        if row is not None:
            small[base + k : base + k + 1, :] = row
    small[base + SMALL : base + SMALL + 2, :] = vec[0:2, :]
    turned = small[...].T
    lane = lax.broadcasted_iota(jnp.int32, (1, 128), 1)
    gain_c, bias_c = turned[:, base + SMALL : base + SMALL + 1], turned[:, base + SMALL + 1 : base + SMALL + 2]
    n1b_c = turned[:, base + 4 : base + 5]
    total = jnp.sum(dw[:, :cut] * w[:, :cut].astype(f32), axis=1, keepdims=True)
    total += jnp.sum(ext[:, : used - cut] * w[:, cut:].astype(f32), axis=1, keepdims=True)
    n1g_c = (total - bias_c * n1b_c) / gain_c
    ext[:, half:] += jnp.where(lane == base + 3, n1g_c, jnp.where(lane < base + 10, turned, 0.0))
    per = SMALL - 10
    for k in range(d // share):
        column = jnp.zeros((share, 128), f32)
        for q in range(per):
            column = jnp.where(lane == base + 10 + q, gb[(per * k + q) * share : (per * k + q + 1) * share, :], column)
        ext[k * share : (k + 1) * share, half:] += column
    for i in range(2):
        for k in range(2):
            sb1[i, k] = ext[rows_of(i, 1 - z0, k), :].astype(bf16)
    b1 = copy(sb1, rb1, to_z0)
    b1.start()

    def chip_rows(block):
        part = at(block, chip)
        return g1[z1, part, :].astype(f32) + g1y[z1, part, :].astype(f32) + rz1[part, :].astype(f32)

    g1_z.wait()
    sg1[...] = chip_rows(1 - xx).astype(bf16)
    g1_x = copy(sg1, rg1, to_x)
    g1_x.start()
    pass_c.wait()
    step[2] = (low[1].astype(f32) + near_c[1].astype(f32)).astype(bf16)
    step_c = copy(step.at[2], got.at[2], to_x)
    step_c.start()

    a1.wait()
    for i in range(2):
        sa2[i] = (dw[rows_of(i, 1 - z0, y), :cut] + ra1[2 * i + 1 - z0].astype(f32)).astype(bf16)
    a2 = copy(sa2, ra2, to_z0)
    a2.start()

    def sum_a(i):
        return dw[rows_of(i, z0, y), :cut] + ra1[2 * i + z0].astype(f32) + ra2[i].astype(f32)

    def sum_b(i):
        return ext[rows_of(i, z0, y), :] + rb1[i, y].astype(f32) + rb2[i].astype(f32)

    def sum_c(i):
        return so[rows_of(i, z0, y), :].astype(f32) + rc1[i, z0].astype(f32) + rc2[i].astype(f32)

    c2.wait()
    sc3[...] = sum_c(1 - z1).astype(bf16)
    c3 = copy(sc3, rc3, to_z1)
    c3.start()

    need(gmid, *x)
    gain = vec[0:1, :]

    def finish(i, g):
        tok[i] = (gmid[i * rows : (i + 1) * rows, :] + norm_back(x[i][...], gain, g)).astype(bf16)

    b1.wait()
    for i in range(2):
        sb2[i] = (ext[rows_of(i, z0, 1 - y), :] + rb1[i, 1 - y].astype(f32)).astype(bf16)
    b2 = copy(sb2, rb2, to_y)
    b2.start()
    step_a.wait()
    finish(1, kept_a[0].astype(f32) + near_a[0].astype(f32) + got[0].astype(f32))
    a2.wait()
    sa3[...] = sum_a(1 - z1).astype(bf16)
    a3 = copy(sa3, ra3, to_z1)
    a3.start()
    b2.wait()
    sb3[...] = sum_b(1 - z1).astype(bf16)
    b3 = copy(sb3, rb3, to_z1)
    b3.start()

    g1_x.wait()
    cg1[...] = chip_rows(xx) + rg1[...].astype(f32)
    dg1_copy = copy(cg1.at[at(1 - core, share), :], dg1, to_core)
    dg1_copy.start()
    g2_z.wait()
    cg2[...] = terms2(z1) + rg2[...].astype(f32)
    wide2 = cg2.shape[0] // 2
    dg2_copy = copy(cg2.at[at(1 - core, wide2), :], dg2, to_core)
    dg2_copy.start()
    step_b.wait()
    finish(2, kept_b[0].astype(f32) + near_b[0].astype(f32) + got[1].astype(f32))

    c3.wait()
    fin[:, wide:] = sum_c(z1) + rc3[...].astype(f32)
    a3.wait()
    fin[:, :cut] = sum_a(z1) + ra3[...].astype(f32)
    b3.wait()
    fin[:, cut:wide] = sum_b(z1) + rb3[...].astype(f32)
    sx[...] = fin[at(1 - xx, chip), :].astype(bf16)
    x_copy = copy(sx, rx, to_x)
    x_copy.start()

    dg1_copy.wait()
    o1[core] = cg1[at(core, share), :]
    o1[1 - core] = dg1[...]
    dg2_copy.wait()
    o2[core] = cg2[at(core, wide2), :]
    o2[1 - core] = dg2[...]
    step_c.wait()
    finish(0, low[0].astype(f32) + near_c[0].astype(f32) + got[2].astype(f32))

    x_copy.wait()
    rxf[...] = rx[...].astype(f32)
    sc[0] = fin[at(2 * xx + 1 - core, share), :]
    sc[1] = rxf[at(1 - core, share), :]
    c_copy = copy(sc, rc, to_core)
    c_copy.start()
    e_out[0] = fin[at(2 * xx + core, share), :]
    e_out[2] = rxf[at(core, share), :]
    c_copy.wait()
    e_out[1] = rc[0]
    e_out[3] = rc[1]


LAST_IN = 28


def last_image(share, shape, wide, c1, r2, c2, nh, at_piece, *args):
    images, rows, d = shape
    blocks, hw = 4, nh * WIDTH
    length = blocks * rows
    four, chip = 4 * share, 2 * share
    both = wide + d // 2
    cut = 2 * 3 * WIDTH
    rest = wide - cut
    vm = pl.BlockSpec(memory_space=pltpu.VMEM)
    pair = lambda shape, dtype=bf16: [pltpu.VMEM(shape, dtype)] * 2
    heads = pltpu.VMEM((nh, length, WIDTH), bf16)
    flat = pltpu.VMEM((hw, length), bf16)
    copies = 21
    return pl.pallas_call(
        partial(last_kernel, blocks, nh, rows, share, at_piece),
        name="last",
        in_specs=[pl.BlockSpec(memory_space=pl.ANY)] * LAST_IN,
        out_specs=[vm] * 4,
        out_shape=[
            jax.ShapeDtypeStruct(shape, bf16),
            jax.ShapeDtypeStruct((4, share, both), f32),
            jax.ShapeDtypeStruct((2, share, c1), f32),
            jax.ShapeDtypeStruct((2, r2 // 2, c2), f32),
        ],
        scratch_shapes=[pltpu.VMEM(v.shape[1:] if k < 4 else v.shape, v.dtype) for k, v in enumerate(args)]
        + [flat, heads, heads, heads, heads, flat, flat]
        + [
            pltpu.VMEM((8, length), f32),
            pltpu.VMEM((hw, length), f32),
            pltpu.VMEM((length, wide), bf16),
            pltpu.VMEM((d, length), bf16),
            pltpu.VMEM((blocks, rows, d), bf16),
            pltpu.VMEM((128, d), f32),
            pltpu.VMEM((d, rest), f32),
            pltpu.VMEM((four, both), f32),
            pltpu.VMEM((chip, both), f32),
        ]
        + pair((4, four, cut))
        + pair((2, 2, four, rest))
        + pair((2, 2, four, d // 2))
        + pair((2, four, cut))
        + pair((2, four, rest))
        + pair((2, four, d // 2))
        + pair((four, cut))
        + pair((four, rest))
        + pair((four, d // 2))
        + pair((chip, both))
        + pair((2, share, both), f32)
        + pair((2, rows, d))
        + pair((3, rows, d))
        + pair((four, c1))
        + pair((chip, c1))
        + [pltpu.VMEM((chip, c1), f32), pltpu.VMEM((share, c1), f32)]
        + pair((r2, c2))
        + [pltpu.VMEM((r2, c2), f32), pltpu.VMEM((r2 // 2, c2), f32)]
        + [
            pltpu.SemaphoreType.DMA((copies,)),
            pltpu.SemaphoreType.DMA((copies,)),
            pltpu.SemaphoreType.DMA((LAST_IN,)),
        ],
        compiler_params=params(collective_id=2, has_side_effects=True),
        cost_estimate=pl.CostEstimate(flops=30_000_000_000, bytes_accessed=20_000_000, transcendentals=0),
    )(*args)


def layout_kernel(nh, counts, tok, out, e, o1, o2, *outs):
    tok_out, out_out, qkv_out, ow_out, fc1_out, fc2_out, b1_out = outs[:7]
    vectors = outs[7:]
    images, rows = tok.shape[:2]
    for k in range(images):
        into = place(counts, k)
        tok_out[into] = tok[k]
        out_out[into] = out[k * rows : (k + 1) * rows, :]
    me = lax.axis_index("blk")
    core = lax.rem(me, 2)
    hw = nh * WIDTH
    d = tok.shape[2]
    half = d // 2
    share = e.shape[1]
    order = [e[flip_all(me, b)] for b in range(e.shape[0])]
    for k in range(3):
        pieces = [v[:, (3 * h + k) * WIDTH : (3 * h + k + 1) * WIDTH] for v in order for h in range(nh)]
        qkv_out[:, k * d : (k + 1) * d] = jnp.concatenate(pieces, axis=1)
    for k in range(o1.shape[2] // half):
        for h in range(2):
            fc1_out[:, k * d + h * half : k * d + (h + 1) * half] = o1[h, :, k * half : (k + 1) * half]
    for h in range(2):
        fc2_out[:, h * half : (h + 1) * half] = o2[h]
    wide = e.shape[2] - half
    parts = [e[k, :, wide:] + e[k + 2, :, wide:] for k in range(2)]
    ow_out[:, :half] = jnp.where(core == 0, parts[0], parts[1])
    ow_out[:, half:] = jnp.where(core == 0, parts[1], parts[0])
    total = order[0][:, wide - 128 : wide]
    for v in order[1:]:
        total = total + v[:, wide - 128 : wide]
    base = 3 * hw - (wide - 128)
    turned = total.T
    for k in range(10):
        vectors[k][...] = turned[base + k : base + k + 1, :]
    for k in range(SMALL - 10):
        b1_out[:, k * share : (k + 1) * share] = turned[base + 10 + k : base + 11 + k, :]


def layout(counts, tok, out, e, o1, o2, nh, ff):
    share, d = e.shape[1], tok.shape[2]
    vm = pl.BlockSpec(memory_space=pltpu.VMEM)
    shapes = [(share, 3 * d), (share, d), (share, ff), (o2.shape[1], d), (1, ff * share // d)] + [(1, share)] * 10
    return pl.pallas_call(
        partial(layout_kernel, nh),
        name="layout",
        in_specs=[pl.BlockSpec(memory_space=pltpu.SMEM)] + [vm] * 5,
        out_specs=[vm] * (2 + len(shapes)),
        out_shape=[jax.ShapeDtypeStruct(tok.shape, bf16)] * 2 + [jax.ShapeDtypeStruct(v, f32) for v in shapes],
        compiler_params=params(),
    )(counts, tok, out, e, o1, o2)


def finish_kernel(x, gmid, gain, *refs):
    out = refs[-1]
    terms = refs[:-1]
    images, rows = x.shape[0], x.shape[1]
    per = len(terms) // images
    for i in range(images):
        z, inverse = standardize(x[i].astype(f32))
        g = sum(terms[i * per + k][0].astype(f32) for k in range(per))
        q = g * gain[...]
        term = inverse * (q - jnp.mean(q, axis=-1, keepdims=True) - z * jnp.mean(q * z, axis=-1, keepdims=True))
        out[i] = (gmid[i * rows : (i + 1) * rows, :] + term).astype(bf16)


def finish(x, gmid, gain, terms):
    rows, d = x.shape[1:]
    images = x.shape[0]
    vm = pl.BlockSpec(memory_space=pltpu.VMEM)
    head = pl.BlockSpec((1, rows, d), lambda i: (0, 0, 0))
    return pl.pallas_call(
        finish_kernel,
        name="finish_tokens",
        grid=(1,),
        in_specs=[vm, vm, vm] + [head] * len(terms),
        out_specs=vm,
        out_shape=jax.ShapeDtypeStruct(x.shape, bf16),
        compiler_params=params(),
    )(x, gmid, gain, *terms)


class Places:
    def __init__(self, mesh):
        self.n_img, self.n_blk = mesh.shape["img"], mesh.shape["blk"]
        self.img_bits = self.n_img.bit_length() - 1
        self.blk_bits = self.n_blk.bit_length() - 1
        self.img, self.blk = lax.axis_index("img"), lax.axis_index("blk")
        self.dims = [("img", k) for k in reversed(range(self.img_bits))] + [
            ("blk", k) for k in reversed(range(self.blk_bits))
        ]

    def bit(self, dim):
        axis, k = dim
        return ((self.img if axis == "img" else self.blk) >> k) & 1

    def swap(self, value, dim):
        axis, k = dim
        n = self.n_img if axis == "img" else self.n_blk
        return lax.ppermute(value, axis, [(i, i ^ (1 << k)) for i in range(n)])


class Halving:
    def __init__(self, places, own, dims, link=bf16):
        self.places, self.link, self.body, self.dims = places, link, own.shape[1:], dims
        self.terms = [(own.reshape((2,) * len(dims) + self.body), list(dims))]
        self.known = {}

    def part(self, term, known):
        value, has = term
        starts = [known[d] if d in known else 0 for d in has] + [0] * len(self.body)
        sizes = [1 if d in known else 2 for d in has] + list(self.body)
        left = [2 for d in has if d not in known]
        return lax.dynamic_slice(value, starts, sizes).reshape(tuple(left) + self.body).astype(f32)

    def add(self, known):
        total = self.part(self.terms[0], known)
        for term in self.terms[1:]:
            total = total + self.part(term, known)
        return total

    def send(self, dim):
        return self.add({**self.known, dim: 1 - self.places.bit(dim)}).astype(self.link)

    def swap(self, send, dim):
        self.known[dim] = self.places.bit(dim)
        self.terms.append((self.places.swap(send, dim), [d for d in self.dims if d not in self.known]))

    def hold(self, done):
        value, has = self.terms[-1]
        self.terms[-1] = (lax.optimization_barrier((value, done))[0], has)

    def rest(self):
        return self.add(self.known)


def scatter_sum(places, own, dims, order, link=bf16):
    work = Halving(places, own, dims, link)
    for dim in order:
        work.swap(work.send(dim), dim)
    return work.rest()


def solution(mesh):
    def per_device(
        tokens,
        counts,
        qkv_weight,
        q_bias,
        v_bias,
        out_weight,
        out_bias,
        norm1_gain,
        norm1_bias,
        norm2_gain,
        norm2_bias,
        fc1_weight,
        fc1_bias,
        fc2_weight,
        fc2_bias,
        scale1,
        scale2,
        cotangent,
    ):
        places = Places(mesh)
        images, rows, d = tokens.shape
        blocks = places.n_blk
        nh = HEADS // blocks
        hw = nh * WIDTH
        total = images * rows
        me = places.blk
        vec = jnp.stack(
            [norm1_gain, norm1_bias, norm2_gain, norm2_bias, scale1, scale2, out_bias, fc2_bias]
        ).astype(f32)
        def own_heads(value):
            pieces = [lax.dynamic_slice_in_dim(value, k * d + me * hw, hw, value.ndim - 1) for k in range(3)]
            pieces = [v.reshape(v.shape[:-1] + (nh, 1, WIDTH)) for v in pieces]
            return jnp.concatenate(pieces, axis=-2).reshape(value.shape[:-1] + (3 * hw,))

        w = own_heads(qkv_weight)
        wb = own_heads(jnp.concatenate([q_bias, jnp.zeros((d,), bf16), v_bias])).astype(f32)[None, :]

        def after(values, *done):
            return lax.optimization_barrier((list(values), done))[0]

        def swap_blk(value, m):
            return lax.ppermute(value, "blk", [(b, b ^ m) for b in range(blocks)])

        lead = jnp.argmax(counts).astype(jnp.int32)

        def turned(value):
            return [
                lax.dynamic_index_in_dim(value, lax.rem(lead + k, images), 0, keepdims=False) for k in range(images)
            ]

        mine = turned(tokens)
        saved, atts = [], []
        for i in range(images):
            found = {0: mine[i]}
            for k in reversed(range(places.blk_bits)):
                if k == 0:
                    found = dict(zip(found, after(list(found.values()), *((w, wb, vec) if i == 0 else saved[-1][3:]))))
                found.update({m | 1 << k: swap_blk(v, 1 << k) for m, v in found.items()})
            xs = [found[m] for m in range(blocks)]
            n1, qkv, full, lse, *outs = forward_image(counts, i, xs, vec, w, wb, nh)
            saved.append((n1, qkv, full, lse))
            atts.extend([outs[0]] + [swap_blk(outs[m], m) if i < images - 1 else outs[m] for m in range(1, blocks)])
        n = places.n_img * blocks
        share = d // n
        ff = fc1_weight.shape[1]
        half = d // 2
        y_bit, z_bit = 0, 1
        bits = (z_bit, y_bit) if share % 8 == 0 and (places.img_bits, places.blk_bits, images) == (3, 2, 3) else ()
        out, gmid, gb1, sums, so, g1, g2, *gats = middle_layers(
            atts,
            mine,
            jnp.concatenate(turned(cotangent)),
            vec,
            out_weight,
            fc1_bias.astype(f32)[None, :],
            fc1_weight,
            fc2_weight,
            blocks,
            images,
            share,
            bits,
        )
        if bits:
            img2, img1, img0, x_dim = ("img", 2), ("img", 1), ("img", 0), ("blk", 1)
            to1, to2, *gats = gats
            wide = -(-3 * hw // 128) * 128
            firsts = gats[:blocks]
            others = [gats[blocks]] + [swap_blk(gats[blocks + m], m) for m in range(1, blocks)]
            sum1 = Halving(places, g1, [img2])
            sum2 = Halving(places, g2.reshape((4,) + g2.shape[2:]), [x_dim, img2])
            sum1.swap(to1, img0)
            sum2.swap(to2, img1)
            before, kept, passed = (), [], []
            for i in (1, 2):
                if i == 2:
                    near = swap_blk(passed[0], 1)
                    others = after(others, *before)
                    sum1.hold(before)
                    sum2.hold(before)
                    send2 = sum2.send(x_dim)
                    before, send2 = lax.optimization_barrier((before, send2))
                    sum2.swap(send2, x_dim)
                *before, kept_i, passed_i = backward_image(
                    counts, i, firsts if i == 1 else others, 0, *saved[i], w, before, wide, nh
                )
                kept.append(kept_i)
                passed.append(passed_i)
            dw, sums1 = before
            (g1y, _), (g2z, _), (g2x, _) = sum1.terms[1], sum2.terms[1], sum2.terms[2]
            pieces = (*others, *saved[0], w, dw, sums1, kept[0], near, kept[1], passed[1])
            pieces += (g1, g1y, g2, g2z, g2x, so, sums, vec, gb1, gmid, *mine)
            tok, e, o1, o2 = last_image(
                share, tokens.shape, wide, g1.shape[-1], 2 * (ff // n), half, nh, images - 2, *pieces
            )
            grad_tokens, output, grad_qkv, grad_out, grad_fc1, grad_fc2, g_b1, *v = layout(
                counts, tok, out, e, o1, o2, nh, ff
            )
            g_b1 = g_b1.reshape(-1)
            v = [item.reshape(-1) for item in v]
        else:
            chips = [dim for dim in places.dims if dim != ("blk", 0)]
            g1 = jnp.concatenate([g1, so], axis=1)
            g1 = scatter_sum(places, g1.reshape(2 ** len(chips), 2 * share, -1), chips, chips[::-1])
            g2 = scatter_sum(places, g2.reshape(2 ** len(chips), 2 * (ff // n), half), chips, chips[::-1])

            def both_cores(value):
                value = value.reshape((2, -1) + value.shape[1:])
                core = places.bit(("blk", 0))
                own = lax.dynamic_index_in_dim(value, core, 0, keepdims=False)
                far = swap_blk(lax.dynamic_index_in_dim(value, 1 - core, 0, keepdims=False).astype(bf16), 1).astype(f32)
                return jnp.where(core == 0, own, far), jnp.where(core == 0, far, own)

            low, high = both_cores(g1)
            merged = jnp.concatenate([low.reshape(share, -1, half), high.reshape(share, -1, half)], axis=2)
            grad_fc1 = merged[:, : ff // d].reshape(share, ff)
            grad_out = merged[:, ff // d]
            grad_fc2 = jnp.concatenate(both_cores(g2), axis=1)

            before, terms = (), [None] * (3 * images)
            others = [gats[blocks]] + [swap_blk(gats[blocks + m], m) for m in range(1, blocks)]
            for k in range(images):
                i = (k + 1) % images
                pieces = others if k else gats[:blocks]
                *before, kept, passed = backward_image(
                    counts, i, pieces, max(k - 1, 0), *saved[i], w, before, 3 * hw, nh
                )
                near = swap_blk(passed, 1)
                step = (kept[1].astype(f32) + near[1].astype(f32)).astype(bf16)[None]
                terms[3 * i : 3 * i + 3] = [kept, near, swap_blk(step, 2)]
            dw, sums1 = before

            def returned(value):
                value = value.reshape(tokens.shape)
                at = [lax.rem(i - lead + images, images) for i in range(images)]
                return jnp.stack([lax.dynamic_index_in_dim(value, k, 0, keepdims=False) for k in at])

            output = returned(out)
            grad_tokens = returned(finish(jnp.stack(mine), gmid, vec[0:1, :], terms))

            img_dims = [("img", k) for k in reversed(range(places.img_bits))]
            part = scatter_sum(places, dw.reshape(places.n_img, blocks * share, 3 * hw), img_dims, img_dims[::-1])
            part = part.reshape(blocks, share, 3 * hw)
            pieces = [
                lax.dynamic_slice(part, (me ^ m, 0, 0), (1, share, 3 * hw))[0].astype(bf16) for m in range(blocks)
            ]
            pieces = jnp.stack([pieces[0]] + [swap_blk(pieces[m], m) for m in range(1, blocks)])
            by_source = jnp.stack([lax.dynamic_index_in_dim(pieces, me ^ b, 0, keepdims=False) for b in range(blocks)])
            by_source = by_source.reshape(blocks, share, nh, 3, WIDTH).transpose(1, 3, 0, 2, 4)
            grad_qkv = by_source.reshape(share, 3 * d).astype(f32)

            row = sums1[1, : 3 * hw].reshape(nh, 3, WIDTH)
            placed = lambda v: lax.dynamic_update_slice(jnp.zeros((d,), f32), v.reshape(hw), (me * hw,))
            g_n1b = sums1[0]
            g_n1g = (jnp.sum(dw * w.astype(f32), axis=1) - vec[1] * sums1[0]) / vec[0]
            g_s2, g_b2, g_n2g, g_n2b, g_s1, g_bo = [sums[k] for k in range(6)]
            small = [placed(row[:, 0]), placed(row[:, 2]), g_bo, g_n1g, g_n1b, g_n2g, g_n2b, g_b2, g_s1, g_s2]
            small = jnp.stack(small).reshape(10, n, share).transpose(1, 0, 2).reshape(n, 1, 10 * share)
            small = jnp.concatenate([small, gb1[:, 0].reshape(n, 1, ff // n)], axis=2)
            small = scatter_sum(places, small, places.dims, places.dims[::-1], link=f32)[0]
            v = [small[k * share : (k + 1) * share] for k in range(10)]
            g_b1 = small[10 * share :]
        return (
            output,
            grad_tokens,
            grad_qkv,
            v[0],
            v[1],
            grad_out,
            v[2],
            v[3],
            v[4],
            v[5],
            v[6],
            grad_fc1,
            g_b1,
            grad_fc2,
            v[7],
            v[8],
            v[9],
        )

    both = P(("img", "blk"))
    both2 = P(("img", "blk"), None)
    rows_spec = P("img", "blk", None)
    in_specs = (rows_spec, P("img")) + (P(),) * 15 + (rows_spec,)
    out_specs = (
        rows_spec,
        rows_spec,
        both2,
        both,
        both,
        both2,
        both,
        both,
        both,
        both,
        both,
        both2,
        both,
        both2,
        both,
        both,
        both,
    )
    return jax.shard_map(per_device, mesh=mesh, in_specs=in_specs, out_specs=out_specs, check_vma=False)
```

profile of v0, /device:TPU:0, one launch (start us, length us, event | category | flops | bytes accessed | tf_op | source)
XLA Modules:
  0.0 217.5 jit_solution(17455981311660671395)
XLA Ops:
  0.8 1.4 iota_reduce_fusion
  4.1 1.3 dynamic-slice_bitcast_fusion.3
  5.5 3.0 %collective-permute-start = (bf16[256,768]{1,0:T(8,128)(2,1)S(1)}, bf16[256,768]{1,0:T(8,128)(2,1)S(1)}, u32[]{:S(2)}, u32[]{:S(2)}) collective-permute-start(bf16[256,768]{1,0:T(8,128)(2,1)S(1)} %get-tuple-element.104.refs_0_.refs_12_.refs_25_), channel_id=1, source_target_pairs={{0,2},{1,3},{2,0},{3,1},{4,6},{5,7},{6,4},{7,5},{8,10},{9,11},{10,... | collective-permute-start | bytes 1179656 | tf_op jit(solution)/shard_map/ppermute | solution.py:1239
  9.0 0.7 reshape.125.refs_6_
  9.7 0.6 convert_element_type.33.refs_4_.refs_16_.refs_22_
  10.4 2.0 constant_dynamic-slice_fusion.2
  13.0 4.6 %collective-permute-done.refs_2_ = bf16[256,768]{1,0:T(8,128)(2,1)S(1)} collective-permute-done((bf16[256,768]{1,0:T(8,128)(2,1)S(1)}, bf16[256,768]{1,0:T(8,128)(2,1)S(1)}, u32[]{:S(2)}, u32[]{:S(2)}) %collective-permute-start) | collective-permute-done | bytes 393248 | tf_op jit(solution)/shard_map/ppermute | solution.py:1239
  18.1 1.7 collective-permute-start.6
  19.8 1.3 copy.40.refs_5_.refs_8_
  21.2 0.7 copy-done.24
  21.9 12.1 %attend_forward.3 = (bf16[4,256,768]{2,1,0:T(8,128)(2,1)}, bf16[4,256,576]{2,1,0:T(8,128)(2,1)}, f32[192,1024]{1,0:T(8,128)}, f32[8,1024]{1,0:T(8,128)}, bf16[19...) custom-call(s32[3]{0:T(128)} %counts.11, ...), custom_call_target="tpu_custom_call" | custom-call | flops 2516582400 | bytes 8000000 | tf_op jit(solution)/shard_map/attend_forward/pallas_call | solution.py:114
  34.9 0.9 collective-permute-done.7.refs_1_
  36.5 0.8 copy-done.26
  37.3 20.4 %attend_forward.4 = (bf16[4,256,768]{2,1,0:T(8,128)(2,1)}, bf16[4,256,576]{2,1,0:T(8,128)(2,1)}, f32[192,1024]{1,0:T(8,128)}, f32[8,1024]{1,0:T(8,128)}, bf16[19...) custom-call(s32[3]{0:T(128)} %counts.11, ...), custom_call_target="tpu_custom_call" | custom-call | flops 2516582400 | bytes 8000000 | tf_op jit(solution)/shard_map/attend_forward/pallas_call | solution.py:114
  59.2 1.1 pad_maximum_fusion.refs_15_
  60.3 0.8 collective-permute-start.4
  61.1 1.0 collective-permute-start.5
  62.6 0.8 collective-permute-start.10
  63.4 0.8 collective-permute-start.11
  64.1 10.6 %attend_forward.5 = (bf16[4,256,768]{2,1,0:T(8,128)(2,1)}, bf16[4,256,576]{2,1,0:T(8,128)(2,1)}, f32[192,1024]{1,0:T(8,128)}, f32[8,1024]{1,0:T(8,128)}, bf16[19...) custom-call(s32[3]{0:T(128)} %counts.11, ...), custom_call_target="tpu_custom_call" | custom-call | flops 2516582400 | bytes 8000000 | tf_op jit(solution)/shard_map/attend_forward/pallas_call | solution.py:114
  75.5 58.5 %middle_layers.1 = (bf16[768,768]{1,0:T(8,128)(2,1)}, f32[768,768]{1,0:T(8,128)}, f32[3072,128]{1,0:T(8,128)}, f32[8,768]{1,0:T(8,128)}, bf16[768,384]{1,0:T(8,1...) custom-call(bf16[192,256]{1,0:T(8,128)(2,1)} %get-tuple-element.106., ...), custom_call_target="tpu_custom_call" | custom-call | flops 24461180928 | bytes 30000000 | tf_op jit(solution)/shard_map/middle_layers/pallas_call | solution.py:612
  134.2 0.9 collective-permute-start.16
  135.1 0.9 collective-permute-start.17
  136.0 1.1 collective-permute-start.18
  137.1 0.9 collective-permute-start.20
  138.0 10.0 %attend_backward.2 = (f32[768,640]{1,0:T(8,128)}, f32[8,768]{1,0:T(8,128)}, bf16[2,256,768]{2,1,0:T(8,128)(2,1)}, bf16[2,256,768]{2,1,0:T(8,128)(2,1)}) custom-call(s32[3]{0:T(128)} %counts.11, bf16[1,192,256]{2,1,0:T(8,128)(2,1)} %get-tuple-element.128.refs_0_, bf16[1,192,256]{2,1,0:T(8,128)(2,1)} %get-tuple-element.129.refs_1_, ...), custom_call_target="tpu_custom_call" | custom-call | flops 5838471168 | bytes 12000000 | tf_op jit(solution)/shard_map/attend_backward/pallas_call | solution.py:251
  148.1 3.7 %collective-permute-done.18.refs_18_ = bf16[2,2,192,384]{3,2,1,0:T(8,128)(2,1)S(1)} collective-permute-done((bf16[2,2,192,384]{3,2,1,0:T(8,128)(2,1)}, bf16[2,2,192,384]{3,2,1,0:T(8,128)(2,1)S(1)}, u32[]{:S(2)}, u32[]{:S(2)}) %collective-permute-start.18) | collective-permute-done | bytes 589856 | tf_op jit(solution)/shard_map/ppermute | solution.py:1152
  151.9 0.9 collective-permute-start.21
  152.8 14.0 %attend_backward.3 = (f32[768,640]{1,0:T(8,128)}, f32[8,768]{1,0:T(8,128)}, bf16[2,256,768]{2,1,0:T(8,128)(2,1)}, bf16[2,256,768]{2,1,0:T(8,128)(2,1)}) custom-call(s32[3]{0:T(128)} %counts.11, bf16[2,192,256]{2,1,0:T(8,128)(2,1)} %get-tuple-element.137.refs_0_, bf16[2,192,256]{2,1,0:T(8,128)(2,1)} %copy-done.28, bf16[2,192,256]{2,1,0:T(8,128)(2,1)} %copy-done.29, ...), custom_call_target="tpu_custom_call" | custom-call | flops 5838471168 | bytes 12000000 | tf_op jit(solution)/shard_map/attend_backward/pallas_call | solution.py:251
  166.9 0.9 copy-done.17
  167.9 45.5 %last.1 = (bf16[3,256,768]{2,1,0:T(8,128)(2,1)}, f32[4,24,1024]{2,1,0:T(8,128)}, f32[2,24,1536]{2,1,0:T(8,128)}, f32[2,96,384]{2,1,0:T(8,128)}) custom-call(bf16[2,192,256]{2,1,0:T(8,128)(2,1)} %get-tuple-element.137.refs_0_, bf16[2,192,256]{2,1,0:T(8,128)(2,1)} %copy-done.28, bf16[2,192,256]{2,1,0:T(8,128)(2,1)} %copy-done.29, ...), custom_call_target="tpu_custom_call" | custom-call | flops 30000001024 | bytes 20000000 | tf_op jit(solution)/shard_map/last/pallas_call | solution.py:1002
  213.4 3.8 %layout.1 = (bf16[3,256,768]{2,1,0:T(8,128)(2,1)}, bf16[3,256,768]{2,1,0:T(8,128)(2,1)}, f32[24,2304]{1,0:T(8,128)}, f32[24,768]{1,0:T(8,128)}, f32[24,3072]{1,0...) custom-call(s32[3]{0:T(128)} %counts.11, ...), custom_call_target="tpu_custom_call" | custom-call | tf_op jit(solution)/shard_map/layout/pallas_call | solution.py:1096
  (138 shorter events, 6.3 us)
Async XLA Ops:
  0.7 8.0 %copy-start.14 = (bf16[768]{0:T(1024)(128)(2,1)S(1)}, bf16[768]{0:T(1024)(128)(2,1)}, u32[]{:S(2)}) copy-start(bf16[768]{0:T(1024)(128)(2,1)} %param.34) | copy-start | bytes 4612
  5.4 12.2 %copy-start.2 = (bf16[256,768]{1,0:T(8,128)(2,1)}, bf16[256,768]{1,0:T(8,128)(2,1)S(1)}, u32[]{:S(2)}) copy-start(bf16[256,768]{1,0:T(8,128)(2,1)S(1)} %get-tuple-element.104.refs_0_.refs_12_.refs_25_) | copy-start | bytes 1179652
  5.4 28.6 %copy-start.3 = (bf16[256,768]{1,0:T(8,128)(2,1)}, bf16[256,768]{1,0:T(8,128)(2,1)S(1)}, u32[]{:S(2)}) copy-start(bf16[256,768]{1,0:T(8,128)(2,1)S(1)} %get-tuple-element.111.refs_0_.refs_13_.refs_26_) | copy-start | bytes 1179652
  5.4 52.3 %copy-start.1 = (bf16[256,768]{1,0:T(8,128)(2,1)}, bf16[256,768]{1,0:T(8,128)(2,1)S(1)}, u32[]{:S(2)}) copy-start(bf16[256,768]{1,0:T(8,128)(2,1)S(1)} %get-tuple-element.118.refs_0_.refs_14_.refs_27_) | copy-start | bytes 1179652
  5.5 12.1 %collective-permute-start = (bf16[256,768]{1,0:T(8,128)(2,1)S(1)}, bf16[256,768]{1,0:T(8,128)(2,1)S(1)}, u32[]{:S(2)}, u32[]{:S(2)}) collective-permute-start(bf16[256,768]{1,0:T(8,128)(2,1)S(1)} %get-tuple-element.104.refs_0_.refs_12_.refs_25_), channel_id=1, source_target_pairs={{0,2},{1,3},{2,0},{3,1},{4,6},{5,7},{6,4},{7,5},{8,10},{9,11},{10,... | collective-permute-start | bytes 1179656 | tf_op jit(solution)/shard_map/ppermute | solution.py:1239
  17.6 3.6 %collective-permute-start.1 = (bf16[256,768]{1,0:T(8,128)(2,1)S(1)}, bf16[256,768]{1,0:T(8,128)(2,1)S(1)}, u32[]{:S(2)}, u32[]{:S(2)}) collective-permute-start(bf16[256,768]{1,0:T(8,128)(2,1)S(1)} %get-tuple-element.104.refs_0_.refs_12_.refs_25_), channel_id=1, source_target_pairs={{0,1},{1,0},{2,3},{3,2},{4,5},{5,4},{6,7},{7,6},{8,9},{9,8},{10,11... | collective-permute-start | bytes 1179656 | tf_op jit(solution)/shard_map/ppermute | solution.py:1239
  17.6 3.6 %collective-permute-start.2 = (bf16[256,768]{1,0:T(8,128)(2,1)S(1)}, bf16[256,768]{1,0:T(8,128)(2,1)}, u32[]{:S(2)}, u32[]{:S(2)}) collective-permute-start(bf16[256,768]{1,0:T(8,128)(2,1)S(1)} %collective-permute-done.refs_2_), channel_id=1, source_target_pairs={{0,1},{1,0},{2,3},{3,2},{4,5},{5,4},{6,7},{7,6},{8,9},{9,8},{10,11... | collective-permute-start | bytes 1179656 | tf_op jit(solution)/shard_map/ppermute | solution.py:1239
  18.1 15.9 %collective-permute-start.6 = (bf16[256,768]{1,0:T(8,128)(2,1)S(1)}, bf16[256,768]{1,0:T(8,128)(2,1)S(1)}, u32[]{:S(2)}, u32[]{:S(2)}) collective-permute-start(bf16[256,768]{1,0:T(8,128)(2,1)S(1)} %get-tuple-element.111.refs_0_.refs_13_.refs_26_), channel_id=1, source_target_pairs={{0,2},{1,3},{2,0},{3,1},{4,6},{5,7},{6,4},{7,5},{8,10},{9,11},{10,... | collective-permute-start | bytes 1179656 | tf_op jit(solution)/shard_map/ppermute | solution.py:1239
  34.0 1.8 collective-permute-start.7
  34.1 2.3 %collective-permute-start.8 = (bf16[256,768]{1,0:T(8,128)(2,1)S(1)}, bf16[256,768]{1,0:T(8,128)(2,1)S(1)}, u32[]{:S(2)}, u32[]{:S(2)}) collective-permute-start(bf16[256,768]{1,0:T(8,128)(2,1)S(1)} %collective-permute-done.6.refs_2_), channel_id=1, source_target_pairs={{0,1},{1,0},{2,3},{3,2},{4,5},{5,4},{6,7},{7,6},{8,9},{9,8},{10,11... | collective-permute-start | bytes 1179656 | tf_op jit(solution)/shard_map/ppermute | solution.py:1239
  34.6 23.7 %copy-start.6 = (bf16[3072]{0:T(1024)(128)(2,1)S(1)}, bf16[3072]{0:T(1024)(128)(2,1)}, u32[]{:S(2)}) copy-start(bf16[3072]{0:T(1024)(128)(2,1)} %param.30) | copy-start | bytes 18436
  34.6 24.3 %copy-start = (bf16[3,256,768]{2,1,0:T(8,128)(2,1)S(1)}, bf16[3,256,768]{2,1,0:T(8,128)(2,1)}, u32[]{:S(2)}) copy-start(bf16[3,256,768]{2,1,0:T(8,128)(2,1)} %param.35) | copy-start | bytes 3538948
  34.6 23.1 %collective-permute-start.12 = (bf16[256,768]{1,0:T(8,128)(2,1)S(1)}, bf16[256,768]{1,0:T(8,128)(2,1)S(1)}, u32[]{:S(2)}, u32[]{:S(2)}) collective-permute-start(bf16[256,768]{1,0:T(8,128)(2,1)S(1)} %get-tuple-element.118.refs_0_.refs_14_.refs_27_), channel_id=1, source_target_pairs={{0,2},{1,3},{2,0},{3,1},{4,6},{5,7},{6,4},{7,5},{8,10},{9,11},{10,... | collective-permute-start | bytes 1179656 | tf_op jit(solution)/shard_map/ppermute | solution.py:1239
  57.7 4.8 %collective-permute-start.13 = (bf16[256,768]{1,0:T(8,128)(2,1)S(1)}, bf16[256,768]{1,0:T(8,128)(2,1)S(1)}, u32[]{:S(2)}, u32[]{:S(2)}) collective-permute-start(bf16[256,768]{1,0:T(8,128)(2,1)S(1)} %get-tuple-element.118.refs_0_.refs_14_.refs_27_), channel_id=1, source_target_pairs={{0,1},{1,0},{2,3},{3,2},{4,5},{5,4},{6,7},{7,6},{8,9},{9,8},{10,11... | collective-permute-start | bytes 1179656 | tf_op jit(solution)/shard_map/ppermute | solution.py:1239
  57.9 5.5 %collective-permute-start.14 = (bf16[256,768]{1,0:T(8,128)(2,1)S(1)}, bf16[256,768]{1,0:T(8,128)(2,1)S(1)}, u32[]{:S(2)}, u32[]{:S(2)}) collective-permute-start(bf16[256,768]{1,0:T(8,128)(2,1)S(1)} %collective-permute-done.12.refs_2_), channel_id=1, source_target_pairs={{0,1},{1,0},{2,3},{3,2},{4,5},{5,4},{6,7},{7,6},{8,9},{9,8},{10,11... | collective-permute-start | bytes 1179656 | tf_op jit(solution)/shard_map/ppermute | solution.py:1239
  59.0 3.0 %collective-permute-start.3 = (bf16[192,256]{1,0:T(8,128)(2,1)S(1)}, bf16[192,256]{1,0:T(8,128)(2,1)S(1)}, u32[]{:S(2)}, u32[]{:S(2)}) collective-permute-start(bf16[192,256]{1,0:T(8,128)(2,1)S(1)} %copy-done.38), channel_id=1, source_target_pairs={{0,1},{1,0},{2,3},{3,2},{4,5},{5,4},{6,7},{7,6},{8,9},{9,8},{10,11... | collective-permute-start | bytes 294920 | tf_op jit(solution)/shard_map/ppermute | solution.py:1239
  60.3 14.4 %collective-permute-start.4 = (bf16[192,256]{1,0:T(8,128)(2,1)S(1)}, bf16[192,256]{1,0:T(8,128)(2,1)S(1)}, u32[]{:S(2)}, u32[]{:S(2)}) collective-permute-start(bf16[192,256]{1,0:T(8,128)(2,1)S(1)} %copy-done.32), channel_id=1, source_target_pairs={{0,2},{1,3},{2,0},{3,1},{4,6},{5,7},{6,4},{7,5},{8,10},{9,11},{10,... | collective-permute-start | bytes 294920 | tf_op jit(solution)/shard_map/ppermute | solution.py:1239
  61.1 13.7 %collective-permute-start.5 = (bf16[192,256]{1,0:T(8,128)(2,1)S(1)}, bf16[192,256]{1,0:T(8,128)(2,1)S(1)}, u32[]{:S(2)}, u32[]{:S(2)}) collective-permute-start(bf16[192,256]{1,0:T(8,128)(2,1)S(1)} %copy-done.31), channel_id=1, source_target_pairs={{0,3},{1,2},{2,1},{3,0},{4,7},{5,6},{6,5},{7,4},{8,11},{9,10},{10,... | collective-permute-start | bytes 294920 | tf_op jit(solution)/shard_map/ppermute | solution.py:1239
  62.1 12.7 %copy-start.36 = (bf16[192,256]{1,0:T(8,128)(2,1)}, bf16[192,256]{1,0:T(8,128)(2,1)S(1)}, u32[]{:S(2)}) copy-start(bf16[192,256]{1,0:T(8,128)(2,1)S(1)} %collective-permute-done.3.refs_1_) | copy-start | bytes 294916
  62.1 12.7 %collective-permute-start.9 = (bf16[192,256]{1,0:T(8,128)(2,1)S(1)}, bf16[192,256]{1,0:T(8,128)(2,1)S(1)}, u32[]{:S(2)}, u32[]{:S(2)}) collective-permute-start(bf16[192,256]{1,0:T(8,128)(2,1)S(1)} %copy-done.35), channel_id=1, source_target_pairs={{0,1},{1,0},{2,3},{3,2},{4,5},{5,4},{6,7},{7,6},{8,9},{9,8},{10,11... | collective-permute-start | bytes 294920 | tf_op jit(solution)/shard_map/ppermute | solution.py:1239
  62.6 12.2 %collective-permute-start.10 = (bf16[192,256]{1,0:T(8,128)(2,1)S(1)}, bf16[192,256]{1,0:T(8,128)(2,1)S(1)}, u32[]{:S(2)}, u32[]{:S(2)}) collective-permute-start(bf16[192,256]{1,0:T(8,128)(2,1)S(1)} %copy-done.34), channel_id=1, source_target_pairs={{0,2},{1,3},{2,0},{3,1},{4,6},{5,7},{6,4},{7,5},{8,10},{9,11},{10,... | collective-permute-start | bytes 294920 | tf_op jit(solution)/shard_map/ppermute | solution.py:1239
  63.4 11.4 %collective-permute-start.11 = (bf16[192,256]{1,0:T(8,128)(2,1)S(1)}, bf16[192,256]{1,0:T(8,128)(2,1)S(1)}, u32[]{:S(2)}, u32[]{:S(2)}) collective-permute-start(bf16[192,256]{1,0:T(8,128)(2,1)S(1)} %copy-done.33), channel_id=1, source_target_pairs={{0,3},{1,2},{2,1},{3,0},{4,7},{5,6},{6,5},{7,4},{8,11},{9,10},{10,... | collective-permute-start | bytes 294920 | tf_op jit(solution)/shard_map/ppermute | solution.py:1239
  134.1 13.9 %collective-permute-start.15 = (bf16[2,192,256]{2,1,0:T(8,128)(2,1)}, bf16[2,192,256]{2,1,0:T(8,128)(2,1)S(1)}, u32[]{:S(2)}, u32[]{:S(2)}) collective-permute-start(bf16[2,192,256]{2,1,0:T(8,128)(2,1)} %get-tuple-element.125), channel_id=1, source_target_pairs={{0,1},{1,0},{2,3},{3,2},{4,5},{5,4},{6,7},{7,6},{8,9},{9,8},{10,11... | collective-permute-start | bytes 589832 | tf_op jit(solution)/shard_map/ppermute | solution.py:1239
  134.2 13.9 %collective-permute-start.16 = (bf16[2,192,256]{2,1,0:T(8,128)(2,1)}, bf16[2,192,256]{2,1,0:T(8,128)(2,1)S(1)}, u32[]{:S(2)}, u32[]{:S(2)}) collective-permute-start(bf16[2,192,256]{2,1,0:T(8,128)(2,1)} %get-tuple-element.126), channel_id=1, source_target_pairs={{0,2},{1,3},{2,0},{3,1},{4,6},{5,7},{6,4},{7,5},{8,10},{9,11},{10,... | collective-permute-start | bytes 589832 | tf_op jit(solution)/shard_map/ppermute | solution.py:1239
  135.1 13.0 %collective-permute-start.17 = (bf16[2,192,256]{2,1,0:T(8,128)(2,1)}, bf16[2,192,256]{2,1,0:T(8,128)(2,1)S(1)}, u32[]{:S(2)}, u32[]{:S(2)}) collective-permute-start(bf16[2,192,256]{2,1,0:T(8,128)(2,1)} %get-tuple-element.127), channel_id=1, source_target_pairs={{0,3},{1,2},{2,1},{3,0},{4,7},{5,6},{6,5},{7,4},{8,11},{9,10},{10,... | collective-permute-start | bytes 589832 | tf_op jit(solution)/shard_map/ppermute | solution.py:1239
  136.0 15.8 %collective-permute-start.18 = (bf16[2,2,192,384]{3,2,1,0:T(8,128)(2,1)}, bf16[2,2,192,384]{3,2,1,0:T(8,128)(2,1)S(1)}, u32[]{:S(2)}, u32[]{:S(2)}) collective-permute-start(bf16[2,2,192,384]{3,2,1,0:T(8,128)(2,1)} %get-tuple-element.149), channel_id=1, source_target_pairs={{0,8},{4,12},{8,0},{12,4},{16,24},{20,28},{24,16},{28,20},{1,9},{5... | collective-permute-start | bytes 1769480 | tf_op jit(solution)/shard_map/ppermute | solution.py:1152
  137.1 15.7 %collective-permute-start.20 = (bf16[2,96,1536]{2,1,0:T(8,128)(2,1)}, bf16[2,96,1536]{2,1,0:T(8,128)(2,1)S(1)}, u32[]{:S(2)}, u32[]{:S(2)}) collective-permute-start(bf16[2,96,1536]{2,1,0:T(8,128)(2,1)} %get-tuple-element.160), channel_id=1, source_target_pairs={{0,4},{4,0},{8,12},{12,8},{16,20},{20,16},{24,28},{28,24},{1,5},{5... | collective-permute-start | bytes 1769480 | tf_op jit(solution)/shard_map/ppermute | solution.py:1152
  138.0 13.8 %copy-start.4 = (bf16[2,2,192,384]{3,2,1,0:T(8,128)(2,1)S(1)}, bf16[2,2,192,384]{3,2,1,0:T(8,128)(2,1)}, u32[]{:S(2)}) copy-start(bf16[2,2,192,384]{3,2,1,0:T(8,128)(2,1)} %get-tuple-element.148.refs_17_) | copy-start | bytes 1769476
  148.0 18.9 %collective-permute-start.19 = (bf16[2,256,768]{2,1,0:T(8,128)(2,1)}, bf16[2,256,768]{2,1,0:T(8,128)(2,1)S(1)}, u32[]{:S(2)}, u32[]{:S(2)}) collective-permute-start(bf16[2,256,768]{2,1,0:T(8,128)(2,1)} %get-tuple-element.156), channel_id=1, source_target_pairs={{0,1},{1,0},{2,3},{3,2},{4,5},{5,4},{6,7},{7,6},{8,9},{9,8},{10,11... | collective-permute-start | bytes 2359304 | tf_op jit(solution)/shard_map/ppermute | solution.py:1239
  151.8 15.1 %copy-start.5 = (bf16[2,2,192,384]{3,2,1,0:T(8,128)(2,1)}, bf16[2,2,192,384]{3,2,1,0:T(8,128)(2,1)S(1)}, u32[]{:S(2)}) copy-start(bf16[2,2,192,384]{3,2,1,0:T(8,128)(2,1)S(1)} %collective-permute-done.18.refs_18_) | copy-start | bytes 1769476
  151.9 15.0 %collective-permute-start.21 = (bf16[2,192,384]{2,1,0:T(8,128)(2,1)S(1)}, bf16[2,192,384]{2,1,0:T(8,128)(2,1)S(1)}, u32[]{:S(2)}, u32[]{:S(2)}) collective-permute-start(bf16[2,192,384]{2,1,0:T(8,128)(2,1)S(1)} %fusion), channel_id=1, source_target_pairs={{0,2},{1,3},{2,0},{3,1},{4,6},{5,7},{6,4},{7,5},{8,10},{9,11},{10,... | collective-permute-start | bytes 884744 | tf_op jit(solution)/shard_map/ppermute | solution.py:1152
  152.8 14.1 %copy-start.18 = (bf16[2,96,1536]{2,1,0:T(8,128)(2,1)}, bf16[2,96,1536]{2,1,0:T(8,128)(2,1)S(1)}, u32[]{:S(2)}) copy-start(bf16[2,96,1536]{2,1,0:T(8,128)(2,1)S(1)} %collective-permute-done.20.refs_16_) | copy-start | bytes 1769476
  (33 other events, 119.7 us)
where the time goes:
time: 221 us; the launch traced here: 217 us
  Pallas kernels  175 us (79%)
  starting transfers between devices  15.6 us (7%)
  waiting for transfers between devices  9.79 us (4%)
  local copies, waits for them, and re-layouts  9.78 us (4%)
  other arithmetic  3.85 us (2%)
  between operations  3.53 us (2%)
    pallas_call x1, Pallas kernels, middle_layers(): pl.pallas_call(partial(middle_kernel, blocks, images, steps, bits), name=...  58.5 us
    pallas_call x1, Pallas kernels, last_image(): pl.pallas_call(partial(last_kernel, blocks, nh, rows, share, at_piece), n...  45.5 us
    pallas_call x3, Pallas kernels, forward_image(): pl.pallas_call(partial(forward_kernel, blocks, nh, rows, image), name='at...  43.1 us
    pallas_call x2, Pallas kernels, backward_image(): pl.pallas_call(partial(backward_kernel, blocks, nh, rows, image, at, not...  24 us
    ppermute x19, starting transfers between devices, swap_blk(): return lax.ppermute(value, 'blk', [(b, b ^ m) for b in range(blocks)])  12.7 us
    ppermute x19, waiting for transfers between devices, swap_blk(): return lax.ppermute(value, 'blk', [(b, b ^ m) for b in range(blocks)])  6.08 us
  transfers between devices with their start and end apart: 22, of which 4 were waited for; matrix products, arithmetic and copies ran while one was open for 3% of the time, Pallas kernels for 31%

commit v1 on v0

--- a/solution.py
+++ b/solution.py
@@ -694,24 +694,25 @@
     tok, e_out, o1, o2 = refs[:4]
     here, refs = refs[4 : 4 + LAST_IN], refs[4 + LAST_IN :]
     (qt, qs, ks, vs, gs, kt, gt, delta, dqt, gall, n1t, low) = refs[:12]
-    (small, ext, fin, rxf, sa1, ra1, sb1, rb1, sc1, rc1, sa2, ra2, sb2, rb2, sc2, rc2) = refs[12:28]
-    (sa3, ra3, sb3, rb3, sc3, rc3, sx, rx, sc, rc) = refs[28:38]
-    (near_b, near_c, step, got, sz1, rz1, sg1, rg1, cg1, dg1, sg2, rg2, cg2, dg2, send_sem, recv_sem, load_sem) = refs[38:]
-    gats, (n1, qkv, full, lse, w, dw, sums1, kept_a, near_a, kept_b, passed_b) = here[:4], here[4:15]
-    (g1, g1y, g2, g2z, g2x, so, sums, vec, gb, gmid, *x) = here[15:]
+    (small, ext, fin, qa, ra, qb, rb, qc, rc, ua, va, ub, vb, uc, vc, give, take) = refs[12:29]
+    (near_b, near_c, step, got, sg1, rg1, cg1, dg1, sg2, rg2, cg2, dg2, send_sem, recv_sem, load_sem) = refs[29:]
+    (passed_b, kept_a, near_a), gats, (qkv, full, lse) = here[:3], here[3:7], here[7:10]
+    (so, g1, g1y, g1z, kept_b, n1, dw, w, sums, sums1, vec, gb, g2, g2z, g2x, gmid, *x) = here[10:]
     me, im = lax.axis_index("blk"), lax.axis_index("img")
     core, xx = lax.rem(me, 2), lax.div(me, 2)
     y, z0, z1 = lax.rem(im, 2), lax.rem(lax.div(im, 2), 2), lax.div(im, 4)
-    to_core, to_x = {"blk": flip(me, 0)}, {"blk": flip(me, 1)}
-    to_y, to_z0, to_z1 = {"img": flip(im, 0)}, {"img": flip(im, 1)}, {"img": flip(im, 2)}
+    to_core, to_x, to_z1 = {"blk": flip(me, 0)}, {"blk": flip(me, 1)}, {"img": flip(im, 2)}
+    to_kin = [{"blk": flip_all(me, m)} for m in range(1, blocks)]
+    to_quad = [{"img": flip_all(im, k)} for k in range(1, 4)]
     d = n1.shape[2]
     hw, chip, four = nh * WIDTH, 2 * share, 4 * share
     wide = dw.shape[1]
-    cut = sa1.shape[2]
+    cut = qa.shape[-1]
     used = w.shape[1]
     slots = iter(range(send_sem.shape[0]))
     loads = [
-        pltpu.make_async_copy(far.at[at_piece] if k < 4 else far, here[k], load_sem.at[k]) for k, far in enumerate(far_refs)
+        pltpu.make_async_copy(far.at[at_piece] if 3 <= k < 7 else far, here[k], load_sem.at[k])
+        for k, far in enumerate(far_refs)
     ]
     for load in loads:
         load.start()
@@ -735,10 +736,33 @@
     def at(block, size):
         return pl.ds(pl.multiple_of(block * size, size), size)
 
-    def rows_of(i, j, k):
-        return at((2 * i + j) * 2 + k, four)
-
-    meet([to_core, to_x, to_y, to_z0, to_z1])
+    def rows_of(i, k):
+        return at((2 * i + flip_all(z0, k >> 1)) * 2 + flip_all(y, k & 1), four)
+
+    def quad(value, send, recv):
+        for k in (3, 1, 2):
+            for i in range(2):
+                send[k - 1, i] = value(rows_of(i, k)).astype(bf16)
+        copies = [copy(send.at[k - 1], recv.at[k - 1], to_quad[k - 1]) for k in range(1, 4)]
+        for k in (2, 0, 1):
+            copies[k].start()
+        return copies
+
+    def quad_sum(value, recv, i):
+        total = value(rows_of(i, 0)).astype(f32)
+        for k in range(3):
+            total = total + recv[k, i].astype(f32)
+        return total
+
+    def onward(value, copies, recv, send, last):
+        for item in copies:
+            item.wait()
+        send[...] = quad_sum(value, recv, 1 - z1).astype(bf16)
+        item = copy(send, last, to_z1)
+        item.start()
+        return item
+
+    meet(to_kin + to_quad + [to_z1])
     need(passed_b)
     pass_b = copy(passed_b, near_b, to_core)
     pass_b.start()
@@ -746,20 +770,6 @@
     step[0] = (kept_a[1].astype(f32) + near_a[1].astype(f32)).astype(bf16)
     step_a = copy(step.at[0], got.at[0], to_x)
     step_a.start()
-    need(so)
-    for i in range(2):
-        for j in range(2):
-            sc1[i, j] = so[rows_of(i, j, 1 - y), :]
-    c1 = copy(sc1, rc1, to_y)
-    c1.start()
-
-    def sum_1(block):
-        return g1[block].astype(f32) + g1y[block].astype(f32)
-
-    need(g1, g1y)
-    sz1[...] = sum_1(1 - z1).astype(bf16)
-    g1_z = copy(sz1, rz1, to_z1)
-    g1_z.start()
 
     need(qkv, full, lse, *gats)
     dqt[...] = jnp.zeros_like(dqt)
@@ -784,6 +794,30 @@
         sl = slice(h * WIDTH, (h + 1) * WIDTH)
         delta[h : h + 1, :] = jnp.sum(gt[sl, :].astype(f32) * full[sl, :], axis=0, keepdims=True)
 
+    need(so)
+    of_c = lambda part: so[part, :]
+    quad_c = quad(of_c, qc, rc)
+
+    def chip_rows(block):
+        part = at(block, chip)
+        return g1[z1, part, :].astype(f32) + g1y[z1, part, :].astype(f32) + g1z[part, :].astype(f32)
+
+    need(g1, g1y, g1z, kept_b)
+    sg1[...] = chip_rows(1 - xx).astype(bf16)
+    g1_x = copy(sg1, rg1, to_x)
+    g1_x.start()
+    def terms2(block):
+        return g2[xx, block].astype(f32) + g2z[xx, block].astype(f32) + g2x[block].astype(f32)
+
+    need(g2, g2z, g2x)
+    sg2[...] = terms2(1 - z1).astype(bf16)
+    g2_z = copy(sg2, rg2, to_z1)
+    g2_z.start()
+    pass_b.wait()
+    step[1] = (kept_b[1].astype(f32) + near_b[1].astype(f32)).astype(bf16)
+    step_b = copy(step.at[1], got.at[1], to_x)
+    step_b.start()
+
     def attend(h):
         sl = slice(h * WIDTH, (h + 1) * WIDTH)
 
@@ -800,66 +834,35 @@
 
         gall[:, 3 * h * WIDTH : (3 * h + 1) * WIDTH] = (dqt[sl, :] * score_scale).T.astype(bf16)
 
-    pass_b.wait()
-    need(kept_b)
-    step[1] = (kept_b[1].astype(f32) + near_b[1].astype(f32)).astype(bf16)
-    step_b = copy(step.at[1], got.at[1], to_x)
-    step_b.start()
-
     for h in range(nh - 1):
         attend(h)
     need(n1, dw)
     for m in range(blocks):
         n1t[:, m * rows : (m + 1) * rows] = n1[m].T
     dw[:, :cut] += dot_nn(n1t[...], gall[:, :cut])
-    for i in range(2):
-        for j in range(2):
-            sa1[2 * i + j] = dw[rows_of(i, j, 1 - y), :cut].astype(bf16)
-    a1 = copy(sa1, ra1, to_y)
-    a1.start()
-    c1.wait()
-    for i in range(2):
-        sc2[i] = (so[rows_of(i, 1 - z0, y), :].astype(f32) + rc1[i, 1 - z0].astype(f32)).astype(bf16)
-    c2 = copy(sc2, rc2, to_z0)
-    c2.start()
-
-    def terms2(block):
-        return g2[xx, block].astype(f32) + g2z[xx, block].astype(f32) + g2x[block].astype(f32)
-
-    need(g2, g2z, g2x)
-    sg2[...] = terms2(1 - z1).astype(bf16)
-    g2_z = copy(sg2, rg2, to_z1)
-    g2_z.start()
+    of_a = lambda part: dw[part, :cut]
+    quad_a = quad(of_a, qa, ra)
 
     attend(nh - 1)
-    need(w)
-    second = jnp.zeros((1, d), f32)
-    for m in (1, 3, 2, 0):
-        gn = dot_nt(gall[m * rows : (m + 1) * rows, :used], w[...])
-        second += jnp.sum(gn, axis=0, keepdims=True)
-        low[m // 2 + 2 * (m % 2)] = gn.astype(bf16)
-        if m == 3:
-            pass_c = copy(low.at[2:4], near_c, to_core)
-            pass_c.start()
+    need(w, sums, sums1, gb, vec)
     third = jnp.sum(gall[:, :used].astype(f32), axis=0, keepdims=True)
-
-    need(sums, sums1, gb, vec)
     rest = wide - cut
     ext[...] = dw[:, cut:] + dot_nn(n1t[...], gall[:, cut:])
     small[...] = jnp.zeros_like(small)
     half = rest - 128
     base = used - cut - half
-    third = third + sums1[1:2, :used]
+    both_third = third + sums1[1:2, :used]
 
     def placed(part):
-        row = jnp.concatenate([third[:, (3 * h + part) * WIDTH : (3 * h + part + 1) * WIDTH] for h in range(nh)], axis=1)
+        pieces = [both_third[:, (3 * h + part) * WIDTH : (3 * h + part + 1) * WIDTH] for h in range(nh)]
+        row = jnp.concatenate(pieces, axis=1)
         spread = jnp.zeros((1, d), f32)
         for b in range(blocks):
             pieces = [jnp.zeros((1, hw), f32) if k != b else row for k in range(blocks)]
             spread = jnp.where(me == b, jnp.concatenate(pieces, axis=1), spread)
         return spread
 
-    rows_in = [placed(0), placed(2), sums[5:6], None, second + sums1[0:1], sums[2:3], sums[3:4], sums[1:2], sums[4:5], sums[0:1]]
+    rows_in = [placed(0), placed(2), sums[5:6], None, sums1[0:1], sums[2:3], sums[3:4], sums[1:2], sums[4:5], sums[0:1]]
     for k, row in enumerate(rows_in):
         if row is not None:
             small[base + k : base + k + 1, :] = row
@@ -867,78 +870,47 @@
     turned = small[...].T
     lane = lax.broadcasted_iota(jnp.int32, (1, 128), 1)
     gain_c, bias_c = turned[:, base + SMALL : base + SMALL + 1], turned[:, base + SMALL + 1 : base + SMALL + 2]
-    n1b_c = turned[:, base + 4 : base + 5]
-    total = jnp.sum(dw[:, :cut] * w[:, :cut].astype(f32), axis=1, keepdims=True)
-    total += jnp.sum(ext[:, : used - cut] * w[:, cut:].astype(f32), axis=1, keepdims=True)
+    weights = w[...].astype(f32)
+    n1b_c = turned[:, base + 4 : base + 5] + jnp.sum(weights * third, axis=1, keepdims=True)
+    total = jnp.sum(dw[:, :cut] * weights[:, :cut], axis=1, keepdims=True)
+    total += jnp.sum(ext[:, : used - cut] * weights[:, cut:], axis=1, keepdims=True)
     n1g_c = (total - bias_c * n1b_c) / gain_c
-    ext[:, half:] += jnp.where(lane == base + 3, n1g_c, jnp.where(lane < base + 10, turned, 0.0))
+    tile = jnp.where(lane < base + 10, turned, 0.0)
+    tile = jnp.where(lane == base + 3, n1g_c, jnp.where(lane == base + 4, n1b_c, tile))
+    ext[:, half:] += tile
     per = SMALL - 10
     for k in range(d // share):
         column = jnp.zeros((share, 128), f32)
         for q in range(per):
             column = jnp.where(lane == base + 10 + q, gb[(per * k + q) * share : (per * k + q + 1) * share, :], column)
         ext[k * share : (k + 1) * share, half:] += column
-    for i in range(2):
-        for k in range(2):
-            sb1[i, k] = ext[rows_of(i, 1 - z0, k), :].astype(bf16)
-    b1 = copy(sb1, rb1, to_z0)
-    b1.start()
-
-    def chip_rows(block):
-        part = at(block, chip)
-        return g1[z1, part, :].astype(f32) + g1y[z1, part, :].astype(f32) + rz1[part, :].astype(f32)
-
-    g1_z.wait()
-    sg1[...] = chip_rows(1 - xx).astype(bf16)
-    g1_x = copy(sg1, rg1, to_x)
-    g1_x.start()
+    of_b = lambda part: ext[part, :]
+    quad_b = quad(of_b, qb, rb)
+
+    for m in (1, 3, 2, 0):
+        low[m // 2 + 2 * (m % 2)] = dot_nt(gall[m * rows : (m + 1) * rows, :used], w[...]).astype(bf16)
+        if m == 3:
+            pass_c = copy(low.at[2:4], near_c, to_core)
+            pass_c.start()
+
+    last_c = onward(of_c, quad_c, rc, uc, vc)
+
+    last_a = onward(of_a, quad_a, ra, ua, va)
+
     pass_c.wait()
     step[2] = (low[1].astype(f32) + near_c[1].astype(f32)).astype(bf16)
     step_c = copy(step.at[2], got.at[2], to_x)
     step_c.start()
 
-    a1.wait()
-    for i in range(2):
-        sa2[i] = (dw[rows_of(i, 1 - z0, y), :cut] + ra1[2 * i + 1 - z0].astype(f32)).astype(bf16)
-    a2 = copy(sa2, ra2, to_z0)
-    a2.start()
-
-    def sum_a(i):
-        return dw[rows_of(i, z0, y), :cut] + ra1[2 * i + z0].astype(f32) + ra2[i].astype(f32)
-
-    def sum_b(i):
-        return ext[rows_of(i, z0, y), :] + rb1[i, y].astype(f32) + rb2[i].astype(f32)
-
-    def sum_c(i):
-        return so[rows_of(i, z0, y), :].astype(f32) + rc1[i, z0].astype(f32) + rc2[i].astype(f32)
-
-    c2.wait()
-    sc3[...] = sum_c(1 - z1).astype(bf16)
-    c3 = copy(sc3, rc3, to_z1)
-    c3.start()
-
     need(gmid, *x)
     gain = vec[0:1, :]
 
     def finish(i, g):
         tok[i] = (gmid[i * rows : (i + 1) * rows, :] + norm_back(x[i][...], gain, g)).astype(bf16)
 
-    b1.wait()
-    for i in range(2):
-        sb2[i] = (ext[rows_of(i, z0, 1 - y), :] + rb1[i, 1 - y].astype(f32)).astype(bf16)
-    b2 = copy(sb2, rb2, to_y)
-    b2.start()
     step_a.wait()
     finish(1, kept_a[0].astype(f32) + near_a[0].astype(f32) + got[0].astype(f32))
-    a2.wait()
-    sa3[...] = sum_a(1 - z1).astype(bf16)
-    a3 = copy(sa3, ra3, to_z1)
-    a3.start()
-    b2.wait()
-    sb3[...] = sum_b(1 - z1).astype(bf16)
-    b3 = copy(sb3, rb3, to_z1)
-    b3.start()
-
+    last_b = onward(of_b, quad_b, rb, ub, vb)
     g1_x.wait()
     cg1[...] = chip_rows(xx) + rg1[...].astype(f32)
     dg1_copy = copy(cg1.at[at(1 - core, share), :], dg1, to_core)
@@ -951,39 +923,35 @@
     step_b.wait()
     finish(2, kept_b[0].astype(f32) + near_b[0].astype(f32) + got[1].astype(f32))
 
-    c3.wait()
-    fin[:, wide:] = sum_c(z1) + rc3[...].astype(f32)
-    a3.wait()
-    fin[:, :cut] = sum_a(z1) + ra3[...].astype(f32)
-    b3.wait()
-    fin[:, cut:wide] = sum_b(z1) + rb3[...].astype(f32)
-    sx[...] = fin[at(1 - xx, chip), :].astype(bf16)
-    x_copy = copy(sx, rx, to_x)
-    x_copy.start()
-
-    dg1_copy.wait()
-    o1[core] = cg1[at(core, share), :]
-    o1[1 - core] = dg1[...]
+    last_c.wait()
+    fin[:, wide:] = quad_sum(of_c, rc, z1) + vc[...].astype(f32)
+    last_a.wait()
+    fin[:, :cut] = quad_sum(of_a, ra, z1) + va[...].astype(f32)
+    last_b.wait()
+    fin[:, cut:wide] = quad_sum(of_b, rb, z1) + vb[...].astype(f32)
+    give[...] = jnp.zeros_like(give)
+    gifts = []
+    for m in range(1, blocks):
+        give[m - 1, :share, :] = fin[at(flip_all(me, m), share), :].astype(bf16)
+        gifts.append(copy(give.at[m - 1], take.at[m - 1], to_kin[m - 1]))
+    for gift in gifts[::-1]:
+        gift.start()
+    e_out[0] = fin[at(me, share), :]
+
     dg2_copy.wait()
     o2[core] = cg2[at(core, wide2), :]
     o2[1 - core] = dg2[...]
     step_c.wait()
     finish(0, low[0].astype(f32) + near_c[0].astype(f32) + got[2].astype(f32))
-
-    x_copy.wait()
-    rxf[...] = rx[...].astype(f32)
-    sc[0] = fin[at(2 * xx + 1 - core, share), :]
-    sc[1] = rxf[at(1 - core, share), :]
-    c_copy = copy(sc, rc, to_core)
-    c_copy.start()
-    e_out[0] = fin[at(2 * xx + core, share), :]
-    e_out[2] = rxf[at(core, share), :]
-    c_copy.wait()
-    e_out[1] = rc[0]
-    e_out[3] = rc[1]
-
-
-LAST_IN = 28
+    dg1_copy.wait()
+    o1[core] = cg1[at(core, share), :]
+    o1[1 - core] = dg1[...]
+    for m in range(1, blocks):
+        gifts[m - 1].wait()
+        e_out[m] = take[m - 1, :share, :].astype(f32)
+
+
+LAST_IN = 29
 
 
 def last_image(share, shape, wide, c1, r2, c2, nh, at_piece, *args):
@@ -998,7 +966,7 @@
     pair = lambda shape, dtype=bf16: [pltpu.VMEM(shape, dtype)] * 2
     heads = pltpu.VMEM((nh, length, WIDTH), bf16)
     flat = pltpu.VMEM((hw, length), bf16)
-    copies = 21
+    copies = 24
     return pl.pallas_call(
         partial(last_kernel, blocks, nh, rows, share, at_piece),
         name="last",
@@ -1010,7 +978,7 @@
             jax.ShapeDtypeStruct((2, share, c1), f32),
             jax.ShapeDtypeStruct((2, r2 // 2, c2), f32),
         ],
-        scratch_shapes=[pltpu.VMEM(v.shape[1:] if k < 4 else v.shape, v.dtype) for k, v in enumerate(args)]
+        scratch_shapes=[pltpu.VMEM(v.shape[1:] if 3 <= k < 7 else v.shape, v.dtype) for k, v in enumerate(args)]
         + [flat, heads, heads, heads, heads, flat, flat]
         + [
             pltpu.VMEM((8, length), f32),
@@ -1021,22 +989,16 @@
             pltpu.VMEM((128, d), f32),
             pltpu.VMEM((d, rest), f32),
             pltpu.VMEM((four, both), f32),
-            pltpu.VMEM((chip, both), f32),
         ]
-        + pair((4, four, cut))
-        + pair((2, 2, four, rest))
-        + pair((2, 2, four, d // 2))
-        + pair((2, four, cut))
-        + pair((2, four, rest))
-        + pair((2, four, d // 2))
+        + pair((3, 2, four, cut))
+        + pair((3, 2, four, rest))
+        + pair((3, 2, four, d // 2))
         + pair((four, cut))
         + pair((four, rest))
         + pair((four, d // 2))
-        + pair((chip, both))
-        + pair((2, share, both), f32)
+        + pair((blocks - 1, -(-share // 16) * 16, both))
         + pair((2, rows, d))
         + pair((3, rows, d))
-        + pair((four, c1))
         + pair((chip, c1))
         + [pltpu.VMEM((chip, c1), f32), pltpu.VMEM((share, c1), f32)]
         + pair((r2, c2))
@@ -1294,18 +1256,20 @@
                     others = after(others, *before)
                     sum1.hold(before)
                     sum2.hold(before)
-                    send2 = sum2.send(x_dim)
-                    before, send2 = lax.optimization_barrier((before, send2))
+                    send2, send1 = sum2.send(x_dim), sum1.send(img2)
+                    before, send2, send1 = lax.optimization_barrier((before, send2, send1))
                     sum2.swap(send2, x_dim)
+                    sum1.swap(send1, img2)
                 *before, kept_i, passed_i = backward_image(
                     counts, i, firsts if i == 1 else others, 0, *saved[i], w, before, wide, nh
                 )
                 kept.append(kept_i)
                 passed.append(passed_i)
             dw, sums1 = before
-            (g1y, _), (g2z, _), (g2x, _) = sum1.terms[1], sum2.terms[1], sum2.terms[2]
-            pieces = (*others, *saved[0], w, dw, sums1, kept[0], near, kept[1], passed[1])
-            pieces += (g1, g1y, g2, g2z, g2x, so, sums, vec, gb1, gmid, *mine)
+            ((g1y, _), (g1z, _)), ((g2z, _), (g2x, _)) = sum1.terms[1:], sum2.terms[1:]
+            n1, *rest = saved[0]
+            pieces = (passed[1], kept[0], near, *others, *rest, so, g1, g1y, g1z, kept[1], n1, dw, w, sums, sums1, vec, gb1)
+            pieces += (g2, g2z, g2x, gmid, *mine)
             tok, e, o1, o2 = last_image(
                 share, tokens.shape, wide, g1.shape[-1], 2 * (ff // n), half, nh, images - 2, *pieces
             )

time: 221 us -> 211 us (0.955); the launches traced: 217 us -> 211 us
  Pallas kernels: 175 us -> 163 us
  waiting for transfers between devices: 9.79 us -> 15.3 us
    pallas_call x1, Pallas kernels: 45.5 us -> 37.3 us  [last_image(): pl.pallas_call(partial(last_kernel, blocks, nh, rows, share, at_piece), n...]
    ppermute x3 -> x4, waiting for transfers between devices: 3.71 us -> 9.18 us  [swap(): return lax.ppermute(value, axis, [(i, i ^ 1 << k) for i in range(n)])]
    pallas_call x2, Pallas kernels: 24 us -> 19.9 us  [backward_image(): pl.pallas_call(partial(backward_kernel, blocks, nh, rows, image, at, not...]
    pallas_call x3, Pallas kernels: 43.1 us -> 40 us  [forward_image(): pl.pallas_call(partial(forward_kernel, blocks, nh, rows, image), name='at...]
    pallas_call x1, Pallas kernels: 58.5 us -> 61.6 us  [middle_layers(): pl.pallas_call(partial(middle_kernel, blocks, images, steps, bits), name=...]
  transfers between devices with their start and end apart: 22 -> 23, of which waited for: 4 -> 6; matrix products, arithmetic and copies ran while one was open for 3% -> 4% of each run, Pallas kernels for 31% -> 28%
where the time goes in v1:
time: 211 us
  Pallas kernels  163 us (77%)
  starting transfers between devices  15.9 us (8%)
  waiting for transfers between devices  15.3 us (7%)
  local copies, waits for them, and re-layouts  9.61 us (5%)
  other arithmetic  3.93 us (2%)
  between operations  3.52 us (2%)
    pallas_call x1, Pallas kernels, middle_layers(): pl.pallas_call(partial(middle_kernel, blocks, images, steps, bits), name=...  61.6 us
    pallas_call x3, Pallas kernels, forward_image(): pl.pallas_call(partial(forward_kernel, blocks, nh, rows, image), name='at...  40 us
    pallas_call x1, Pallas kernels, last_image(): pl.pallas_call(partial(last_kernel, blocks, nh, rows, share, at_piece), n...  37.3 us
    pallas_call x2, Pallas kernels, backward_image(): pl.pallas_call(partial(backward_kernel, blocks, nh, rows, image, at, not...  19.9 us
    ppermute x19, starting transfers between devices, swap_blk(): return lax.ppermute(value, 'blk', [(b, b ^ m) for b in range(blocks)])  12.6 us
    ppermute x4, waiting for transfers between devices, swap(): return lax.ppermute(value, axis, [(i, i ^ 1 << k) for i in range(n)])  9.18 us
    ppermute x19, waiting for transfers between devices, swap_blk(): return lax.ppermute(value, 'blk', [(b, b ^ m) for b in range(blocks)])  6.09 us
  transfers between devices with their start and end apart: 23, of which 6 were waited for; matrix products, arithmetic and copies ran while one was open for 4% of the time, Pallas kernels for 28%

profile of v1, /device:TPU:0, one launch (start us, length us, event | category | flops | bytes accessed | tf_op | source)
XLA Modules:
  0.0 210.8 jit_solution(13219211757255418600)
XLA Ops:
  0.8 1.4 iota_reduce_fusion
  4.1 1.3 dynamic-slice_bitcast_fusion.3
  5.5 3.0 %collective-permute-start = (bf16[256,768]{1,0:T(8,128)(2,1)S(1)}, bf16[256,768]{1,0:T(8,128)(2,1)S(1)}, u32[]{:S(2)}, u32[]{:S(2)}) collective-permute-start(bf16[256,768]{1,0:T(8,128)(2,1)S(1)} %get-tuple-element.105.refs_0_.refs_12_.refs_26_), channel_id=1, source_target_pairs={{0,2},{1,3},{2,0},{3,1},{4,6},{5,7},{6,4},{7,5},{8,10},{9,11},{10,... | collective-permute-start | bytes 1179656 | tf_op jit(solution)/shard_map/ppermute | solution.py:1201
  10.3 2.0 constant_dynamic-slice_fusion.2
  13.0 4.6 %collective-permute-done.refs_2_ = bf16[256,768]{1,0:T(8,128)(2,1)S(1)} collective-permute-done((bf16[256,768]{1,0:T(8,128)(2,1)S(1)}, bf16[256,768]{1,0:T(8,128)(2,1)S(1)}, u32[]{:S(2)}, u32[]{:S(2)}) %collective-permute-start) | collective-permute-done | bytes 393248 | tf_op jit(solution)/shard_map/ppermute | solution.py:1201
  18.1 1.7 collective-permute-start.6
  19.8 1.3 copy.40.refs_5_.refs_8_.refs_17_
  21.2 0.7 copy-done.25
  21.9 12.1 %attend_forward.3 = (bf16[4,256,768]{2,1,0:T(8,128)(2,1)}, bf16[4,256,576]{2,1,0:T(8,128)(2,1)}, f32[192,1024]{1,0:T(8,128)}, f32[8,1024]{1,0:T(8,128)}, bf16[19...) custom-call(s32[3]{0:T(128)} %counts.11, ...), custom_call_target="tpu_custom_call" | custom-call | flops 2516582400 | bytes 8000000 | tf_op jit(solution)/shard_map/attend_forward/pallas_call | solution.py:114
  34.9 0.9 collective-permute-done.7.refs_1_
  36.5 0.7 copy-done.27
  37.3 20.4 %attend_forward.4 = (bf16[4,256,768]{2,1,0:T(8,128)(2,1)}, bf16[4,256,576]{2,1,0:T(8,128)(2,1)}, f32[192,1024]{1,0:T(8,128)}, f32[8,1024]{1,0:T(8,128)}, bf16[19...) custom-call(s32[3]{0:T(128)} %counts.11, ...), custom_call_target="tpu_custom_call" | custom-call | flops 2516582400 | bytes 8000000 | tf_op jit(solution)/shard_map/attend_forward/pallas_call | solution.py:114
  59.3 1.1 pad_maximum_fusion.refs_15_
  60.4 0.8 collective-permute-start.4
  61.1 1.0 collective-permute-start.5
  62.6 0.8 collective-permute-start.10
  63.4 0.7 collective-permute-start.11
  64.2 7.4 %attend_forward.5 = (bf16[4,256,768]{2,1,0:T(8,128)(2,1)}, bf16[4,256,576]{2,1,0:T(8,128)(2,1)}, f32[192,1024]{1,0:T(8,128)}, f32[8,1024]{1,0:T(8,128)}, bf16[19...) custom-call(s32[3]{0:T(128)} %counts.11, ...), custom_call_target="tpu_custom_call" | custom-call | flops 2516582400 | bytes 8000000 | tf_op jit(solution)/shard_map/attend_forward/pallas_call | solution.py:114
  72.4 61.6 %middle_layers.1 = (bf16[768,768]{1,0:T(8,128)(2,1)}, f32[768,768]{1,0:T(8,128)}, f32[3072,128]{1,0:T(8,128)}, f32[8,768]{1,0:T(8,128)}, bf16[768,384]{1,0:T(8,1...) custom-call(bf16[192,256]{1,0:T(8,128)(2,1)} %get-tuple-element.107., ...), custom_call_target="tpu_custom_call" | custom-call | flops 24461180928 | bytes 30000000 | tf_op jit(solution)/shard_map/middle_layers/pallas_call | solution.py:612
  134.0 1.2 collective-permute-start.18
  135.3 1.1 collective-permute-start.16
  136.4 0.8 collective-permute-start.17
  137.1 0.8 collective-permute-start.19
  138.0 10.0 %attend_backward.2 = (f32[768,640]{1,0:T(8,128)}, f32[8,768]{1,0:T(8,128)}, bf16[2,256,768]{2,1,0:T(8,128)(2,1)}, bf16[2,256,768]{2,1,0:T(8,128)(2,1)}) custom-call(s32[3]{0:T(128)} %counts.11, bf16[1,192,256]{2,1,0:T(8,128)(2,1)} %get-tuple-element.129.refs_0_, bf16[1,192,256]{2,1,0:T(8,128)(2,1)} %get-tuple-element.130.refs_1_, ...), custom_call_target="tpu_custom_call" | custom-call | flops 5838471168 | bytes 12000000 | tf_op jit(solution)/shard_map/attend_backward/pallas_call | solution.py:251
  148.1 1.4 collective-permute-done.18.refs_23_
  149.6 3.3 %collective-permute-done.19.refs_12_ = bf16[2,96,1536]{2,1,0:T(8,128)(2,1)S(1)} collective-permute-done((bf16[2,96,1536]{2,1,0:T(8,128)(2,1)}, bf16[2,96,1536]{2,1,0:T(8,128)(2,1)S(1)}, u32[]{:S(2)}, u32[]{:S(2)}) %collective-permute-start.19) | collective-permute-done | bytes 589856 | tf_op jit(solution)/shard_map/ppermute | solution.py:1114
  153.0 1.2 collective-permute-start.22
  154.2 9.9 %attend_backward.3 = (f32[768,640]{1,0:T(8,128)}, f32[8,768]{1,0:T(8,128)}, bf16[2,256,768]{2,1,0:T(8,128)(2,1)}, bf16[2,256,768]{2,1,0:T(8,128)(2,1)}) custom-call(s32[3]{0:T(128)} %counts.11, bf16[2,192,256]{2,1,0:T(8,128)(2,1)} %get-tuple-element.138.refs_0_.refs_3_, bf16[2,192,256]{2,1,0:T(8,128)(2,1)} %copy-done.30, bf16[2,192,256]{2,1,0:T(8,128)(2,1)} %copy-done.31, ...), custom_call_target="tpu_custom_call" | custom-call | flops 5838471168 | bytes 12000000 | tf_op jit(solution)/shard_map/attend_backward/pallas_call | solution.py:251
  164.1 4.5 %collective-permute-done.21.refs_13_ = bf16[96,1536]{1,0:T(8,128)(2,1)S(1)} collective-permute-done((bf16[96,1536]{1,0:T(8,128)(2,1)S(1)}, bf16[96,1536]{1,0:T(8,128)(2,1)S(1)}, u32[]{:S(2)}, u32[]{:S(2)}) %collective-permute-start.21) | collective-permute-done | bytes 294944 | tf_op jit(solution)/shard_map/ppermute | solution.py:1114
  168.6 0.7 copy-done.28
  169.4 37.3 %last.1 = (bf16[3,256,768]{2,1,0:T(8,128)(2,1)}, f32[4,24,1024]{2,1,0:T(8,128)}, f32[2,24,1536]{2,1,0:T(8,128)}, f32[2,96,384]{2,1,0:T(8,128)}) custom-call(bf16[2,256,768]{2,1,0:T(8,128)(2,1)} %get-tuple-element.154.refs_0_, bf16[2,256,768]{2,1,0:T(8,128)(2,1)} %get-tuple-element.155.refs_1_, bf16[2,256,768]{2,1,0:T(8,128)(2,1)} %copy-done.19, ...), custom_call_target="tpu_custom_call" | custom-call | flops 30000001024 | bytes 20000000 | tf_op jit(solution)/shard_map/last/pallas_call | solution.py:970
  206.8 3.8 %layout.1 = (bf16[3,256,768]{2,1,0:T(8,128)(2,1)}, bf16[3,256,768]{2,1,0:T(8,128)(2,1)}, f32[24,2304]{1,0:T(8,128)}, f32[24,768]{1,0:T(8,128)}, f32[24,3072]{1,0...) custom-call(s32[3]{0:T(128)} %counts.11, ...), custom_call_target="tpu_custom_call" | custom-call | tf_op jit(solution)/shard_map/layout/pallas_call | solution.py:1058
  (145 shorter events, 7.7 us)
Async XLA Ops:
  5.4 12.2 %copy-start.2 = (bf16[256,768]{1,0:T(8,128)(2,1)}, bf16[256,768]{1,0:T(8,128)(2,1)S(1)}, u32[]{:S(2)}) copy-start(bf16[256,768]{1,0:T(8,128)(2,1)S(1)} %get-tuple-element.105.refs_0_.refs_12_.refs_26_) | copy-start | bytes 1179652
  5.4 28.6 %copy-start.3 = (bf16[256,768]{1,0:T(8,128)(2,1)}, bf16[256,768]{1,0:T(8,128)(2,1)S(1)}, u32[]{:S(2)}) copy-start(bf16[256,768]{1,0:T(8,128)(2,1)S(1)} %get-tuple-element.112.refs_0_.refs_13_.refs_27_) | copy-start | bytes 1179652
  5.4 52.3 %copy-start.1 = (bf16[256,768]{1,0:T(8,128)(2,1)}, bf16[256,768]{1,0:T(8,128)(2,1)S(1)}, u32[]{:S(2)}) copy-start(bf16[256,768]{1,0:T(8,128)(2,1)S(1)} %get-tuple-element.119.refs_0_.refs_14_.refs_28_) | copy-start | bytes 1179652
  5.5 12.1 %collective-permute-start = (bf16[256,768]{1,0:T(8,128)(2,1)S(1)}, bf16[256,768]{1,0:T(8,128)(2,1)S(1)}, u32[]{:S(2)}, u32[]{:S(2)}) collective-permute-start(bf16[256,768]{1,0:T(8,128)(2,1)S(1)} %get-tuple-element.105.refs_0_.refs_12_.refs_26_), channel_id=1, source_target_pairs={{0,2},{1,3},{2,0},{3,1},{4,6},{5,7},{6,4},{7,5},{8,10},{9,11},{10,... | collective-permute-start | bytes 1179656 | tf_op jit(solution)/shard_map/ppermute | solution.py:1201
  17.6 3.6 %collective-permute-start.1 = (bf16[256,768]{1,0:T(8,128)(2,1)S(1)}, bf16[256,768]{1,0:T(8,128)(2,1)S(1)}, u32[]{:S(2)}, u32[]{:S(2)}) collective-permute-start(bf16[256,768]{1,0:T(8,128)(2,1)S(1)} %get-tuple-element.105.refs_0_.refs_12_.refs_26_), channel_id=1, source_target_pairs={{0,1},{1,0},{2,3},{3,2},{4,5},{5,4},{6,7},{7,6},{8,9},{9,8},{10,11... | collective-permute-start | bytes 1179656 | tf_op jit(solution)/shard_map/ppermute | solution.py:1201
  17.6 3.6 %collective-permute-start.2 = (bf16[256,768]{1,0:T(8,128)(2,1)S(1)}, bf16[256,768]{1,0:T(8,128)(2,1)}, u32[]{:S(2)}, u32[]{:S(2)}) collective-permute-start(bf16[256,768]{1,0:T(8,128)(2,1)S(1)} %collective-permute-done.refs_2_), channel_id=1, source_target_pairs={{0,1},{1,0},{2,3},{3,2},{4,5},{5,4},{6,7},{7,6},{8,9},{9,8},{10,11... | collective-permute-start | bytes 1179656 | tf_op jit(solution)/shard_map/ppermute | solution.py:1201
  18.1 15.9 %collective-permute-start.6 = (bf16[256,768]{1,0:T(8,128)(2,1)S(1)}, bf16[256,768]{1,0:T(8,128)(2,1)S(1)}, u32[]{:S(2)}, u32[]{:S(2)}) collective-permute-start(bf16[256,768]{1,0:T(8,128)(2,1)S(1)} %get-tuple-element.112.refs_0_.refs_13_.refs_27_), channel_id=1, source_target_pairs={{0,2},{1,3},{2,0},{3,1},{4,6},{5,7},{6,4},{7,5},{8,10},{9,11},{10,... | collective-permute-start | bytes 1179656 | tf_op jit(solution)/shard_map/ppermute | solution.py:1201
  34.0 1.8 collective-permute-start.7
  34.1 2.3 %collective-permute-start.8 = (bf16[256,768]{1,0:T(8,128)(2,1)S(1)}, bf16[256,768]{1,0:T(8,128)(2,1)S(1)}, u32[]{:S(2)}, u32[]{:S(2)}) collective-permute-start(bf16[256,768]{1,0:T(8,128)(2,1)S(1)} %collective-permute-done.6.refs_2_), channel_id=1, source_target_pairs={{0,1},{1,0},{2,3},{3,2},{4,5},{5,4},{6,7},{7,6},{8,9},{9,8},{10,11... | collective-permute-start | bytes 1179656 | tf_op jit(solution)/shard_map/ppermute | solution.py:1201
  34.6 23.7 %copy-start.8 = (bf16[3072]{0:T(1024)(128)(2,1)S(1)}, bf16[3072]{0:T(1024)(128)(2,1)}, u32[]{:S(2)}) copy-start(bf16[3072]{0:T(1024)(128)(2,1)} %param.30) | copy-start | bytes 18436
  34.6 24.3 %copy-start = (bf16[3,256,768]{2,1,0:T(8,128)(2,1)S(1)}, bf16[3,256,768]{2,1,0:T(8,128)(2,1)}, u32[]{:S(2)}) copy-start(bf16[3,256,768]{2,1,0:T(8,128)(2,1)} %param.35) | copy-start | bytes 3538948
  34.6 23.1 %collective-permute-start.12 = (bf16[256,768]{1,0:T(8,128)(2,1)S(1)}, bf16[256,768]{1,0:T(8,128)(2,1)S(1)}, u32[]{:S(2)}, u32[]{:S(2)}) collective-permute-start(bf16[256,768]{1,0:T(8,128)(2,1)S(1)} %get-tuple-element.119.refs_0_.refs_14_.refs_28_), channel_id=1, source_target_pairs={{0,2},{1,3},{2,0},{3,1},{4,6},{5,7},{6,4},{7,5},{8,10},{9,11},{10,... | collective-permute-start | bytes 1179656 | tf_op jit(solution)/shard_map/ppermute | solution.py:1201
  57.7 4.9 %collective-permute-start.13 = (bf16[256,768]{1,0:T(8,128)(2,1)S(1)}, bf16[256,768]{1,0:T(8,128)(2,1)S(1)}, u32[]{:S(2)}, u32[]{:S(2)}) collective-permute-start(bf16[256,768]{1,0:T(8,128)(2,1)S(1)} %get-tuple-element.119.refs_0_.refs_14_.refs_28_), channel_id=1, source_target_pairs={{0,1},{1,0},{2,3},{3,2},{4,5},{5,4},{6,7},{7,6},{8,9},{9,8},{10,11... | collective-permute-start | bytes 1179656 | tf_op jit(solution)/shard_map/ppermute | solution.py:1201
  57.9 5.5 %collective-permute-start.14 = (bf16[256,768]{1,0:T(8,128)(2,1)S(1)}, bf16[256,768]{1,0:T(8,128)(2,1)S(1)}, u32[]{:S(2)}, u32[]{:S(2)}) collective-permute-start(bf16[256,768]{1,0:T(8,128)(2,1)S(1)} %collective-permute-done.12.refs_2_), channel_id=1, source_target_pairs={{0,1},{1,0},{2,3},{3,2},{4,5},{5,4},{6,7},{7,6},{8,9},{9,8},{10,11... | collective-permute-start | bytes 1179656 | tf_op jit(solution)/shard_map/ppermute | solution.py:1201
  59.1 3.0 %collective-permute-start.3 = (bf16[192,256]{1,0:T(8,128)(2,1)S(1)}, bf16[192,256]{1,0:T(8,128)(2,1)S(1)}, u32[]{:S(2)}, u32[]{:S(2)}) collective-permute-start(bf16[192,256]{1,0:T(8,128)(2,1)S(1)} %copy-done.40), channel_id=1, source_target_pairs={{0,1},{1,0},{2,3},{3,2},{4,5},{5,4},{6,7},{7,6},{8,9},{9,8},{10,11... | collective-permute-start | bytes 294920 | tf_op jit(solution)/shard_map/ppermute | solution.py:1201
  60.4 11.2 %collective-permute-start.4 = (bf16[192,256]{1,0:T(8,128)(2,1)S(1)}, bf16[192,256]{1,0:T(8,128)(2,1)S(1)}, u32[]{:S(2)}, u32[]{:S(2)}) collective-permute-start(bf16[192,256]{1,0:T(8,128)(2,1)S(1)} %copy-done.34), channel_id=1, source_target_pairs={{0,2},{1,3},{2,0},{3,1},{4,6},{5,7},{6,4},{7,5},{8,10},{9,11},{10,... | collective-permute-start | bytes 294920 | tf_op jit(solution)/shard_map/ppermute | solution.py:1201
  61.1 10.5 %collective-permute-start.5 = (bf16[192,256]{1,0:T(8,128)(2,1)S(1)}, bf16[192,256]{1,0:T(8,128)(2,1)S(1)}, u32[]{:S(2)}, u32[]{:S(2)}) collective-permute-start(bf16[192,256]{1,0:T(8,128)(2,1)S(1)} %copy-done.33), channel_id=1, source_target_pairs={{0,3},{1,2},{2,1},{3,0},{4,7},{5,6},{6,5},{7,4},{8,11},{9,10},{10,... | collective-permute-start | bytes 294920 | tf_op jit(solution)/shard_map/ppermute | solution.py:1201
  62.1 9.6 %collective-permute-start.9 = (bf16[192,256]{1,0:T(8,128)(2,1)S(1)}, bf16[192,256]{1,0:T(8,128)(2,1)S(1)}, u32[]{:S(2)}, u32[]{:S(2)}) collective-permute-start(bf16[192,256]{1,0:T(8,128)(2,1)S(1)} %copy-done.37), channel_id=1, source_target_pairs={{0,1},{1,0},{2,3},{3,2},{4,5},{5,4},{6,7},{7,6},{8,9},{9,8},{10,11... | collective-permute-start | bytes 294920 | tf_op jit(solution)/shard_map/ppermute | solution.py:1201
  62.6 9.1 %collective-permute-start.10 = (bf16[192,256]{1,0:T(8,128)(2,1)S(1)}, bf16[192,256]{1,0:T(8,128)(2,1)S(1)}, u32[]{:S(2)}, u32[]{:S(2)}) collective-permute-start(bf16[192,256]{1,0:T(8,128)(2,1)S(1)} %copy-done.36), channel_id=1, source_target_pairs={{0,2},{1,3},{2,0},{3,1},{4,6},{5,7},{6,4},{7,5},{8,10},{9,11},{10,... | collective-permute-start | bytes 294920 | tf_op jit(solution)/shard_map/ppermute | solution.py:1201
  63.4 8.3 %collective-permute-start.11 = (bf16[192,256]{1,0:T(8,128)(2,1)S(1)}, bf16[192,256]{1,0:T(8,128)(2,1)S(1)}, u32[]{:S(2)}, u32[]{:S(2)}) collective-permute-start(bf16[192,256]{1,0:T(8,128)(2,1)S(1)} %copy-done.35), channel_id=1, source_target_pairs={{0,3},{1,2},{2,1},{3,0},{4,7},{5,6},{6,5},{7,4},{8,11},{9,10},{10,... | collective-permute-start | bytes 294920 | tf_op jit(solution)/shard_map/ppermute | solution.py:1201
  134.0 15.5 %collective-permute-start.18 = (bf16[2,2,192,384]{3,2,1,0:T(8,128)(2,1)}, bf16[2,2,192,384]{3,2,1,0:T(8,128)(2,1)S(1)}, u32[]{:S(2)}, u32[]{:S(2)}) collective-permute-start(bf16[2,2,192,384]{3,2,1,0:T(8,128)(2,1)} %get-tuple-element.147), channel_id=1, source_target_pairs={{0,8},{4,12},{8,0},{12,4},{16,24},{20,28},{24,16},{28,20},{1,9},{5... | collective-permute-start | bytes 1769480 | tf_op jit(solution)/shard_map/ppermute | solution.py:1114
  135.3 12.7 %collective-permute-start.15 = (bf16[2,192,256]{2,1,0:T(8,128)(2,1)}, bf16[2,192,256]{2,1,0:T(8,128)(2,1)S(1)}, u32[]{:S(2)}, u32[]{:S(2)}) collective-permute-start(bf16[2,192,256]{2,1,0:T(8,128)(2,1)} %get-tuple-element.126), channel_id=1, source_target_pairs={{0,1},{1,0},{2,3},{3,2},{4,5},{5,4},{6,7},{7,6},{8,9},{9,8},{10,11... | collective-permute-start | bytes 589832 | tf_op jit(solution)/shard_map/ppermute | solution.py:1201
  135.3 12.8 %collective-permute-start.16 = (bf16[2,192,256]{2,1,0:T(8,128)(2,1)}, bf16[2,192,256]{2,1,0:T(8,128)(2,1)S(1)}, u32[]{:S(2)}, u32[]{:S(2)}) collective-permute-start(bf16[2,192,256]{2,1,0:T(8,128)(2,1)} %get-tuple-element.127), channel_id=1, source_target_pairs={{0,2},{1,3},{2,0},{3,1},{4,6},{5,7},{6,4},{7,5},{8,10},{9,11},{10,... | collective-permute-start | bytes 589832 | tf_op jit(solution)/shard_map/ppermute | solution.py:1201
  136.4 11.7 %collective-permute-start.17 = (bf16[2,192,256]{2,1,0:T(8,128)(2,1)}, bf16[2,192,256]{2,1,0:T(8,128)(2,1)S(1)}, u32[]{:S(2)}, u32[]{:S(2)}) collective-permute-start(bf16[2,192,256]{2,1,0:T(8,128)(2,1)} %get-tuple-element.128), channel_id=1, source_target_pairs={{0,3},{1,2},{2,1},{3,0},{4,7},{5,6},{6,5},{7,4},{8,11},{9,10},{10,... | collective-permute-start | bytes 589832 | tf_op jit(solution)/shard_map/ppermute | solution.py:1201
  137.1 15.7 %collective-permute-start.19 = (bf16[2,96,1536]{2,1,0:T(8,128)(2,1)}, bf16[2,96,1536]{2,1,0:T(8,128)(2,1)S(1)}, u32[]{:S(2)}, u32[]{:S(2)}) collective-permute-start(bf16[2,96,1536]{2,1,0:T(8,128)(2,1)} %get-tuple-element.150), channel_id=1, source_target_pairs={{0,4},{4,0},{8,12},{12,8},{16,20},{20,16},{24,28},{28,24},{1,5},{5... | collective-permute-start | bytes 1769480 | tf_op jit(solution)/shard_map/ppermute | solution.py:1114
  138.0 11.6 %copy-start.5 = (bf16[2,2,192,384]{3,2,1,0:T(8,128)(2,1)S(1)}, bf16[2,2,192,384]{3,2,1,0:T(8,128)(2,1)}, u32[]{:S(2)}) copy-start(bf16[2,2,192,384]{3,2,1,0:T(8,128)(2,1)} %get-tuple-element.146.refs_22_) | copy-start | bytes 1769476
  138.0 14.9 %copy-start.4 = (bf16[2,96,1536]{2,1,0:T(8,128)(2,1)S(1)}, bf16[2,96,1536]{2,1,0:T(8,128)(2,1)}, u32[]{:S(2)}) copy-start(bf16[2,96,1536]{2,1,0:T(8,128)(2,1)} %get-tuple-element.149.refs_11_) | copy-start | bytes 1769476
  148.0 16.1 %collective-permute-start.20 = (bf16[2,256,768]{2,1,0:T(8,128)(2,1)}, bf16[2,256,768]{2,1,0:T(8,128)(2,1)S(1)}, u32[]{:S(2)}, u32[]{:S(2)}) collective-permute-start(bf16[2,256,768]{2,1,0:T(8,128)(2,1)} %get-tuple-element.156), channel_id=1, source_target_pairs={{0,1},{1,0},{2,3},{3,2},{4,5},{5,4},{6,7},{7,6},{8,9},{9,8},{10,11... | collective-permute-start | bytes 2359304 | tf_op jit(solution)/shard_map/ppermute | solution.py:1201
  149.5 14.6 %copy-start.6 = (bf16[2,2,192,384]{3,2,1,0:T(8,128)(2,1)}, bf16[2,2,192,384]{3,2,1,0:T(8,128)(2,1)S(1)}, u32[]{:S(2)}) copy-start(bf16[2,2,192,384]{3,2,1,0:T(8,128)(2,1)S(1)} %collective-permute-done.18.refs_23_) | copy-start | bytes 1769476
  152.9 11.2 %copy-start.7 = (bf16[2,96,1536]{2,1,0:T(8,128)(2,1)}, bf16[2,96,1536]{2,1,0:T(8,128)(2,1)S(1)}, u32[]{:S(2)}) copy-start(bf16[2,96,1536]{2,1,0:T(8,128)(2,1)S(1)} %collective-permute-done.19.refs_12_) | copy-start | bytes 1769476
  152.9 15.7 %collective-permute-start.21 = (bf16[96,1536]{1,0:T(8,128)(2,1)S(1)}, bf16[96,1536]{1,0:T(8,128)(2,1)S(1)}, u32[]{:S(2)}, u32[]{:S(2)}) collective-permute-start(bf16[96,1536]{1,0:T(8,128)(2,1)S(1)} %fusion.1), channel_id=1, source_target_pairs={{0,16},{4,20},{8,24},{12,28},{16,0},{20,4},{24,8},{28,12},{1,17},{... | collective-permute-start | bytes 884744 | tf_op jit(solution)/shard_map/ppermute | solution.py:1114
  153.0 15.6 %collective-permute-start.22 = (bf16[2,192,384]{2,1,0:T(8,128)(2,1)S(1)}, bf16[2,192,384]{2,1,0:T(8,128)(2,1)S(1)}, u32[]{:S(2)}, u32[]{:S(2)}) collective-permute-start(bf16[2,192,384]{2,1,0:T(8,128)(2,1)S(1)} %fusion), channel_id=1, source_target_pairs={{0,2},{1,3},{2,0},{3,1},{4,6},{5,7},{6,4},{7,5},{8,10},{9,11},{10,... | collective-permute-start | bytes 884744 | tf_op jit(solution)/shard_map/ppermute | solution.py:1114
  (36 other events, 145.4 us)

commit v2 on v1

--- a/solution.py
+++ b/solution.py
@@ -45,19 +45,246 @@
 
 
 def place(counts, k):
-    best, top = 0, counts[0]
-    for i in range(1, counts.shape[0]):
-        best = jnp.where(counts[i] > top, i, best)
-        top = jnp.maximum(top, counts[i])
-    return lax.rem(best + k, counts.shape[0])
-
-
-def forward_kernel(blocks, nh, rows, image, counts, *refs):
+    images = counts.shape[0]
+    found = 0
+    for i in range(images):
+        before = 0
+        for j in range(images):
+            if j != i:
+                ahead = counts[j] >= counts[i] if j < i else counts[j] > counts[i]
+                before = before + jnp.where(ahead, 1, 0)
+        found = found + jnp.where(before == k, i, 0)
+    return found
+
+
+def turn_kernel(counts, tokens, *refs):
+    images = tokens.shape[0]
+    outs, (held, load_sem, save_sem) = refs[:images], refs[images:]
+    loads = [pltpu.make_async_copy(tokens.at[place(counts, k)], held.at[k], load_sem.at[k]) for k in range(images)]
+    saves = [pltpu.make_async_copy(held.at[k], outs[k], save_sem.at[k]) for k in range(images)]
+    for load in loads:
+        load.start()
+    for load, save in zip(loads, saves):
+        load.wait()
+        save.start()
+    for save in saves:
+        save.wait()
+
+
+def turn(counts, tokens):
+    images = tokens.shape[0]
+    far = pl.BlockSpec(memory_space=pl.ANY)
+    return pl.pallas_call(
+        turn_kernel,
+        name="turn",
+        in_specs=[pl.BlockSpec(memory_space=pltpu.SMEM), far],
+        out_specs=[far] * images,
+        out_shape=[jax.ShapeDtypeStruct(tokens.shape[1:], tokens.dtype)] * images,
+        scratch_shapes=[
+            pltpu.VMEM(tokens.shape, tokens.dtype),
+            pltpu.SemaphoreType.DMA((images,)),
+            pltpu.SemaphoreType.DMA((images,)),
+        ],
+        compiler_params=params(),
+    )(counts, tokens)
+
+
+def first_kernel(blocks, nh, rows, *refs):
+    x0_far, x1_far, weight_far = refs[:3]
+    gain, shift, bias_q, bias_v = (ref[...].astype(f32).reshape(1, -1) for ref in refs[3:7])
+    n1_far, qkv_far, full_far, lse_far = refs[7:11]
+    refs = refs[11:]
+    out_far, (w_far, wb_out), next_far, refs = refs[:blocks], refs[blocks : blocks + 2], refs[blocks + 2 : blocks + 5], refs[blocks + 5 :]
+    xs, xn, window, w, n1, qkv, outs, lse, qt, ks, vt, peak, acc, send_sem, recv_sem, load_sem, save_sem = refs
+    hw = nh * WIDTH
+    length = rows * blocks
+    d = xs.shape[2]
+    me = lax.axis_index("blk")
+    odd = lax.rem(me, 2)
+    to_core, to_x = {"blk": flip(me, 0)}, {"blk": flip(me, 1)}
+    low = pl.multiple_of(me * hw - odd * WIDTH, 128)
+    loads = [pltpu.make_async_copy(x0_far, xs.at[0], load_sem.at[0]), pltpu.make_async_copy(x1_far, xn.at[0], load_sem.at[1])]
+    for k in range(3):
+        part = weight_far.at[:, pl.ds(pl.multiple_of(k * d + low, 128), 256)]
+        loads.append(pltpu.make_async_copy(part, window.at[k], load_sem.at[2 + k]))
+    for load in loads:
+        load.start()
+    saves = []
+
+    def save(src, dst):
+        saves.append(pltpu.make_async_copy(src, dst, save_sem.at[len(saves)]))
+        saves[-1].start()
+
+    def copy(k, src, dst, peer):
+        return pltpu.make_async_remote_copy(
+            src_ref=src,
+            dst_ref=dst,
+            send_sem=send_sem.at[k],
+            recv_sem=recv_sem.at[k],
+            device_id=peer,
+            device_id_type=pl.DeviceIdType.MESH,
+        )
+
+    meet([to_core, to_x])
+    loads[0].wait()
+    far_0 = copy(0, xs.at[0], xs.at[2], to_x)
+    far_0.start()
+    near_0 = copy(1, xs.at[0], xs.at[1], to_core)
+    near_0.start()
+    loads[1].wait()
+    far_1 = copy(2, xn.at[0], xn.at[2], to_x)
+    far_1.start()
+    near_1 = copy(3, xn.at[0], xn.at[1], to_core)
+    near_1.start()
+    for k in range(3):
+        loads[2 + k].wait()
+    bias = jnp.zeros((1, 3 * hw), f32)
+    for b in range(blocks):
+        pieces = []
+        for h in range(nh):
+            at = slice(b * hw + h * WIDTH, b * hw + (h + 1) * WIDTH)
+            pieces += [bias_q[:, at], jnp.zeros((1, WIDTH), f32), bias_v[:, at]]
+        bias = jnp.where(me == b, jnp.concatenate(pieces, axis=1), bias)
+    wb_out[...] = bias
+    for h in range(nh):
+        for k in range(3):
+            even = window[k, :, h * WIDTH : (h + 1) * WIDTH]
+            moved = window[k, :, (h + 1) * WIDTH : (h + 2) * WIDTH]
+            w[:, (3 * h + k) * WIDTH : (3 * h + k + 1) * WIDTH] = jnp.where(odd == 1, moved, even)
+    save(w, w_far)
+    peak[...] = jnp.full_like(peak, masked_value)
+    acc[...] = jnp.zeros_like(acc)
+
+    def project(m):
+        rs = slice(m * rows, (m + 1) * rows)
+        z, _ = standardize(xs[m].astype(f32))
+        normed = (z * gain + shift).astype(bf16)
+        n1[m] = normed
+        proj = (dot_nn(normed, w[...]) + wb_out[...]).astype(bf16)
+        qkv[m] = proj
+        turned = proj.T
+        for h in range(nh):
+            q, k, v = (slice((3 * h + i) * WIDTH, (3 * h + i + 1) * WIDTH) for i in range(3))
+            qt[h * WIDTH : (h + 1) * WIDTH, rs] = turned[q, :] * score_scale
+            ks[h, rs, :] = proj[:, k]
+            vt[h, :WIDTH, rs] = turned[v, :]
+            vt[h, WIDTH:, rs] = jnp.ones((ONES, rows), bf16)
+
+    def attend(start, stop, cs):
+        @pl.loop(start, stop)
+        def _(m):
+            rs = pl.ds(pl.multiple_of(m * rows, rows), rows)
+            for h in range(nh):
+                s = dot_nn(ks[h, rs, :], qt[h * WIDTH : (h + 1) * WIDTH, cs])
+                old = peak[h : h + 1, cs]
+                new = jnp.maximum(old, jnp.max(s, axis=0, keepdims=True))
+                p = jnp.exp(s - new)
+                peak[h : h + 1, cs] = new
+                acc[h, :, cs] = acc[h, :, cs] * jnp.exp(old - new) + dot_nn(vt[h, :, rs], p.astype(bf16))
+
+    early, late = slice(0, length // 2), slice(length // 2, length)
+    project(0)
+    near_0.wait()
+    project(1)
+    attend(0, blocks // 2, early)
+    far_0.wait()
+    relay_0 = copy(4, xs.at[2], xs.at[3], to_core)
+    relay_0.start()
+    project(2)
+    relay_0.wait()
+    project(3)
+    save(n1, n1_far)
+    save(qkv, qkv_far)
+    attend(0, blocks // 2, late)
+    attend(blocks // 2, blocks, slice(0, length))
+    lse[...] = jnp.zeros_like(lse)
+    for h in range(nh):
+        sl = slice(h * WIDTH, (h + 1) * WIDTH)
+        total = acc[h, WIDTH : WIDTH + 1, :]
+        lse[h : h + 1, :] = peak[h : h + 1, :] + jnp.log(total)
+        done = acc[h, :WIDTH, :] / total
+        acc[h, :WIDTH, :] = done
+        save(acc.at[h, :WIDTH, :], full_far.at[sl, :])
+        for m in range(blocks):
+            outs[m, sl, :] = done[:, m * rows : (m + 1) * rows].astype(bf16)
+    save(lse, lse_far)
+    for m in range(blocks):
+        save(outs.at[m], out_far[m])
+    far_1.wait()
+    relay_1 = copy(5, xn.at[2], xn.at[3], to_core)
+    relay_1.start()
+    near_1.wait()
+    save(xn.at[1], next_far[0])
+    save(xn.at[2], next_far[1])
+    relay_1.wait()
+    save(xn.at[3], next_far[2])
+    for item in saves:
+        item.wait()
+
+
+def first_image(x0, x1, qkv_weight, vectors, nh, blocks):
+    rows, d = x0.shape
+    length, hw = rows * blocks, nh * WIDTH
+    vm, far = pl.BlockSpec(memory_space=pltpu.VMEM), pl.BlockSpec(memory_space=pl.ANY)
+    copies = 6
+    return pl.pallas_call(
+        partial(first_kernel, blocks, nh, rows),
+        name="first",
+        in_specs=[far, far, far] + [vm] * len(vectors),
+        out_specs=[far] * (4 + blocks) + [far, vm] + [far] * 3,
+        out_shape=[
+            jax.ShapeDtypeStruct((blocks, rows, d), bf16),
+            jax.ShapeDtypeStruct((blocks, rows, 3 * hw), bf16),
+            jax.ShapeDtypeStruct((hw, length), f32),
+            jax.ShapeDtypeStruct((8, length), f32),
+        ]
+        + [jax.ShapeDtypeStruct((hw, rows), bf16)] * blocks
+        + [jax.ShapeDtypeStruct((d, 3 * hw), bf16), jax.ShapeDtypeStruct((1, 3 * hw), f32)]
+        + [jax.ShapeDtypeStruct((rows, d), bf16)] * 3,
+        scratch_shapes=[
+            pltpu.VMEM((blocks, rows, d), bf16),
+            pltpu.VMEM((blocks, rows, d), bf16),
+            pltpu.VMEM((3, d, 256), bf16),
+            pltpu.VMEM((d, 3 * hw), bf16),
+            pltpu.VMEM((blocks, rows, d), bf16),
+            pltpu.VMEM((blocks, rows, 3 * hw), bf16),
+            pltpu.VMEM((blocks, hw, rows), bf16),
+            pltpu.VMEM((8, length), f32),
+            pltpu.VMEM((hw, length), bf16),
+            pltpu.VMEM((nh, length, WIDTH), bf16),
+            pltpu.VMEM((nh, WIDTH + ONES, length), bf16),
+            pltpu.VMEM((8, length), f32),
+            pltpu.VMEM((nh, WIDTH + ONES, length), f32),
+            pltpu.SemaphoreType.DMA((copies,)),
+            pltpu.SemaphoreType.DMA((copies,)),
+            pltpu.SemaphoreType.DMA((5,)),
+            pltpu.SemaphoreType.DMA((3 + nh + 1 + blocks + 3,)),
+        ],
+        compiler_params=params(collective_id=3, has_side_effects=True),
+        cost_estimate=pl.CostEstimate(
+            flops=2 * length * d * 3 * hw + 8 * length * length * hw, bytes_accessed=8_000_000, transcendentals=0
+        ),
+    )(x0, x1, qkv_weight, *vectors)
+
+
+def forward_kernel(blocks, nh, rows, image, moved, counts, *refs):
     xs = refs[:blocks]
     vec, w, wb = refs[blocks : blocks + 3]
-    n1, qkv, full, lse = refs[blocks + 3 : blocks + 7]
-    outs = refs[blocks + 7 : 2 * blocks + 7]
-    qt, ks, vt, peak, acc = refs[2 * blocks + 7 :]
+    refs = refs[blocks + 3 :]
+    if moved:
+        cot, refs = refs[0], refs[1:]
+    n1, qkv, full, lse = refs[:4]
+    outs, refs = refs[4 : blocks + 4], refs[blocks + 4 :]
+    if moved:
+        cot_out, held, load_sem, save_sem = refs[0], *refs[-3:]
+        refs = refs[1:-3]
+        loads = [pltpu.make_async_copy(cot.at[place(counts, k)], held.at[k], load_sem.at[k]) for k in range(moved)]
+        saves = [
+            pltpu.make_async_copy(held.at[k], cot_out.at[k * rows : (k + 1) * rows, :], save_sem.at[k]) for k in range(moved)
+        ]
+        for load in loads:
+            load.start()
+    qt, ks, vt, peak, acc = refs
     hw = nh * WIDTH
     count, me = counts[place(counts, image)], lax.axis_index("blk")
     gain, shift = vec[0:1, :], vec[1:2, :]
@@ -95,6 +322,10 @@
                 part = dot_nn(vt[h, :, rs], p.astype(bf16))
                 acc[h] = acc[h] * jnp.exp(old - new) + part
 
+    if moved:
+        for load, item in zip(loads, saves):
+            load.wait()
+            item.start()
     lse[...] = jnp.zeros_like(lse)
     for h in range(nh):
         sl = slice(h * WIDTH, (h + 1) * WIDTH)
@@ -104,37 +335,45 @@
         full[sl, :] = done
         for m in range(blocks):
             outs[m][sl, :] = done[:, m * rows : (m + 1) * rows].astype(bf16)
-
-
-def forward_image(counts, image, xs, vec, w, wb, nh):
+    if moved:
+        for item in saves:
+            item.wait()
+
+
+def forward_image(counts, image, xs, vec, w, wb, nh, cot=None):
     blocks = len(xs)
     rows, d = xs[0].shape
     length, hw = rows * blocks, nh * WIDTH
-    vm = pl.BlockSpec(memory_space=pltpu.VMEM)
+    vm, far = pl.BlockSpec(memory_space=pltpu.VMEM), pl.BlockSpec(memory_space=pl.ANY)
+    extra = [] if cot is None else [cot]
+    moved = 0 if cot is None else cot.shape[0]
     return pl.pallas_call(
-        partial(forward_kernel, blocks, nh, rows, image),
+        partial(forward_kernel, blocks, nh, rows, image, moved),
         name="attend_forward",
-        in_specs=[pl.BlockSpec(memory_space=pltpu.SMEM)] + [vm] * (blocks + 3),
-        out_specs=[vm] * (4 + blocks),
+        in_specs=[pl.BlockSpec(memory_space=pltpu.SMEM)] + [vm] * (blocks + 3) + [far] * len(extra),
+        out_specs=[vm] * (4 + blocks) + [far] * len(extra),
         out_shape=[
             jax.ShapeDtypeStruct((blocks, rows, d), bf16),
             jax.ShapeDtypeStruct((blocks, rows, 3 * hw), bf16),
             jax.ShapeDtypeStruct((hw, length), f32),
             jax.ShapeDtypeStruct((8, length), f32),
         ]
-        + [jax.ShapeDtypeStruct((hw, rows), bf16)] * blocks,
+        + [jax.ShapeDtypeStruct((hw, rows), bf16)] * blocks
+        + [jax.ShapeDtypeStruct((moved * rows, d), bf16)] * len(extra),
         scratch_shapes=[
             pltpu.VMEM((hw, length), bf16),
             pltpu.VMEM((nh, length, WIDTH), bf16),
             pltpu.VMEM((nh, WIDTH + ONES, length), bf16),
             pltpu.VMEM((8, length), f32),
             pltpu.VMEM((nh, WIDTH + ONES, length), f32),
-        ],
+        ]
+        + [pltpu.VMEM((moved, rows, d), bf16) for _ in extra]
+        + [pltpu.SemaphoreType.DMA((moved,)) for _ in 2 * extra],
         compiler_params=params(),
         cost_estimate=pl.CostEstimate(
             flops=2 * length * d * 3 * hw + 8 * length * length * hw, bytes_accessed=8_000_000, transcendentals=0
         ),
-    )(counts, *xs, vec, w, wb)
+    )(counts, *xs, vec, w, wb, *extra)
 
 
 def backward_kernel(blocks, nh, rows, image, at, first, counts, *refs):
@@ -1183,52 +1422,68 @@
         hw = nh * WIDTH
         total = images * rows
         me = places.blk
-        vec = jnp.stack(
-            [norm1_gain, norm1_bias, norm2_gain, norm2_bias, scale1, scale2, out_bias, fc2_bias]
-        ).astype(f32)
+        rows_in = [norm1_gain, norm1_bias, norm2_gain, norm2_bias, scale1, scale2, out_bias, fc2_bias]
+        n = places.n_img * blocks
+        share = d // n
+        fast = share % 8 == 0 and (places.img_bits, places.blk_bits, images) == (3, 2, 3)
+
         def own_heads(value):
             pieces = [lax.dynamic_slice_in_dim(value, k * d + me * hw, hw, value.ndim - 1) for k in range(3)]
             pieces = [v.reshape(v.shape[:-1] + (nh, 1, WIDTH)) for v in pieces]
             return jnp.concatenate(pieces, axis=-2).reshape(value.shape[:-1] + (3 * hw,))
 
-        w = own_heads(qkv_weight)
-        wb = own_heads(jnp.concatenate([q_bias, jnp.zeros((d,), bf16), v_bias])).astype(f32)[None, :]
-
         def after(values, *done):
             return lax.optimization_barrier((list(values), done))[0]
 
         def swap_blk(value, m):
             return lax.ppermute(value, "blk", [(b, b ^ m) for b in range(blocks)])
 
-        lead = jnp.argmax(counts).astype(jnp.int32)
-
-        def turned(value):
-            return [
-                lax.dynamic_index_in_dim(value, lax.rem(lead + k, images), 0, keepdims=False) for k in range(images)
+        vectors = lambda items: jnp.stack(items).astype(f32)
+        if fast:
+            mine = turn(counts, tokens)
+            x0, x1, x2 = mine
+            n1, qkv, full, lse, *outs = first_image(
+                x0, x1, qkv_weight, (norm1_gain, norm1_bias, q_bias, v_bias), nh, blocks
+            )
+            outs, (w, wb, *given) = outs[:blocks], outs[blocks:]
+            saved = [(n1, qkv, full, lse)]
+            vec = vectors(after(rows_in, lse))
+            far_2, near_2, first_lse = lax.optimization_barrier((x2, x2, lse))
+            far_2, near_2 = swap_blk(far_2, 2), swap_blk(near_2, 1)
+            atts = [outs[0]] + [swap_blk(outs[m], m) for m in range(1, blocks)]
+            n1, qkv, full, lse, *outs, cot = forward_image(counts, 1, [x1, *given], vec, w, wb, nh, cotangent)
+            saved.append((n1, qkv, full, lse))
+            atts += [outs[0]] + [swap_blk(outs[m], m) for m in range(1, blocks)]
+            far_2 = after([far_2], lse)[0]
+            n1, qkv, full, lse, *outs = forward_image(counts, 2, [x2, near_2, far_2, swap_blk(far_2, 1)], vec, w, wb, nh)
+            saved.append((n1, qkv, full, lse))
+            atts += outs
+        else:
+            vec = vectors(rows_in)
+            order = jnp.argsort(-counts, stable=True)
+            turned = lambda value: [
+                lax.dynamic_index_in_dim(value, order[k], 0, keepdims=False) for k in range(images)
             ]
-
-        mine = turned(tokens)
-        saved, atts = [], []
-        for i in range(images):
-            found = {0: mine[i]}
-            for k in reversed(range(places.blk_bits)):
-                if k == 0:
-                    found = dict(zip(found, after(list(found.values()), *((w, wb, vec) if i == 0 else saved[-1][3:]))))
-                found.update({m | 1 << k: swap_blk(v, 1 << k) for m, v in found.items()})
-            xs = [found[m] for m in range(blocks)]
-            n1, qkv, full, lse, *outs = forward_image(counts, i, xs, vec, w, wb, nh)
-            saved.append((n1, qkv, full, lse))
-            atts.extend([outs[0]] + [swap_blk(outs[m], m) if i < images - 1 else outs[m] for m in range(1, blocks)])
-        n = places.n_img * blocks
-        share = d // n
+            mine, cot = turned(tokens), jnp.concatenate(turned(cotangent))
+            w = own_heads(qkv_weight)
+            wb = own_heads(jnp.concatenate([q_bias, jnp.zeros((d,), bf16), v_bias])).astype(f32)[None, :]
+            saved, atts = [], []
+            for i in range(images):
+                found = {0: mine[i]}
+                for k in reversed(range(places.blk_bits)):
+                    found.update({m | 1 << k: swap_blk(v, 1 << k) for m, v in found.items()})
+                xs = [found[m] for m in range(blocks)]
+                n1, qkv, full, lse, *outs = forward_image(counts, i, xs, vec, w, wb, nh)
+                saved.append((n1, qkv, full, lse))
+                atts.extend([outs[0]] + [swap_blk(outs[m], m) if i < images - 1 else outs[m] for m in range(1, blocks)])
         ff = fc1_weight.shape[1]
         half = d // 2
         y_bit, z_bit = 0, 1
-        bits = (z_bit, y_bit) if share % 8 == 0 and (places.img_bits, places.blk_bits, images) == (3, 2, 3) else ()
+        bits = (z_bit, y_bit) if fast else ()
         out, gmid, gb1, sums, so, g1, g2, *gats = middle_layers(
             atts,
             mine,
-            jnp.concatenate(turned(cotangent)),
+            cot,
             vec,
             out_weight,
             fc1_bias.astype(f32)[None, :],
@@ -1312,8 +1567,8 @@
 
             def returned(value):
                 value = value.reshape(tokens.shape)
-                at = [lax.rem(i - lead + images, images) for i in range(images)]
-                return jnp.stack([lax.dynamic_index_in_dim(value, k, 0, keepdims=False) for k in at])
+                at = jnp.argsort(order)
+                return jnp.stack([lax.dynamic_index_in_dim(value, at[i], 0, keepdims=False) for i in range(images)])
 
             output = returned(out)
             grad_tokens = returned(finish(jnp.stack(mine), gmid, vec[0:1, :], terms))

time: 211 us -> 195 us (0.924)
  waiting for transfers between devices: 15.3 us -> 3.29 us
  local copies, waits for them, and re-layouts: 9.61 us -> 1.91 us
  Pallas kernels: 163 us -> 168 us
  other arithmetic: 3.93 us -> 1.36 us
    pallas_call x1, Pallas kernels: 61.6 us -> 54.1 us  [middle_layers(): pl.pallas_call(partial(middle_kernel, blocks, images, steps, bits), name=...]
    pallas_call x3 -> x4, Pallas kernels: 40 us -> 47.4 us  [the longest x1 25.5 us: first_image(): pl.pallas_call(partial(first_kernel, blocks, nh, rows), name='first', in_...]
    ppermute x19 -> x13, waiting for transfers between devices: 6.09 us -> 0.03 us  [swap_blk(): return lax.ppermute(value, 'blk', [(b, b ^ m) for b in range(blocks)])]
    ppermute x4, starting transfers between devices: 3.3 us -> 9.35 us  [swap(): return lax.ppermute(value, axis, [(i, i ^ 1 << k) for i in range(n)])]
    ppermute x4, waiting for transfers between devices: 9.18 us -> 3.26 us  [swap(): return lax.ppermute(value, axis, [(i, i ^ 1 << k) for i in range(n)])]
    ppermute x19 -> x13, starting transfers between devices: 12.6 us -> 7.33 us  [swap_blk(): return lax.ppermute(value, 'blk', [(b, b ^ m) for b in range(blocks)])]
    pallas_call x2, Pallas kernels: 19.9 us -> 24 us  [backward_image(): pl.pallas_call(partial(backward_kernel, blocks, nh, rows, image, at, not...]
  transfers between devices with their start and end apart: 23 -> 17, of which waited for: 6 -> 2; matrix products, arithmetic and copies ran while one was open for 4% -> 1% of each run, Pallas kernels for 28% -> 22%
where the time goes in v2:
time: 195 us; the launch traced here: 193 us
  Pallas kernels  168 us (86%)
  starting transfers between devices  16.7 us (9%)
  waiting for transfers between devices  3.29 us (2%)
    pallas_call x1, Pallas kernels, middle_layers(): pl.pallas_call(partial(middle_kernel, blocks, images, steps, bits), name=...  54.1 us
    pallas_call x1, Pallas kernels, last_image(): pl.pallas_call(partial(last_kernel, blocks, nh, rows, share, at_piece), n...  38.8 us
    pallas_call x1, Pallas kernels, first_image(): pl.pallas_call(partial(first_kernel, blocks, nh, rows), name='first', in_...  25.5 us
    pallas_call x2, Pallas kernels, backward_image(): pl.pallas_call(partial(backward_kernel, blocks, nh, rows, image, at, not...  24 us
    pallas_call x2, Pallas kernels, forward_image(): pl.pallas_call(partial(forward_kernel, blocks, nh, rows, image, moved), n...  19.1 us
    ppermute x4, starting transfers between devices, swap(): return lax.ppermute(value, axis, [(i, i ^ 1 << k) for i in range(n)])  9.35 us
    ppermute x13, starting transfers between devices, swap_blk(): return lax.ppermute(value, 'blk', [(b, b ^ m) for b in range(blocks)])  7.33 us
  transfers between devices with their start and end apart: 17, of which 2 were waited for; matrix products, arithmetic and copies ran while one was open for 1% of the time, Pallas kernels for 22%

profile of v2, /device:TPU:0, one launch (start us, length us, event | category | flops | bytes accessed | tf_op | source)
XLA Modules:
  0.0 192.8 jit_solution(13922078427444681054)
XLA Ops:
  0.7 2.7 %turn.1 = (bf16[256,768]{1,0:T(8,128)(2,1)}, bf16[256,768]{1,0:T(8,128)(2,1)}, bf16[256,768]{1,0:T(8,128)(2,1)}) custom-call(s32[3]{0:T(128)} %counts.11, bf16[3,256,768]{2,1,0:T(8,128)(2,1)} %tokens.1), custom_call_target="tpu_custom_call" | custom-call | tf_op jit(solution)/shard_map/turn/pallas_call | solution.py:77
  3.5 25.5 %first.1 = (bf16[4,256,768]{2,1,0:T(8,128)(2,1)}, bf16[4,256,576]{2,1,0:T(8,128)(2,1)}, f32[192,1024]{1,0:T(8,128)}, f32[8,1024]{1,0:T(8,128)}, bf16[192,256]{1,...) custom-call(bf16[256,768]{1,0:T(8,128)(2,1)} %get-tuple-element.117., ...), custom_call_target="tpu_custom_call" | custom-call | flops 2516582400 | bytes 8000000 | tf_op jit(solution)/shard_map/first/pallas_call | solution.py:230
  29.1 1.1 collective-permute-start.7
  30.4 0.6 convert_element_type.32.refs_4_.refs_16_.refs_20_
  31.0 11.6 %attend_forward.2 = (bf16[4,256,768]{2,1,0:T(8,128)(2,1)}, bf16[4,256,576]{2,1,0:T(8,128)(2,1)}, f32[192,1024]{1,0:T(8,128)}, f32[8,1024]{1,0:T(8,128)}, bf16[19...) custom-call(s32[3]{0:T(128)} %counts.11, ...), custom_call_target="tpu_custom_call" | custom-call | flops 2516582400 | bytes 8000000 | tf_op jit(solution)/shard_map/attend_forward/pallas_call | solution.py:350
  42.7 0.5 collective-permute-start.8
  43.2 0.1 collective-permute-start
  43.3 1.0 collective-permute-start.1
  44.3 0.8 collective-permute-start.2
  45.1 0.6 broadcast_in_dim.7
  45.7 0.4 collective-permute-start.3
  46.1 1.0 collective-permute-start.4
  47.1 0.5 collective-permute-start.5
  47.6 0.2 copy-done.17
  47.8 7.4 %attend_forward.3 = (bf16[4,256,768]{2,1,0:T(8,128)(2,1)}, bf16[4,256,576]{2,1,0:T(8,128)(2,1)}, f32[192,1024]{1,0:T(8,128)}, f32[8,1024]{1,0:T(8,128)}, bf16[19...) custom-call(s32[3]{0:T(128)} %counts.11, ...), custom_call_target="tpu_custom_call" | custom-call | flops 2516582400 | bytes 8000000 | tf_op jit(solution)/shard_map/attend_forward/pallas_call | solution.py:350
  55.4 0.5 copy-done.26
  56.0 54.1 %middle_layers.1 = (bf16[768,768]{1,0:T(8,128)(2,1)}, f32[768,768]{1,0:T(8,128)}, f32[3072,128]{1,0:T(8,128)}, f32[8,768]{1,0:T(8,128)}, bf16[768,384]{1,0:T(8,1...) custom-call(bf16[192,256]{1,0:T(8,128)(2,1)} %get-tuple-element.119., ...), custom_call_target="tpu_custom_call" | custom-call | flops 24461180928 | bytes 30000000 | tf_op jit(solution)/shard_map/middle_layers/pallas_call | solution.py:851
  110.2 1.4 collective-permute-start.12
  111.6 0.9 collective-permute-start.10
  112.5 0.9 collective-permute-start.11
  113.4 0.7 collective-permute-start.13
  114.2 14.1 %attend_backward.2 = (f32[768,640]{1,0:T(8,128)}, f32[8,768]{1,0:T(8,128)}, bf16[2,256,768]{2,1,0:T(8,128)(2,1)}, bf16[2,256,768]{2,1,0:T(8,128)(2,1)}) custom-call(s32[3]{0:T(128)} %counts.11, bf16[1,192,256]{2,1,0:T(8,128)(2,1)} %get-tuple-element.155.refs_0_, bf16[1,192,256]{2,1,0:T(8,128)(2,1)} %get-tuple-element.156.refs_1_, ...), custom_call_target="tpu_custom_call" | custom-call | flops 5838471168 | bytes 12000000 | tf_op jit(solution)/shard_map/attend_backward/pallas_call | solution.py:490
  128.4 0.1 fusion
  128.5 0.7 collective-permute-done.13.refs_12_
  129.2 6.2 %collective-permute-start.15 = (bf16[96,1536]{1,0:T(8,128)(2,1)S(1)}, bf16[96,1536]{1,0:T(8,128)(2,1)S(1)}, u32[]{:S(2)}, u32[]{:S(2)}) collective-permute-start(bf16[96,1536]{1,0:T(8,128)(2,1)S(1)} %fusion.1), channel_id=1, source_target_pairs={{0,16},{4,20},{8,24},{12,28},{16,0},{20,4},{24,8},{28,12},{1,17},{... | collective-permute-start | bytes 884744 | tf_op jit(solution)/shard_map/ppermute | solution.py:1353
  135.4 1.1 collective-permute-start.16
  136.5 10.0 %attend_backward.3 = (f32[768,640]{1,0:T(8,128)}, f32[8,768]{1,0:T(8,128)}, bf16[2,256,768]{2,1,0:T(8,128)(2,1)}, bf16[2,256,768]{2,1,0:T(8,128)(2,1)}) custom-call(s32[3]{0:T(128)} %counts.11, bf16[2,192,256]{2,1,0:T(8,128)(2,1)} %get-tuple-element.164.refs_0_.refs_3_, bf16[2,192,256]{2,1,0:T(8,128)(2,1)} %copy-done.20, bf16[2,192,256]{2,1,0:T(8,128)(2,1)} %copy-done.21, ...), custom_call_target="tpu_custom_call" | custom-call | flops 5838471168 | bytes 12000000 | tf_op jit(solution)/shard_map/attend_backward/pallas_call | solution.py:490
  146.5 2.6 %collective-permute-done.15.refs_13_ = bf16[96,1536]{1,0:T(8,128)(2,1)S(1)} collective-permute-done((bf16[96,1536]{1,0:T(8,128)(2,1)S(1)}, bf16[96,1536]{1,0:T(8,128)(2,1)S(1)}, u32[]{:S(2)}, u32[]{:S(2)}) %collective-permute-start.15) | collective-permute-done | bytes 294944 | tf_op jit(solution)/shard_map/ppermute | solution.py:1353
  149.1 0.7 copy-done.18
  149.8 0.1 copy-done.19
  149.9 38.8 %last.1 = (bf16[3,256,768]{2,1,0:T(8,128)(2,1)}, f32[4,24,1024]{2,1,0:T(8,128)}, f32[2,24,1536]{2,1,0:T(8,128)}, f32[2,96,384]{2,1,0:T(8,128)}) custom-call(bf16[2,256,768]{2,1,0:T(8,128)(2,1)} %get-tuple-element.180.refs_0_, bf16[2,256,768]{2,1,0:T(8,128)(2,1)} %get-tuple-element.181.refs_1_, bf16[2,256,768]{2,1,0:T(8,128)(2,1)} %copy-done.13, ...), custom_call_target="tpu_custom_call" | custom-call | flops 30000001024 | bytes 20000000 | tf_op jit(solution)/shard_map/last/pallas_call | solution.py:1209
  188.7 3.8 %layout.1 = (bf16[3,256,768]{2,1,0:T(8,128)(2,1)}, bf16[3,256,768]{2,1,0:T(8,128)(2,1)}, f32[24,2304]{1,0:T(8,128)}, f32[24,768]{1,0:T(8,128)}, f32[24,3072]{1,0...) custom-call(s32[3]{0:T(128)} %counts.11, ...), custom_call_target="tpu_custom_call" | custom-call | tf_op jit(solution)/shard_map/layout/pallas_call | solution.py:1297
  (88 shorter events, 0.5 us)
Async XLA Ops:
  3.4 25.6 %copy-start.14 = (bf16[256,768]{1,0:T(8,128)(2,1)S(1)}, bf16[256,768]{1,0:T(8,128)(2,1)}, u32[]{:S(2)}) copy-start(bf16[256,768]{1,0:T(8,128)(2,1)} %get-tuple-element.143.refs_0_.refs_14_.refs_28_) | copy-start | bytes 1179652
  3.4 26.8 %copy-start.5 = (bf16[768]{0:T(1024)(128)(2,1)S(1)}, bf16[768]{0:T(1024)(128)(2,1)}, u32[]{:S(2)}) copy-start(bf16[768]{0:T(1024)(128)(2,1)} %refs_3_.1) | copy-start | bytes 4612
  3.4 26.8 %copy-start.6 = (bf16[768]{0:T(1024)(128)(2,1)S(1)}, bf16[768]{0:T(1024)(128)(2,1)}, u32[]{:S(2)}) copy-start(bf16[768]{0:T(1024)(128)(2,1)} %refs_4_.1) | copy-start | bytes 4612
  3.4 26.8 %copy-start.7 = (bf16[768]{0:T(1024)(128)(2,1)S(1)}, bf16[768]{0:T(1024)(128)(2,1)}, u32[]{:S(2)}) copy-start(bf16[768]{0:T(1024)(128)(2,1)} %param.27) | copy-start | bytes 4612
  3.5 26.8 %copy-start.8 = (bf16[768]{0:T(1024)(128)(2,1)S(1)}, bf16[768]{0:T(1024)(128)(2,1)}, u32[]{:S(2)}) copy-start(bf16[768]{0:T(1024)(128)(2,1)} %param.28) | copy-start | bytes 4612
  3.5 26.8 %copy-start.9 = (bf16[768]{0:T(1024)(128)(2,1)S(1)}, bf16[768]{0:T(1024)(128)(2,1)}, u32[]{:S(2)}) copy-start(bf16[768]{0:T(1024)(128)(2,1)} %param.33) | copy-start | bytes 4612
  3.5 26.8 %copy-start.10 = (bf16[768]{0:T(1024)(128)(2,1)S(1)}, bf16[768]{0:T(1024)(128)(2,1)}, u32[]{:S(2)}) copy-start(bf16[768]{0:T(1024)(128)(2,1)} %param.34) | copy-start | bytes 4612
  3.5 26.8 %copy-start.11 = (bf16[768]{0:T(1024)(128)(2,1)S(1)}, bf16[768]{0:T(1024)(128)(2,1)}, u32[]{:S(2)}) copy-start(bf16[768]{0:T(1024)(128)(2,1)} %param.24) | copy-start | bytes 4612
  3.5 26.8 %copy-start.12 = (bf16[768]{0:T(1024)(128)(2,1)S(1)}, bf16[768]{0:T(1024)(128)(2,1)}, u32[]{:S(2)}) copy-start(bf16[768]{0:T(1024)(128)(2,1)} %param.32) | copy-start | bytes 4612
  29.1 13.6 %collective-permute-start.7 = (bf16[256,768]{1,0:T(8,128)(2,1)S(1)}, bf16[256,768]{1,0:T(8,128)(2,1)S(1)}, u32[]{:S(2)}, u32[]{:S(2)}) collective-permute-start(bf16[256,768]{1,0:T(8,128)(2,1)S(1)} %copy-done.14), channel_id=1, source_target_pairs={{0,2},{1,3},{2,0},{3,1},{4,6},{5,7},{6,4},{7,5},{8,10},{9,11},{10,... | collective-permute-start | bytes 1179656 | tf_op jit(solution)/shard_map/ppermute | solution.py:1439
  30.2 15.9 %collective-permute-start.6 = (bf16[256,768]{1,0:T(8,128)(2,1)S(1)}, bf16[256,768]{1,0:T(8,128)(2,1)S(1)}, u32[]{:S(2)}, u32[]{:S(2)}) collective-permute-start(bf16[256,768]{1,0:T(8,128)(2,1)S(1)} %copy-done.14), channel_id=1, source_target_pairs={{0,1},{1,0},{2,3},{3,2},{4,5},{5,4},{6,7},{7,6},{8,9},{9,8},{10,11... | collective-permute-start | bytes 1179656 | tf_op jit(solution)/shard_map/ppermute | solution.py:1439
  31.0 13.3 %copy-start.23 = (bf16[192,256]{1,0:T(8,128)(2,1)S(1)}, bf16[192,256]{1,0:T(8,128)(2,1)}, u32[]{:S(2)}) copy-start(bf16[192,256]{1,0:T(8,128)(2,1)} %get-tuple-element.122) | copy-start | bytes 294916
  31.0 14.1 %copy-start.4 = (bf16[3072]{0:T(1024)(128)(2,1)S(1)}, bf16[3072]{0:T(1024)(128)(2,1)}, u32[]{:S(2)}) copy-start(bf16[3072]{0:T(1024)(128)(2,1)} %param.30) | copy-start | bytes 18436
  42.7 4.4 %collective-permute-start.8 = (bf16[256,768]{1,0:T(8,128)(2,1)S(1)}, bf16[256,768]{1,0:T(8,128)(2,1)S(1)}, u32[]{:S(2)}, u32[]{:S(2)}) collective-permute-start(bf16[256,768]{1,0:T(8,128)(2,1)S(1)} %collective-permute-done.7.refs_2_), channel_id=1, source_target_pairs={{0,1},{1,0},{2,3},{3,2},{4,5},{5,4},{6,7},{7,6},{8,9},{9,8},{10,11... | collective-permute-start | bytes 1179656 | tf_op jit(solution)/shard_map/ppermute | solution.py:1439
  43.2 2.5 %collective-permute-start = (bf16[192,256]{1,0:T(8,128)(2,1)S(1)}, bf16[192,256]{1,0:T(8,128)(2,1)S(1)}, u32[]{:S(2)}, u32[]{:S(2)}) collective-permute-start(bf16[192,256]{1,0:T(8,128)(2,1)S(1)} %copy-done.29), channel_id=1, source_target_pairs={{0,1},{1,0},{2,3},{3,2},{4,5},{5,4},{6,7},{7,6},{8,9},{9,8},{10,11... | collective-permute-start | bytes 294920 | tf_op jit(solution)/shard_map/ppermute | solution.py:1439
  43.3 11.9 %collective-permute-start.1 = (bf16[192,256]{1,0:T(8,128)(2,1)S(1)}, bf16[192,256]{1,0:T(8,128)(2,1)S(1)}, u32[]{:S(2)}, u32[]{:S(2)}) collective-permute-start(bf16[192,256]{1,0:T(8,128)(2,1)S(1)} %copy-done.24), channel_id=1, source_target_pairs={{0,2},{1,3},{2,0},{3,1},{4,6},{5,7},{6,4},{7,5},{8,10},{9,11},{10,... | collective-permute-start | bytes 294920 | tf_op jit(solution)/shard_map/ppermute | solution.py:1439
  44.3 11.0 %collective-permute-start.2 = (bf16[192,256]{1,0:T(8,128)(2,1)S(1)}, bf16[192,256]{1,0:T(8,128)(2,1)S(1)}, u32[]{:S(2)}, u32[]{:S(2)}) collective-permute-start(bf16[192,256]{1,0:T(8,128)(2,1)S(1)} %copy-done.23), channel_id=1, source_target_pairs={{0,3},{1,2},{2,1},{3,0},{4,7},{5,6},{6,5},{7,4},{8,11},{9,10},{10,... | collective-permute-start | bytes 294920 | tf_op jit(solution)/shard_map/ppermute | solution.py:1439
  45.7 9.6 %collective-permute-start.3 = (bf16[192,256]{1,0:T(8,128)(2,1)}, bf16[192,256]{1,0:T(8,128)(2,1)S(1)}, u32[]{:S(2)}, u32[]{:S(2)}) collective-permute-start(bf16[192,256]{1,0:T(8,128)(2,1)} %get-tuple-element.138), channel_id=1, source_target_pairs={{0,1},{1,0},{2,3},{3,2},{4,5},{5,4},{6,7},{7,6},{8,9},{9,8},{10,11... | collective-permute-start | bytes 294920 | tf_op jit(solution)/shard_map/ppermute | solution.py:1439
  46.1 9.3 %collective-permute-start.4 = (bf16[192,256]{1,0:T(8,128)(2,1)}, bf16[192,256]{1,0:T(8,128)(2,1)S(1)}, u32[]{:S(2)}, u32[]{:S(2)}) collective-permute-start(bf16[192,256]{1,0:T(8,128)(2,1)} %get-tuple-element.139), channel_id=1, source_target_pairs={{0,2},{1,3},{2,0},{3,1},{4,6},{5,7},{6,4},{7,5},{8,10},{9,11},{10,... | collective-permute-start | bytes 294920 | tf_op jit(solution)/shard_map/ppermute | solution.py:1439
  47.1 8.3 %collective-permute-start.5 = (bf16[192,256]{1,0:T(8,128)(2,1)}, bf16[192,256]{1,0:T(8,128)(2,1)S(1)}, u32[]{:S(2)}, u32[]{:S(2)}) collective-permute-start(bf16[192,256]{1,0:T(8,128)(2,1)} %get-tuple-element.140), channel_id=1, source_target_pairs={{0,3},{1,2},{2,1},{3,0},{4,7},{5,6},{6,5},{7,4},{8,11},{9,10},{10,... | collective-permute-start | bytes 294920 | tf_op jit(solution)/shard_map/ppermute | solution.py:1439
  110.2 18.2 %collective-permute-start.12 = (bf16[2,2,192,384]{3,2,1,0:T(8,128)(2,1)}, bf16[2,2,192,384]{3,2,1,0:T(8,128)(2,1)S(1)}, u32[]{:S(2)}, u32[]{:S(2)}) collective-permute-start(bf16[2,2,192,384]{3,2,1,0:T(8,128)(2,1)} %get-tuple-element.173), channel_id=1, source_target_pairs={{0,8},{4,12},{8,0},{12,4},{16,24},{20,28},{24,16},{28,20},{1,9},{5... | collective-permute-start | bytes 1769480 | tf_op jit(solution)/shard_map/ppermute | solution.py:1353
  111.6 16.7 %collective-permute-start.9 = (bf16[2,192,256]{2,1,0:T(8,128)(2,1)}, bf16[2,192,256]{2,1,0:T(8,128)(2,1)S(1)}, u32[]{:S(2)}, u32[]{:S(2)}) collective-permute-start(bf16[2,192,256]{2,1,0:T(8,128)(2,1)} %get-tuple-element.152), channel_id=1, source_target_pairs={{0,1},{1,0},{2,3},{3,2},{4,5},{5,4},{6,7},{7,6},{8,9},{9,8},{10,11... | collective-permute-start | bytes 589832 | tf_op jit(solution)/shard_map/ppermute | solution.py:1439
  111.6 16.8 %collective-permute-start.10 = (bf16[2,192,256]{2,1,0:T(8,128)(2,1)}, bf16[2,192,256]{2,1,0:T(8,128)(2,1)S(1)}, u32[]{:S(2)}, u32[]{:S(2)}) collective-permute-start(bf16[2,192,256]{2,1,0:T(8,128)(2,1)} %get-tuple-element.153), channel_id=1, source_target_pairs={{0,2},{1,3},{2,0},{3,1},{4,6},{5,7},{6,4},{7,5},{8,10},{9,11},{10,... | collective-permute-start | bytes 589832 | tf_op jit(solution)/shard_map/ppermute | solution.py:1439
  112.5 15.9 %collective-permute-start.11 = (bf16[2,192,256]{2,1,0:T(8,128)(2,1)}, bf16[2,192,256]{2,1,0:T(8,128)(2,1)S(1)}, u32[]{:S(2)}, u32[]{:S(2)}) collective-permute-start(bf16[2,192,256]{2,1,0:T(8,128)(2,1)} %get-tuple-element.154), channel_id=1, source_target_pairs={{0,3},{1,2},{2,1},{3,0},{4,7},{5,6},{6,5},{7,4},{8,11},{9,10},{10,... | collective-permute-start | bytes 589832 | tf_op jit(solution)/shard_map/ppermute | solution.py:1439
  113.4 15.7 %collective-permute-start.13 = (bf16[2,96,1536]{2,1,0:T(8,128)(2,1)}, bf16[2,96,1536]{2,1,0:T(8,128)(2,1)S(1)}, u32[]{:S(2)}, u32[]{:S(2)}) collective-permute-start(bf16[2,96,1536]{2,1,0:T(8,128)(2,1)} %get-tuple-element.176), channel_id=1, source_target_pairs={{0,4},{4,0},{8,12},{12,8},{16,20},{20,16},{24,28},{28,24},{1,5},{5... | collective-permute-start | bytes 1769480 | tf_op jit(solution)/shard_map/ppermute | solution.py:1353
  114.2 14.2 %copy-start.1 = (bf16[2,2,192,384]{3,2,1,0:T(8,128)(2,1)S(1)}, bf16[2,2,192,384]{3,2,1,0:T(8,128)(2,1)}, u32[]{:S(2)}) copy-start(bf16[2,2,192,384]{3,2,1,0:T(8,128)(2,1)} %get-tuple-element.172.refs_22_) | copy-start | bytes 1769476
  114.2 15.0 %copy-start = (bf16[2,96,1536]{2,1,0:T(8,128)(2,1)S(1)}, bf16[2,96,1536]{2,1,0:T(8,128)(2,1)}, u32[]{:S(2)}) copy-start(bf16[2,96,1536]{2,1,0:T(8,128)(2,1)} %get-tuple-element.175.refs_11_) | copy-start | bytes 1769476
  128.2 18.2 %collective-permute-start.14 = (bf16[2,256,768]{2,1,0:T(8,128)(2,1)}, bf16[2,256,768]{2,1,0:T(8,128)(2,1)S(1)}, u32[]{:S(2)}, u32[]{:S(2)}) collective-permute-start(bf16[2,256,768]{2,1,0:T(8,128)(2,1)} %get-tuple-element.182), channel_id=1, source_target_pairs={{0,1},{1,0},{2,3},{3,2},{4,5},{5,4},{6,7},{7,6},{8,9},{9,8},{10,11... | collective-permute-start | bytes 2359304 | tf_op jit(solution)/shard_map/ppermute | solution.py:1439
  128.4 18.1 %copy-start.2 = (bf16[2,2,192,384]{3,2,1,0:T(8,128)(2,1)}, bf16[2,2,192,384]{3,2,1,0:T(8,128)(2,1)S(1)}, u32[]{:S(2)}) copy-start(bf16[2,2,192,384]{3,2,1,0:T(8,128)(2,1)S(1)} %collective-permute-done.12.refs_23_) | copy-start | bytes 1769476
  129.1 17.3 %copy-start.3 = (bf16[2,96,1536]{2,1,0:T(8,128)(2,1)}, bf16[2,96,1536]{2,1,0:T(8,128)(2,1)S(1)}, u32[]{:S(2)}) copy-start(bf16[2,96,1536]{2,1,0:T(8,128)(2,1)S(1)} %collective-permute-done.13.refs_12_) | copy-start | bytes 1769476
  129.2 19.8 %collective-permute-start.15 = (bf16[96,1536]{1,0:T(8,128)(2,1)S(1)}, bf16[96,1536]{1,0:T(8,128)(2,1)S(1)}, u32[]{:S(2)}, u32[]{:S(2)}) collective-permute-start(bf16[96,1536]{1,0:T(8,128)(2,1)S(1)} %fusion.1), channel_id=1, source_target_pairs={{0,16},{4,20},{8,24},{12,28},{16,0},{20,4},{24,8},{28,12},{1,17},{... | collective-permute-start | bytes 884744 | tf_op jit(solution)/shard_map/ppermute | solution.py:1353
  135.4 13.7 %collective-permute-start.16 = (bf16[2,192,384]{2,1,0:T(8,128)(2,1)S(1)}, bf16[2,192,384]{2,1,0:T(8,128)(2,1)S(1)}, u32[]{:S(2)}, u32[]{:S(2)}) collective-permute-start(bf16[2,192,384]{2,1,0:T(8,128)(2,1)S(1)} %fusion), channel_id=1, source_target_pairs={{0,2},{1,3},{2,0},{3,1},{4,6},{5,7},{6,4},{7,5},{8,10},{9,11},{10,... | collective-permute-start | bytes 884744 | tf_op jit(solution)/shard_map/ppermute | solution.py:1353
  (17 other events, 73.1 us)

commit v3 on v2

--- a/solution.py
+++ b/solution.py
@@ -304,14 +304,17 @@
             vt[h, WIDTH:, rs] = jnp.ones((ONES, rows), bf16)
     peak[...] = jnp.full_like(peak, masked_value)
     acc[...] = jnp.zeros_like(acc)
+    if moved:
+        for load, item in zip(loads, saves):
+            load.wait()
+            item.start()
     @pl.loop(0, blocks)
     def _(m):
         valid = count - (me ^ m) * rows
-        rs = pl.ds(pl.multiple_of(m * rows, rows), rows)
-
-        @pl.when(valid > 0)
-        def _():
-            keep = lax.broadcasted_iota(jnp.int32, (rows, 1), 0) < valid
+
+        def work(size):
+            rs = pl.ds(pl.multiple_of(m * rows, rows), size)
+            keep = lax.broadcasted_iota(jnp.int32, (size, 1), 0) < valid
             for h in range(nh):
                 s = dot_nn(ks[h, rs, :], qt[h * WIDTH : (h + 1) * WIDTH, :])
                 s = jnp.where(keep, s, masked_value)
@@ -322,10 +325,9 @@
                 part = dot_nn(vt[h, :, rs], p.astype(bf16))
                 acc[h] = acc[h] * jnp.exp(old - new) + part
 
-    if moved:
-        for load, item in zip(loads, saves):
-            load.wait()
-            item.start()
+        pl.when(valid > rows // 2)(lambda: work(rows))
+        pl.when(jnp.logical_and(valid > 0, valid <= rows // 2))(lambda: work(rows // 2))
+
     lse[...] = jnp.zeros_like(lse)
     for h in range(nh):
         sl = slice(h * WIDTH, (h + 1) * WIDTH)
@@ -376,14 +378,24 @@
     )(counts, *xs, vec, w, wb, *extra)
 
 
-def backward_kernel(blocks, nh, rows, image, at, first, counts, *refs):
+def backward_kernel(blocks, nh, rows, image, at, first, moved, counts, *refs):
     g_far = refs[:blocks]
     n1_far, qkv_far, full_far, lse_far, w_far = refs[blocks : blocks + 5]
     refs = refs[blocks + 5 :]
     if not first:
         dw_far, sums_in = refs[:2]
         refs = refs[2:]
+    if moved:
+        out_far, refs = refs[0], refs[1:]
     dw_out, sums, keep_out, pass_out = refs[:4]
+    if moved:
+        out_turned, refs = refs[4], refs[1:]
+        held, move_in, move_out = refs[-3:]
+        refs = refs[:-3]
+        ins = [
+            pltpu.make_async_copy(out_far.at[k * rows : (k + 1) * rows, :], held.at[k], move_in.at[k]) for k in range(moved)
+        ]
+        turns = [pltpu.make_async_copy(held.at[k], out_turned.at[place(counts, k)], move_out.at[k]) for k in range(moved)]
     gats, n1, qkv, full, lse, w, dw, low, qt, qs, ks, vs, gs, kt, gt, delta, dqt, gall, n1t, load_sem, save_sem = refs[4:]
     hw = nh * WIDTH
     length = rows * blocks
@@ -399,6 +411,9 @@
     soon = [(load(g_far[m].at[at], gats.at[m]), load(qkv_far.at[m], qkv.at[m])) for m in range(blocks)]
     full_load, lse_load = load(full_far, full), load(lse_far, lse)
     late = [load(n1_far, n1), load(w_far, w)] + ([] if first else [load(dw_far, dw)])
+    if moved:
+        for item in ins:
+            item.start()
     saves = []
 
     def save(src, dst):
@@ -434,11 +449,10 @@
     @pl.loop(0, blocks)
     def _(m):
         valid = count - (me ^ m) * rows
-        rs = pl.ds(pl.multiple_of(m * rows, rows), rows)
-
-        @pl.when(valid > 0)
-        def _():
-            keep = lax.broadcasted_iota(jnp.int32, (rows, 1), 0) < valid
+
+        def work(size):
+            rs = pl.ds(pl.multiple_of(m * rows, rows), size)
+            keep = lax.broadcasted_iota(jnp.int32, (size, 1), 0) < valid
             for h in range(nh):
                 sl = slice(h * WIDTH, (h + 1) * WIDTH)
                 s = dot_nn(ks[h, rs, :], qt[sl, :])
@@ -450,12 +464,23 @@
                 gall[rs, (3 * h + 2) * WIDTH : (3 * h + 3) * WIDTH] = dot_nn(p.astype(bf16), gs[h]).astype(bf16)
                 dqt[sl, :] += dot_nn(kt[sl, rs], ds)
 
-        @pl.when(valid <= 0)
-        def _():
-            gall[rs, : 3 * hw] = jnp.zeros((rows, 3 * hw), bf16)
+        def clear(size):
+            gall[pl.ds(pl.multiple_of((m + 1) * rows - size, size), size), : 3 * hw] = jnp.zeros((size, 3 * hw), bf16)
+
+        def half():
+            work(rows // 2)
+            clear(rows // 2)
+
+        pl.when(valid > rows // 2)(lambda: work(rows))
+        pl.when(jnp.logical_and(valid > 0, valid <= rows // 2))(half)
+        pl.when(valid <= 0)(lambda: clear(rows))
 
     for item in late:
         item.wait()
+    if moved:
+        for item, move in zip(ins, turns):
+            item.wait()
+            move.start()
     for m in range(blocks):
         rs = slice(m * rows, (m + 1) * rows)
         gq = (dqt[:, rs] * score_scale).T.astype(bf16)
@@ -478,26 +503,29 @@
     sums[...] = jnp.zeros_like(sums) if first else sums_in[...]
     sums[0:1, :] += second
     sums[1:2, : 3 * hw] += third
-    for item in saves:
+    for item in saves + (turns if moved else []):
         item.wait()
 
 
-def backward_image(counts, image, gats, at, n1, qkv, full, lse, w, before, wide, nh):
+def backward_image(counts, image, gats, at, n1, qkv, full, lse, w, before, wide, nh, out=None):
     blocks = len(gats)
     hw, rows = gats[0].shape[1:]
     length, d = rows * blocks, n1.shape[2]
+    extra = [] if out is None else [out]
+    moved = 0 if out is None else out.shape[0] // rows
     vm, far = pl.BlockSpec(memory_space=pltpu.VMEM), pl.BlockSpec(memory_space=pl.ANY)
     return pl.pallas_call(
-        partial(backward_kernel, blocks, nh, rows, image, at, not before),
+        partial(backward_kernel, blocks, nh, rows, image, at, not before, moved),
         name="attend_backward",
-        in_specs=[pl.BlockSpec(memory_space=pltpu.SMEM)] + [far] * (blocks + 5) + ([far, vm] if before else []),
-        out_specs=[far, vm, far, far],
+        in_specs=[pl.BlockSpec(memory_space=pltpu.SMEM)] + [far] * (blocks + 5) + ([far, vm] if before else []) + [far] * len(extra),
+        out_specs=[far, vm, far, far] + [far] * len(extra),
         out_shape=[
             jax.ShapeDtypeStruct((d, wide), f32),
             jax.ShapeDtypeStruct((8, d), f32),
             jax.ShapeDtypeStruct((blocks // 2, rows, d), bf16),
             jax.ShapeDtypeStruct((blocks // 2, rows, d), bf16),
-        ],
+        ]
+        + [jax.ShapeDtypeStruct((moved, rows, d), bf16) for _ in extra],
         scratch_shapes=[
             pltpu.VMEM((blocks, hw, rows), bf16),
             pltpu.VMEM((blocks, rows, d), bf16),
@@ -520,12 +548,14 @@
             pltpu.VMEM((d, length), bf16),
             pltpu.SemaphoreType.DMA((2 * blocks + 5,)),
             pltpu.SemaphoreType.DMA((blocks + 1,)),
-        ],
+        ]
+        + [pltpu.VMEM((moved, rows, d), bf16) for _ in extra]
+        + [pltpu.SemaphoreType.DMA((moved,)) for _ in 2 * extra],
         compiler_params=params(),
         cost_estimate=pl.CostEstimate(
             flops=4 * length * d * 3 * hw + 20 * length * length * hw, bytes_accessed=12_000_000, transcendentals=0
         ),
-    )(counts, *gats, n1, qkv, full, lse, w, *before)
+    )(counts, *gats, n1, qkv, full, lse, w, *before, *extra)
 
 
 def flip(index, k):
@@ -712,6 +742,12 @@
         low = (dot_nt(gm[rs, :], w2[...]) * slope).astype(bf16)
         gpre[rs, :] = low
 
+    def collect(rs):
+        gmid[rs, :] += dot_nn(act[rs, :], w2[...])
+        gn2[rs, :] += dot_nt(gpre[rs, :], w1[...])
+
+    ready = slice(0, final * rows)
+
     @pl.when(t < steps)
     def _():
         for i in range(final):
@@ -719,6 +755,7 @@
 
     @pl.when(t == 0)
     def _():
+        collect(ready)
         for m in range(1, blocks):
             head_copy(m).wait()
         enter(final)
@@ -746,8 +783,14 @@
         s2[t] = send.astype(bf16)
         keep2[...] = keep
         cross(s2, r2, ds2, dr2, t, near).start()
-        gmid[...] += dot_nn(act[...], w2[...])
-        gn2[...] += dot_nt(gpre[...], w1[...])
+
+    @pl.when(t == 0)
+    def _():
+        collect(slice(final * rows, images * rows))
+
+    @pl.when(jnp.logical_and(t > 0, t < steps))
+    def _():
+        collect(slice(0, images * rows))
 
     @pl.when(t == steps)
     def _():
@@ -1252,14 +1295,11 @@
     )(*args)
 
 
-def layout_kernel(nh, counts, tok, out, e, o1, o2, *outs):
-    tok_out, out_out, qkv_out, ow_out, fc1_out, fc2_out, b1_out = outs[:7]
-    vectors = outs[7:]
-    images, rows = tok.shape[:2]
-    for k in range(images):
-        into = place(counts, k)
-        tok_out[into] = tok[k]
-        out_out[into] = out[k * rows : (k + 1) * rows, :]
+def layout_kernel(nh, counts, tok, e, o1, o2, *outs):
+    tok_out, qkv_out, ow_out, fc1_out, fc2_out, b1_out = outs[:6]
+    vectors = outs[6:]
+    for k in range(tok.shape[0]):
+        tok_out[place(counts, k)] = tok[k]
     me = lax.axis_index("blk")
     core = lax.rem(me, 2)
     hw = nh * WIDTH
@@ -1290,18 +1330,18 @@
         b1_out[:, k * share : (k + 1) * share] = turned[base + 10 + k : base + 11 + k, :]
 
 
-def layout(counts, tok, out, e, o1, o2, nh, ff):
+def layout(counts, tok, e, o1, o2, nh, ff):
     share, d = e.shape[1], tok.shape[2]
     vm = pl.BlockSpec(memory_space=pltpu.VMEM)
     shapes = [(share, 3 * d), (share, d), (share, ff), (o2.shape[1], d), (1, ff * share // d)] + [(1, share)] * 10
     return pl.pallas_call(
         partial(layout_kernel, nh),
         name="layout",
-        in_specs=[pl.BlockSpec(memory_space=pltpu.SMEM)] + [vm] * 5,
-        out_specs=[vm] * (2 + len(shapes)),
-        out_shape=[jax.ShapeDtypeStruct(tok.shape, bf16)] * 2 + [jax.ShapeDtypeStruct(v, f32) for v in shapes],
+        in_specs=[pl.BlockSpec(memory_space=pltpu.SMEM)] + [vm] * 4,
+        out_specs=[vm] * (1 + len(shapes)),
+        out_shape=[jax.ShapeDtypeStruct(tok.shape, bf16)] + [jax.ShapeDtypeStruct(v, f32) for v in shapes],
         compiler_params=params(),
-    )(counts, tok, out, e, o1, o2)
+    )(counts, tok, e, o1, o2)
 
 
 def finish_kernel(x, gmid, gain, *refs):
@@ -1516,11 +1556,12 @@
                     sum2.swap(send2, x_dim)
                     sum1.swap(send1, img2)
                 *before, kept_i, passed_i = backward_image(
-                    counts, i, firsts if i == 1 else others, 0, *saved[i], w, before, wide, nh
+                    counts, i, firsts if i == 1 else others, 0, *saved[i], w, before, wide, nh, *([out] if i == 2 else [])
                 )
+                if i == 2:
+                    dw, sums1, kept_i, passed_i, output = *before, kept_i, passed_i
                 kept.append(kept_i)
                 passed.append(passed_i)
-            dw, sums1 = before
             ((g1y, _), (g1z, _)), ((g2z, _), (g2x, _)) = sum1.terms[1:], sum2.terms[1:]
             n1, *rest = saved[0]
             pieces = (passed[1], kept[0], near, *others, *rest, so, g1, g1y, g1z, kept[1], n1, dw, w, sums, sums1, vec, gb1)
@@ -1528,9 +1569,7 @@
             tok, e, o1, o2 = last_image(
                 share, tokens.shape, wide, g1.shape[-1], 2 * (ff // n), half, nh, images - 2, *pieces
             )
-            grad_tokens, output, grad_qkv, grad_out, grad_fc1, grad_fc2, g_b1, *v = layout(
-                counts, tok, out, e, o1, o2, nh, ff
-            )
+            grad_tokens, grad_qkv, grad_out, grad_fc1, grad_fc2, g_b1, *v = layout(counts, tok, e, o1, o2, nh, ff)
             g_b1 = g_b1.reshape(-1)
             v = [item.reshape(-1) for item in v]
         else:

time: 195 us -> 191 us (0.979)
  Pallas kernels: 168 us -> 163 us
  waiting for transfers between devices: 3.29 us -> 8.1 us
  starting transfers between devices: 16.7 us -> 14.5 us
    pallas_call x2, Pallas kernels: 24 us -> 19.3 us  [backward_image(): pl.pallas_call(partial(backward_kernel, blocks, nh, rows, image, at, not...]
    pallas_call x2, Pallas kernels: 19.1 us -> 14.6 us  [forward_image(): pl.pallas_call(partial(forward_kernel, blocks, nh, rows, image, moved), n...]
    pallas_call x1, Pallas kernels: 54.1 us -> 57.5 us  [middle_layers(): pl.pallas_call(partial(middle_kernel, blocks, images, steps, bits), name=...]
    ppermute x4, waiting for transfers between devices: 3.26 us -> 6.45 us  [swap(): return lax.ppermute(value, axis, [(i, i ^ 1 << k) for i in range(n)])]
    ppermute x4, starting transfers between devices: 9.35 us -> 7.31 us  [swap(): return lax.ppermute(value, axis, [(i, i ^ 1 << k) for i in range(n)])]
  transfers between devices with their start and end apart: 17 -> 17, of which waited for: 2 -> 4; matrix products, arithmetic and copies ran while one was open for 1% -> 1% of each run, Pallas kernels for 22% -> 18%
where the time goes in v3:
time: 191 us; the launch traced here: 190 us
  Pallas kernels  163 us (85%)
  starting transfers between devices  14.5 us (8%)
  waiting for transfers between devices  8.1 us (4%)
  local copies, waits for them, and re-layouts  2.08 us (1%)
    pallas_call x1, Pallas kernels, middle_layers(): pl.pallas_call(partial(middle_kernel, blocks, images, steps, bits), name=...  57.5 us
    pallas_call x1, Pallas kernels, last_image(): pl.pallas_call(partial(last_kernel, blocks, nh, rows, share, at_piece), n...  40.1 us
    pallas_call x1, Pallas kernels, first_image(): pl.pallas_call(partial(first_kernel, blocks, nh, rows), name='first', in_...  25.5 us
    pallas_call x2, Pallas kernels, backward_image(): pl.pallas_call(partial(backward_kernel, blocks, nh, rows, image, at, not...  19.3 us
    pallas_call x2, Pallas kernels, forward_image(): pl.pallas_call(partial(forward_kernel, blocks, nh, rows, image, moved), n...  14.6 us
    ppermute x4, starting transfers between devices, swap(): return lax.ppermute(value, axis, [(i, i ^ 1 << k) for i in range(n)])  7.31 us
    ppermute x13, starting transfers between devices, swap_blk(): return lax.ppermute(value, 'blk', [(b, b ^ m) for b in range(blocks)])  7.14 us
    ppermute x4, waiting for transfers between devices, swap(): return lax.ppermute(value, axis, [(i, i ^ 1 << k) for i in range(n)])  6.45 us
  transfers between devices with their start and end apart: 17, of which 4 were waited for; matrix products, arithmetic and copies ran while one was open for 1% of the time, Pallas kernels for 18%

profile of v3, /device:TPU:0, one launch (start us, length us, event | category | flops | bytes accessed | tf_op | source)
XLA Modules:
  0.0 190.1 jit_solution(9604751915849047305)
XLA Ops:
  0.7 2.8 %turn.1 = (bf16[256,768]{1,0:T(8,128)(2,1)}, bf16[256,768]{1,0:T(8,128)(2,1)}, bf16[256,768]{1,0:T(8,128)(2,1)}) custom-call(s32[3]{0:T(128)} %counts.11, bf16[3,256,768]{2,1,0:T(8,128)(2,1)} %tokens.1), custom_call_target="tpu_custom_call" | custom-call | tf_op jit(solution)/shard_map/turn/pallas_call | solution.py:77
  3.6 25.5 %first.1 = (bf16[4,256,768]{2,1,0:T(8,128)(2,1)}, bf16[4,256,576]{2,1,0:T(8,128)(2,1)}, f32[192,1024]{1,0:T(8,128)}, f32[8,1024]{1,0:T(8,128)}, bf16[192,256]{1,...) custom-call(bf16[256,768]{1,0:T(8,128)(2,1)} %get-tuple-element.117., ...), custom_call_target="tpu_custom_call" | custom-call | flops 2516582400 | bytes 8000000 | tf_op jit(solution)/shard_map/first/pallas_call | solution.py:230
  29.1 1.1 collective-permute-start.7
  30.4 0.6 convert_element_type.32.refs_4_.refs_16_.refs_20_
  31.1 7.6 %attend_forward.2 = (bf16[4,256,768]{2,1,0:T(8,128)(2,1)}, bf16[4,256,576]{2,1,0:T(8,128)(2,1)}, f32[192,1024]{1,0:T(8,128)}, f32[8,1024]{1,0:T(8,128)}, bf16[19...) custom-call(s32[3]{0:T(128)} %counts.11, ...), custom_call_target="tpu_custom_call" | custom-call | flops 2516582400 | bytes 8000000 | tf_op jit(solution)/shard_map/attend_forward/pallas_call | solution.py:352
  38.7 1.6 collective-permute-done.7.refs_2_
  40.3 0.5 collective-permute-start
  40.8 1.1 collective-permute-start.1
  41.9 0.3 collective-permute-start.2
  42.3 0.6 broadcast_in_dim.7
  42.9 0.7 collective-permute-start.3
  43.6 1.1 collective-permute-start.4
  44.7 0.4 collective-permute-start.5
  45.0 0.4 copy-done.17
  45.4 6.9 %attend_forward.3 = (bf16[4,256,768]{2,1,0:T(8,128)(2,1)}, bf16[4,256,576]{2,1,0:T(8,128)(2,1)}, f32[192,1024]{1,0:T(8,128)}, f32[8,1024]{1,0:T(8,128)}, bf16[19...) custom-call(s32[3]{0:T(128)} %counts.11, ...), custom_call_target="tpu_custom_call" | custom-call | flops 2516582400 | bytes 8000000 | tf_op jit(solution)/shard_map/attend_forward/pallas_call | solution.py:352
  52.5 0.5 copy-done.26
  53.1 57.5 %middle_layers.1 = (bf16[768,768]{1,0:T(8,128)(2,1)}, f32[768,768]{1,0:T(8,128)}, f32[3072,128]{1,0:T(8,128)}, f32[8,768]{1,0:T(8,128)}, bf16[768,384]{1,0:T(8,1...) custom-call(bf16[192,256]{1,0:T(8,128)(2,1)} %get-tuple-element.119., ...), custom_call_target="tpu_custom_call" | custom-call | flops 24461180928 | bytes 30000000 | tf_op jit(solution)/shard_map/middle_layers/pallas_call | solution.py:894
  110.6 0.5 collective-permute-start.12
  111.0 0.9 collective-permute-start.10
  112.0 0.9 collective-permute-start.11
  112.9 1.7 collective-permute-start.13
  114.6 10.0 %attend_backward.2 = (f32[768,640]{1,0:T(8,128)}, f32[8,768]{1,0:T(8,128)}, bf16[2,256,768]{2,1,0:T(8,128)(2,1)}, bf16[2,256,768]{2,1,0:T(8,128)(2,1)}) custom-call(s32[3]{0:T(128)} %counts.11, bf16[1,192,256]{2,1,0:T(8,128)(2,1)} %get-tuple-element.155.refs_0_, bf16[1,192,256]{2,1,0:T(8,128)(2,1)} %get-tuple-element.156.refs_1_, ...), custom_call_target="tpu_custom_call" | custom-call | flops 5838471168 | bytes 12000000 | tf_op jit(solution)/shard_map/attend_backward/pallas_call | solution.py:517
  124.7 0.8 collective-permute-done.12.refs_23_
  125.6 3.1 %collective-permute-done.13.refs_12_ = bf16[2,96,1536]{2,1,0:T(8,128)(2,1)S(1)} collective-permute-done((bf16[2,96,1536]{2,1,0:T(8,128)(2,1)}, bf16[2,96,1536]{2,1,0:T(8,128)(2,1)S(1)}, u32[]{:S(2)}, u32[]{:S(2)}) %collective-permute-start.13) | collective-permute-done | bytes 589856 | tf_op jit(solution)/shard_map/ppermute | solution.py:1393
  128.7 4.2 %collective-permute-start.15 = (bf16[96,1536]{1,0:T(8,128)(2,1)S(1)}, bf16[96,1536]{1,0:T(8,128)(2,1)S(1)}, u32[]{:S(2)}, u32[]{:S(2)}) collective-permute-start(bf16[96,1536]{1,0:T(8,128)(2,1)S(1)} %fusion.1), channel_id=1, source_target_pairs={{0,16},{4,20},{8,24},{12,28},{16,0},{20,4},{24,8},{28,12},{1,17},{... | collective-permute-start | bytes 884744 | tf_op jit(solution)/shard_map/ppermute | solution.py:1393
  132.9 1.0 collective-permute-start.16
  133.9 9.3 %attend_backward.3 = (f32[768,640]{1,0:T(8,128)}, f32[8,768]{1,0:T(8,128)}, bf16[2,256,768]{2,1,0:T(8,128)(2,1)}, bf16[2,256,768]{2,1,0:T(8,128)(2,1)}, bf16[3,256,768]{2,1,0:T(8,128)(2,1)}) custom-call(s32[3]{0:T(128)} %counts.11, bf16[2,192,256]{2,1,0:T(8,128)(2,1)} %get-tuple-element.164.refs_0_.refs_3_, bf16[2,192,256]{2,1,0:T(8,128)(2,1)} %copy-done.20, ...), custom_call_target="tpu_custom_call" | custom-call | flops 5838471168 | bytes 12000000 | tf_op jit(solution)/shard_map/attend_backward/pallas_call | solution.py:517
  143.2 2.6 %collective-permute-done.15.refs_13_ = bf16[96,1536]{1,0:T(8,128)(2,1)S(1)} collective-permute-done((bf16[96,1536]{1,0:T(8,128)(2,1)S(1)}, bf16[96,1536]{1,0:T(8,128)(2,1)S(1)}, u32[]{:S(2)}, u32[]{:S(2)}) %collective-permute-start.15) | collective-permute-done | bytes 294944 | tf_op jit(solution)/shard_map/ppermute | solution.py:1393
  145.9 0.7 copy-done.18
  146.6 0.1 copy-done.19
  146.7 40.1 %last.1 = (bf16[3,256,768]{2,1,0:T(8,128)(2,1)}, f32[4,24,1024]{2,1,0:T(8,128)}, f32[2,24,1536]{2,1,0:T(8,128)}, f32[2,96,384]{2,1,0:T(8,128)}) custom-call(bf16[2,256,768]{2,1,0:T(8,128)(2,1)} %get-tuple-element.182.refs_0_, bf16[2,256,768]{2,1,0:T(8,128)(2,1)} %get-tuple-element.183.refs_1_, bf16[2,256,768]{2,1,0:T(8,128)(2,1)} %copy-done.13, ...), custom_call_target="tpu_custom_call" | custom-call | flops 30000001024 | bytes 20000000 | tf_op jit(solution)/shard_map/last/pallas_call | solution.py:1252
  186.8 3.0 %layout.1 = (bf16[3,256,768]{2,1,0:T(8,128)(2,1)}, f32[24,2304]{1,0:T(8,128)}, f32[24,768]{1,0:T(8,128)}, f32[24,3072]{1,0:T(8,128)}, f32[96,768]{1,0:T(8,128)},...) custom-call(s32[3]{0:T(128)} %counts.11, ...), custom_call_target="tpu_custom_call" | custom-call | tf_op jit(solution)/shard_map/layout/pallas_call | solution.py:1337
  (88 shorter events, 0.6 us)
Async XLA Ops:
  3.4 25.6 %copy-start.14 = (bf16[256,768]{1,0:T(8,128)(2,1)S(1)}, bf16[256,768]{1,0:T(8,128)(2,1)}, u32[]{:S(2)}) copy-start(bf16[256,768]{1,0:T(8,128)(2,1)} %get-tuple-element.143.refs_0_.refs_14_.refs_28_) | copy-start | bytes 1179652
  3.5 26.8 %copy-start.5 = (bf16[768]{0:T(1024)(128)(2,1)S(1)}, bf16[768]{0:T(1024)(128)(2,1)}, u32[]{:S(2)}) copy-start(bf16[768]{0:T(1024)(128)(2,1)} %refs_3_.1) | copy-start | bytes 4612
  3.5 26.8 %copy-start.6 = (bf16[768]{0:T(1024)(128)(2,1)S(1)}, bf16[768]{0:T(1024)(128)(2,1)}, u32[]{:S(2)}) copy-start(bf16[768]{0:T(1024)(128)(2,1)} %refs_4_.1) | copy-start | bytes 4612
  3.5 26.8 %copy-start.7 = (bf16[768]{0:T(1024)(128)(2,1)S(1)}, bf16[768]{0:T(1024)(128)(2,1)}, u32[]{:S(2)}) copy-start(bf16[768]{0:T(1024)(128)(2,1)} %param.27) | copy-start | bytes 4612
  3.5 26.8 %copy-start.8 = (bf16[768]{0:T(1024)(128)(2,1)S(1)}, bf16[768]{0:T(1024)(128)(2,1)}, u32[]{:S(2)}) copy-start(bf16[768]{0:T(1024)(128)(2,1)} %param.28) | copy-start | bytes 4612
  3.5 26.8 %copy-start.9 = (bf16[768]{0:T(1024)(128)(2,1)S(1)}, bf16[768]{0:T(1024)(128)(2,1)}, u32[]{:S(2)}) copy-start(bf16[768]{0:T(1024)(128)(2,1)} %param.33) | copy-start | bytes 4612
  3.5 26.8 %copy-start.10 = (bf16[768]{0:T(1024)(128)(2,1)S(1)}, bf16[768]{0:T(1024)(128)(2,1)}, u32[]{:S(2)}) copy-start(bf16[768]{0:T(1024)(128)(2,1)} %param.34) | copy-start | bytes 4612
  3.5 26.8 %copy-start.11 = (bf16[768]{0:T(1024)(128)(2,1)S(1)}, bf16[768]{0:T(1024)(128)(2,1)}, u32[]{:S(2)}) copy-start(bf16[768]{0:T(1024)(128)(2,1)} %param.24) | copy-start | bytes 4612
  3.5 26.8 %copy-start.12 = (bf16[768]{0:T(1024)(128)(2,1)S(1)}, bf16[768]{0:T(1024)(128)(2,1)}, u32[]{:S(2)}) copy-start(bf16[768]{0:T(1024)(128)(2,1)} %param.32) | copy-start | bytes 4612
  29.1 11.2 %collective-permute-start.7 = (bf16[256,768]{1,0:T(8,128)(2,1)S(1)}, bf16[256,768]{1,0:T(8,128)(2,1)S(1)}, u32[]{:S(2)}, u32[]{:S(2)}) collective-permute-start(bf16[256,768]{1,0:T(8,128)(2,1)S(1)} %copy-done.14), channel_id=1, source_target_pairs={{0,2},{1,3},{2,0},{3,1},{4,6},{5,7},{6,4},{7,5},{8,10},{9,11},{10,... | collective-permute-start | bytes 1179656 | tf_op jit(solution)/shard_map/ppermute | solution.py:1479
  30.2 13.4 %collective-permute-start.6 = (bf16[256,768]{1,0:T(8,128)(2,1)S(1)}, bf16[256,768]{1,0:T(8,128)(2,1)S(1)}, u32[]{:S(2)}, u32[]{:S(2)}) collective-permute-start(bf16[256,768]{1,0:T(8,128)(2,1)S(1)} %copy-done.14), channel_id=1, source_target_pairs={{0,1},{1,0},{2,3},{3,2},{4,5},{5,4},{6,7},{7,6},{8,9},{9,8},{10,11... | collective-permute-start | bytes 1179656 | tf_op jit(solution)/shard_map/ppermute | solution.py:1479
  31.0 10.9 %copy-start.23 = (bf16[192,256]{1,0:T(8,128)(2,1)S(1)}, bf16[192,256]{1,0:T(8,128)(2,1)}, u32[]{:S(2)}) copy-start(bf16[192,256]{1,0:T(8,128)(2,1)} %get-tuple-element.122) | copy-start | bytes 294916
  31.0 11.2 %copy-start.4 = (bf16[3072]{0:T(1024)(128)(2,1)S(1)}, bf16[3072]{0:T(1024)(128)(2,1)}, u32[]{:S(2)}) copy-start(bf16[3072]{0:T(1024)(128)(2,1)} %param.30) | copy-start | bytes 18436
  40.3 4.4 %collective-permute-start.8 = (bf16[256,768]{1,0:T(8,128)(2,1)S(1)}, bf16[256,768]{1,0:T(8,128)(2,1)S(1)}, u32[]{:S(2)}, u32[]{:S(2)}) collective-permute-start(bf16[256,768]{1,0:T(8,128)(2,1)S(1)} %collective-permute-done.7.refs_2_), channel_id=1, source_target_pairs={{0,1},{1,0},{2,3},{3,2},{4,5},{5,4},{6,7},{7,6},{8,9},{9,8},{10,11... | collective-permute-start | bytes 1179656 | tf_op jit(solution)/shard_map/ppermute | solution.py:1479
  40.3 2.5 %collective-permute-start = (bf16[192,256]{1,0:T(8,128)(2,1)S(1)}, bf16[192,256]{1,0:T(8,128)(2,1)S(1)}, u32[]{:S(2)}, u32[]{:S(2)}) collective-permute-start(bf16[192,256]{1,0:T(8,128)(2,1)S(1)} %copy-done.29), channel_id=1, source_target_pairs={{0,1},{1,0},{2,3},{3,2},{4,5},{5,4},{6,7},{7,6},{8,9},{9,8},{10,11... | collective-permute-start | bytes 294920 | tf_op jit(solution)/shard_map/ppermute | solution.py:1479
  40.8 11.5 %collective-permute-start.1 = (bf16[192,256]{1,0:T(8,128)(2,1)S(1)}, bf16[192,256]{1,0:T(8,128)(2,1)S(1)}, u32[]{:S(2)}, u32[]{:S(2)}) collective-permute-start(bf16[192,256]{1,0:T(8,128)(2,1)S(1)} %copy-done.24), channel_id=1, source_target_pairs={{0,2},{1,3},{2,0},{3,1},{4,6},{5,7},{6,4},{7,5},{8,10},{9,11},{10,... | collective-permute-start | bytes 294920 | tf_op jit(solution)/shard_map/ppermute | solution.py:1479
  41.9 10.5 %collective-permute-start.2 = (bf16[192,256]{1,0:T(8,128)(2,1)S(1)}, bf16[192,256]{1,0:T(8,128)(2,1)S(1)}, u32[]{:S(2)}, u32[]{:S(2)}) collective-permute-start(bf16[192,256]{1,0:T(8,128)(2,1)S(1)} %copy-done.23), channel_id=1, source_target_pairs={{0,3},{1,2},{2,1},{3,0},{4,7},{5,6},{6,5},{7,4},{8,11},{9,10},{10,... | collective-permute-start | bytes 294920 | tf_op jit(solution)/shard_map/ppermute | solution.py:1479
  42.9 9.5 %collective-permute-start.3 = (bf16[192,256]{1,0:T(8,128)(2,1)}, bf16[192,256]{1,0:T(8,128)(2,1)S(1)}, u32[]{:S(2)}, u32[]{:S(2)}) collective-permute-start(bf16[192,256]{1,0:T(8,128)(2,1)} %get-tuple-element.138), channel_id=1, source_target_pairs={{0,1},{1,0},{2,3},{3,2},{4,5},{5,4},{6,7},{7,6},{8,9},{9,8},{10,11... | collective-permute-start | bytes 294920 | tf_op jit(solution)/shard_map/ppermute | solution.py:1479
  43.6 8.8 %collective-permute-start.4 = (bf16[192,256]{1,0:T(8,128)(2,1)}, bf16[192,256]{1,0:T(8,128)(2,1)S(1)}, u32[]{:S(2)}, u32[]{:S(2)}) collective-permute-start(bf16[192,256]{1,0:T(8,128)(2,1)} %get-tuple-element.139), channel_id=1, source_target_pairs={{0,2},{1,3},{2,0},{3,1},{4,6},{5,7},{6,4},{7,5},{8,10},{9,11},{10,... | collective-permute-start | bytes 294920 | tf_op jit(solution)/shard_map/ppermute | solution.py:1479
  44.7 7.8 %collective-permute-start.5 = (bf16[192,256]{1,0:T(8,128)(2,1)}, bf16[192,256]{1,0:T(8,128)(2,1)S(1)}, u32[]{:S(2)}, u32[]{:S(2)}) collective-permute-start(bf16[192,256]{1,0:T(8,128)(2,1)} %get-tuple-element.140), channel_id=1, source_target_pairs={{0,3},{1,2},{2,1},{3,0},{4,7},{5,6},{6,5},{7,4},{8,11},{9,10},{10,... | collective-permute-start | bytes 294920 | tf_op jit(solution)/shard_map/ppermute | solution.py:1479
  110.6 14.9 %collective-permute-start.12 = (bf16[2,2,192,384]{3,2,1,0:T(8,128)(2,1)}, bf16[2,2,192,384]{3,2,1,0:T(8,128)(2,1)S(1)}, u32[]{:S(2)}, u32[]{:S(2)}) collective-permute-start(bf16[2,2,192,384]{3,2,1,0:T(8,128)(2,1)} %get-tuple-element.173), channel_id=1, source_target_pairs={{0,8},{4,12},{8,0},{12,4},{16,24},{20,28},{24,16},{28,20},{1,9},{5... | collective-permute-start | bytes 1769480 | tf_op jit(solution)/shard_map/ppermute | solution.py:1393
  111.0 13.5 %collective-permute-start.9 = (bf16[2,192,256]{2,1,0:T(8,128)(2,1)}, bf16[2,192,256]{2,1,0:T(8,128)(2,1)S(1)}, u32[]{:S(2)}, u32[]{:S(2)}) collective-permute-start(bf16[2,192,256]{2,1,0:T(8,128)(2,1)} %get-tuple-element.152), channel_id=1, source_target_pairs={{0,1},{1,0},{2,3},{3,2},{4,5},{5,4},{6,7},{7,6},{8,9},{9,8},{10,11... | collective-permute-start | bytes 589832 | tf_op jit(solution)/shard_map/ppermute | solution.py:1479
  111.0 13.6 %collective-permute-start.10 = (bf16[2,192,256]{2,1,0:T(8,128)(2,1)}, bf16[2,192,256]{2,1,0:T(8,128)(2,1)S(1)}, u32[]{:S(2)}, u32[]{:S(2)}) collective-permute-start(bf16[2,192,256]{2,1,0:T(8,128)(2,1)} %get-tuple-element.153), channel_id=1, source_target_pairs={{0,2},{1,3},{2,0},{3,1},{4,6},{5,7},{6,4},{7,5},{8,10},{9,11},{10,... | collective-permute-start | bytes 589832 | tf_op jit(solution)/shard_map/ppermute | solution.py:1479
  112.0 12.7 %collective-permute-start.11 = (bf16[2,192,256]{2,1,0:T(8,128)(2,1)}, bf16[2,192,256]{2,1,0:T(8,128)(2,1)S(1)}, u32[]{:S(2)}, u32[]{:S(2)}) collective-permute-start(bf16[2,192,256]{2,1,0:T(8,128)(2,1)} %get-tuple-element.154), channel_id=1, source_target_pairs={{0,3},{1,2},{2,1},{3,0},{4,7},{5,6},{6,5},{7,4},{8,11},{9,10},{10,... | collective-permute-start | bytes 589832 | tf_op jit(solution)/shard_map/ppermute | solution.py:1479
  112.9 15.7 %collective-permute-start.13 = (bf16[2,96,1536]{2,1,0:T(8,128)(2,1)}, bf16[2,96,1536]{2,1,0:T(8,128)(2,1)S(1)}, u32[]{:S(2)}, u32[]{:S(2)}) collective-permute-start(bf16[2,96,1536]{2,1,0:T(8,128)(2,1)} %get-tuple-element.176), channel_id=1, source_target_pairs={{0,4},{4,0},{8,12},{12,8},{16,20},{20,16},{24,28},{28,24},{1,5},{5... | collective-permute-start | bytes 1769480 | tf_op jit(solution)/shard_map/ppermute | solution.py:1393
  114.6 10.9 %copy-start.1 = (bf16[2,2,192,384]{3,2,1,0:T(8,128)(2,1)S(1)}, bf16[2,2,192,384]{3,2,1,0:T(8,128)(2,1)}, u32[]{:S(2)}) copy-start(bf16[2,2,192,384]{3,2,1,0:T(8,128)(2,1)} %get-tuple-element.172.refs_22_) | copy-start | bytes 1769476
  114.6 14.0 %copy-start = (bf16[2,96,1536]{2,1,0:T(8,128)(2,1)S(1)}, bf16[2,96,1536]{2,1,0:T(8,128)(2,1)}, u32[]{:S(2)}) copy-start(bf16[2,96,1536]{2,1,0:T(8,128)(2,1)} %get-tuple-element.175.refs_11_) | copy-start | bytes 1769476
  124.6 18.6 %collective-permute-start.14 = (bf16[2,256,768]{2,1,0:T(8,128)(2,1)}, bf16[2,256,768]{2,1,0:T(8,128)(2,1)S(1)}, u32[]{:S(2)}, u32[]{:S(2)}) collective-permute-start(bf16[2,256,768]{2,1,0:T(8,128)(2,1)} %get-tuple-element.184), channel_id=1, source_target_pairs={{0,1},{1,0},{2,3},{3,2},{4,5},{5,4},{6,7},{7,6},{8,9},{9,8},{10,11... | collective-permute-start | bytes 2359304 | tf_op jit(solution)/shard_map/ppermute | solution.py:1479
  125.5 17.7 %copy-start.2 = (bf16[2,2,192,384]{3,2,1,0:T(8,128)(2,1)}, bf16[2,2,192,384]{3,2,1,0:T(8,128)(2,1)S(1)}, u32[]{:S(2)}) copy-start(bf16[2,2,192,384]{3,2,1,0:T(8,128)(2,1)S(1)} %collective-permute-done.12.refs_23_) | copy-start | bytes 1769476
  128.6 14.6 %copy-start.3 = (bf16[2,96,1536]{2,1,0:T(8,128)(2,1)}, bf16[2,96,1536]{2,1,0:T(8,128)(2,1)S(1)}, u32[]{:S(2)}) copy-start(bf16[2,96,1536]{2,1,0:T(8,128)(2,1)S(1)} %collective-permute-done.13.refs_12_) | copy-start | bytes 1769476
  128.7 17.2 %collective-permute-start.15 = (bf16[96,1536]{1,0:T(8,128)(2,1)S(1)}, bf16[96,1536]{1,0:T(8,128)(2,1)S(1)}, u32[]{:S(2)}, u32[]{:S(2)}) collective-permute-start(bf16[96,1536]{1,0:T(8,128)(2,1)S(1)} %fusion.1), channel_id=1, source_target_pairs={{0,16},{4,20},{8,24},{12,28},{16,0},{20,4},{24,8},{28,12},{1,17},{... | collective-permute-start | bytes 884744 | tf_op jit(solution)/shard_map/ppermute | solution.py:1393
  132.9 13.0 %collective-permute-start.16 = (bf16[2,192,384]{2,1,0:T(8,128)(2,1)S(1)}, bf16[2,192,384]{2,1,0:T(8,128)(2,1)S(1)}, u32[]{:S(2)}, u32[]{:S(2)}) collective-permute-start(bf16[2,192,384]{2,1,0:T(8,128)(2,1)S(1)} %fusion), channel_id=1, source_target_pairs={{0,2},{1,3},{2,0},{3,1},{4,6},{5,7},{6,4},{7,5},{8,10},{9,11},{10,... | collective-permute-start | bytes 884744 | tf_op jit(solution)/shard_map/ppermute | solution.py:1393
  (17 other events, 70.6 us)
